TPU v7x, 32 devices: a whole 2x2x4 slice. The times are simulated.
32 devices in a mesh: seq: 16 (over z, y, core), fsdp: 2 (over x).
Axes of the slice: x: 2, y: 2, z: 4, core: 2. Of those that a mesh axis runs over, the one named last changes fastest.
Arguments:
- tokens: bfloat16 [2, 3072, 1536], P('fsdp', 'seq'), may hold values from -6 to 6
- norm1_gain: bfloat16 [1536], P('seq'), may hold values from 0.099609375 to 1.8984375
- in_weight: bfloat16 [1536, 3, 1536], P('seq', None, 'fsdp'), may hold values from -0.15625 to 0.15625
- conv_kernel: bfloat16 [1536, 3], P('seq'), may hold values from -3.5 to 3.5
- out_weight: bfloat16 [1536, 1536], P('seq', 'fsdp'), may hold values from -0.15625 to 0.15625
- norm2_gain: bfloat16 [1536], P('seq'), may hold values from 0.099609375 to 1.8984375
- gate_weight: bfloat16 [1536, 6912], P('seq', 'fsdp'), may hold values from -0.15625 to 0.15625
- up_weight: bfloat16 [1536, 6912], P('seq', 'fsdp'), may hold values from -0.15625 to 0.15625
- down_weight: bfloat16 [1536, 6912], P('seq', 'fsdp'), may hold values from -0.109375 to 0.109375
- d_out: bfloat16 [2, 3072, 1536], P('fsdp', 'seq'), may hold values from -6 to 6
Outputs:
- result: bfloat16 [2, 3072, 1536], P('fsdp', 'seq')
- d_tokens: bfloat16 [2, 3072, 1536], P('fsdp', 'seq')
- d_norm1_gain: float32 [1536], P('seq')
- d_in_weight: float32 [1536, 3, 1536], P('seq', None, 'fsdp')
- d_conv_kernel: float32 [1536, 3], P('seq')
- d_out_weight: float32 [1536, 1536], P('seq', 'fsdp')
- d_norm2_gain: float32 [1536], P('seq')
- d_gate_weight: float32 [1536, 6912], P('seq', 'fsdp')
- d_up_weight: float32 [1536, 6912], P('seq', 'fsdp')
- d_down_weight: float32 [1536, 6912], P('seq', 'fsdp')
All inputs are finite; a program needn't handle non-finite values.
Results may differ from a plain program's by a relative error of at most 0.012.
Values may be sent and summed in bfloat16 or wider, within the bound.
A program may use at most 576 MiB of HBM per device.

v0:
```python
import jax
import jax.numpy as jnp
from jax import lax
from jax.sharding import PartitionSpec as P

SEQS = 3


EPSILON = 1e-05


def passed_along(value, axis, steps):
    count = lax.axis_size(axis)
    initial, last = (max(0, -steps), min(count, count - steps))
    return lax.ppermute(value, axis, [(source, source + steps) for source in range(initial, last)])


def times_transposed(left, right):
    return lax.dot_general(
        left, right, (((1,), (1,)), ((), ())), preferred_element_type=jnp.float32
    )


def transposed_times(left, right):
    return lax.dot_general(
        left, right, (((0,), (0,)), ((), ())), preferred_element_type=jnp.float32
    )


def root_norm(hidden, gain):
    scale = lax.rsqrt(jnp.mean(hidden * hidden, axis=-1, keepdims=True) + EPSILON)
    return (hidden * scale * gain, scale)


def norm_back(grad, hidden, scale, gain):
    weighted = grad * gain
    inner = jnp.sum(weighted * hidden, axis=-1, keepdims=True)
    d_hidden = scale * weighted - hidden * (scale * scale * scale) * inner / hidden.shape[-1]
    d_gain = jnp.sum(grad * hidden * scale, axis=0)
    return (d_hidden, d_gain)


def on_device(
    tokens,
    norm1_gain,
    in_weight,
    conv_kernel,
    out_weight,
    norm2_gain,
    gate_weight,
    up_weight,
    down_weight,
    d_out,
):

    def fetch_mixer():
        gain_one, w_in, kernel, w_out = (
            lax.all_gather(norm1_gain, "seq", axis=0, tiled=True),
            lax.all_gather(in_weight, "seq", axis=0, tiled=True),
            lax.all_gather(conv_kernel, "seq", axis=0, tiled=True),
            lax.all_gather(out_weight, "seq", axis=0, tiled=True),
        )
        w_in, w_out = (
            lax.all_gather(w_in, "fsdp", axis=2, tiled=True),
            lax.all_gather(w_out, "fsdp", axis=1, tiled=True),
        )
        return (gain_one.astype(jnp.float32), w_in, kernel.astype(jnp.float32), w_out)

    def fetch_ffn():
        gain_two, w_gate, w_up, w_down = (
            lax.all_gather(norm2_gain, "seq", axis=0, tiled=True),
            lax.all_gather(gate_weight, "seq", axis=0, tiled=True),
            lax.all_gather(up_weight, "seq", axis=0, tiled=True),
            lax.all_gather(down_weight, "seq", axis=0, tiled=True),
        )
        w_gate, w_up, w_down = (
            lax.all_gather(w_gate, "fsdp", axis=1, tiled=True),
            lax.all_gather(w_up, "fsdp", axis=1, tiled=True),
            lax.all_gather(w_down, "fsdp", axis=1, tiled=True),
        )
        return (gain_two.astype(jnp.float32), w_gate, w_up, w_down)

    hidden = tokens[0].astype(jnp.float32)
    rows, width = hidden.shape
    gain_one_f, w_in, kernel_f, w_out = fetch_mixer()
    channels = w_in.shape[2]
    taps = kernel_f.shape[1]
    margin = taps - 1
    kernel_here = kernel_f
    normed, scale_one = root_norm(hidden, gain_one_f)
    normed_low = normed.astype(jnp.bfloat16)
    lead = normed_low.shape[0] // rows
    w_in_flat = w_in.reshape(width, 3 * channels)
    projected = jnp.dot(normed_low, w_in_flat, preferred_element_type=jnp.float32).reshape(
        lead, rows, 3 * channels
    )
    b_part = projected[:, :, :channels]
    c_part = projected[:, :, channels : 2 * channels]
    x_part = projected[:, :, 2 * channels :]
    gated = (b_part * x_part).astype(jnp.bfloat16)
    before = passed_along(gated[:, rows - margin :], "seq", 1)
    padded = jnp.concatenate([before, gated], axis=1).astype(jnp.float32)
    seq_len = lax.axis_size("seq") * rows // SEQS
    position = lax.axis_index("seq") * rows + jnp.arange(rows, dtype=jnp.int32)
    in_sequence = position % seq_len
    masks = [
        (in_sequence >= margin - offset).astype(jnp.float32)[:, None] for offset in range(taps)
    ]
    conv = jnp.zeros((lead, rows, channels), jnp.float32)
    for offset in range(taps):
        conv = conv + masks[offset] * padded[:, offset : offset + rows] * kernel_here[:, offset]
    mixed = (c_part * conv).astype(jnp.bfloat16)
    mixed_flat = mixed.reshape(lead * rows, channels)
    branch = times_transposed(mixed_flat, w_out)
    hidden_one = hidden + branch
    gain_two_f, w_gate, w_up, w_down = fetch_ffn()
    normed_two, scale_two = root_norm(hidden_one, gain_two_f)
    normed_two_low = normed_two.astype(jnp.bfloat16)
    gate = jnp.dot(normed_two_low, w_gate, preferred_element_type=jnp.float32)
    upper = jnp.dot(normed_two_low, w_up, preferred_element_type=jnp.float32)
    active = (jax.nn.silu(gate) * upper).astype(jnp.bfloat16)
    ffn_out = times_transposed(active, w_down)
    result = hidden_one + ffn_out
    gain_two_f, w_gate, w_up, w_down = fetch_ffn()
    grad_low = d_out[0]
    grad_out = grad_low.astype(jnp.float32)
    d_down = transposed_times(grad_low, active)
    d_active = jnp.dot(grad_low, w_down, preferred_element_type=jnp.float32)
    sigma = jax.nn.sigmoid(gate)
    d_upper = (d_active * gate * sigma).astype(jnp.bfloat16)
    d_gate = (d_active * upper * sigma * (1.0 + gate * (1.0 - sigma))).astype(jnp.bfloat16)
    d_gate_w = transposed_times(normed_two_low, d_gate)
    d_up_w = transposed_times(normed_two_low, d_upper)
    d_normed_two = times_transposed(d_gate, w_gate) + times_transposed(d_upper, w_up)
    d_hidden_two, d_gain_two = norm_back(d_normed_two, hidden_one, scale_two, gain_two_f)
    d_gate_w, d_up_w, d_down = (
        lax.psum_scatter(
            d_gate_w.astype(jnp.bfloat16), "fsdp", scatter_dimension=1, tiled=True
        ).astype(jnp.float32),
        lax.psum_scatter(
            d_up_w.astype(jnp.bfloat16), "fsdp", scatter_dimension=1, tiled=True
        ).astype(jnp.float32),
        lax.psum_scatter(
            d_down.astype(jnp.bfloat16), "fsdp", scatter_dimension=1, tiled=True
        ).astype(jnp.float32),
    )
    ffn_grads = (
        lax.psum_scatter(d_gain_two, "seq", scatter_dimension=0, tiled=True),
        lax.psum_scatter(d_gate_w, "seq", scatter_dimension=0, tiled=True),
        lax.psum_scatter(d_up_w, "seq", scatter_dimension=0, tiled=True),
        lax.psum_scatter(d_down, "seq", scatter_dimension=0, tiled=True),
    )
    grad_one = grad_out + d_hidden_two
    gain_one_f, w_in, kernel_f, w_out = fetch_mixer()
    kernel_here = kernel_f
    w_in_flat = w_in.reshape(width, 3 * channels)
    grad_one_low = grad_one.astype(jnp.bfloat16)
    d_out_w = transposed_times(grad_one_low, mixed_flat)
    d_mixed = jnp.dot(grad_one_low, w_out, preferred_element_type=jnp.float32).reshape(
        lead, rows, channels
    )
    d_c = d_mixed * conv
    d_conv = d_mixed * c_part
    kernel_cols = []
    d_padded = jnp.zeros((lead, rows + margin, channels), jnp.float32)
    for offset in range(taps):
        masked = masks[offset] * d_conv
        kernel_cols.append(jnp.sum(masked * padded[:, offset : offset + rows], axis=(0, 1)))
        d_padded = d_padded + jnp.pad(
            masked * kernel_here[:, offset], ((0, 0), (offset, margin - offset), (0, 0))
        )
    d_kernel_here = jnp.stack(kernel_cols, axis=1)
    from_next = passed_along(d_padded[:, :margin], "seq", -1)
    d_gated = d_padded[:, margin:] + jnp.pad(from_next, ((0, 0), (rows - margin, 0), (0, 0)))
    d_projected = (
        jnp.concatenate([d_gated * x_part, d_c, d_gated * b_part], axis=2)
        .astype(jnp.bfloat16)
        .reshape(lead * rows, 3 * channels)
    )
    d_in_w = transposed_times(normed_low, d_projected).reshape(width, 3, channels)
    d_normed = times_transposed(d_projected, w_in_flat)
    d_hidden, d_gain_one = norm_back(d_normed, hidden, scale_one, gain_one_f)
    d_in_w, d_out_w = (
        lax.psum_scatter(
            d_in_w.astype(jnp.bfloat16), "fsdp", scatter_dimension=2, tiled=True
        ).astype(jnp.float32),
        lax.psum_scatter(
            d_out_w.astype(jnp.bfloat16), "fsdp", scatter_dimension=1, tiled=True
        ).astype(jnp.float32),
    )
    mixer_grads = (
        lax.psum_scatter(d_gain_one, "seq", scatter_dimension=0, tiled=True),
        lax.psum_scatter(d_in_w, "seq", scatter_dimension=0, tiled=True),
        lax.psum_scatter(d_kernel_here, "seq", scatter_dimension=0, tiled=True),
        lax.psum_scatter(d_out_w, "seq", scatter_dimension=0, tiled=True),
    )
    gain_one_sum, kernel_sum, gain_two_sum = lax.psum(
        (mixer_grads[0], mixer_grads[2], ffn_grads[0]), "fsdp"
    )
    d_tokens = (grad_one + d_hidden).astype(jnp.bfloat16)
    return (
        result.astype(jnp.bfloat16)[None],
        d_tokens[None],
        gain_one_sum,
        mixer_grads[1],
        kernel_sum,
        mixer_grads[3],
        gain_two_sum,
        ffn_grads[1],
        ffn_grads[2],
        ffn_grads[3],
    )


def solution(mesh):
    return jax.shard_map(
        on_device,
        mesh=mesh,
        in_specs=(
            P("fsdp", "seq", None),
            P("seq"),
            P("seq", None, "fsdp"),
            P("seq", None),
            P("seq", "fsdp"),
            P("seq"),
            P("seq", "fsdp"),
            P("seq", "fsdp"),
            P("seq", "fsdp"),
            P("fsdp", "seq", None),
        ),
        out_specs=(
            P("fsdp", "seq", None),
            P("fsdp", "seq", None),
            P("seq"),
            P("seq", None, "fsdp"),
            P("seq", None),
            P("seq", "fsdp"),
            P("seq"),
            P("seq", "fsdp"),
            P("seq", "fsdp"),
            P("seq", "fsdp"),
        ),
        check_vma=False,
    )
```

profile of v0, /device:TPU:0, one launch (start us, length us, event | category | flops | bytes accessed | tf_op | source)
XLA Modules:
  0.0 3316.9 jit_solution(9601434577534924413)
XLA Ops:
  7.2 0.7 all-gather.12.cloned.1.call-update
  8.0 0.7 all-gather.16.cloned.1.call-update
  8.7 0.7 all-gather.24.cloned.1.call-update
  10.6 69.1 %all-gather.12.cloned.1.call-done = bf16[1536,3,768]{2,0,1:T(8,128)(2,1)} async-done(((bf16[96,3,768]{2,0,1:T(8,128)(2,1)}), bf16[1536,3,768]{2,0,1:T(8,128)(2,1)}) %all-gather.12.cloned.1.call-update) | async-done | bytes 7077904 | tf_op jit(solution)/shard_map/all_gather | solution.py:59
  79.7 10.3 copy.30
  90.0 32.7 all-gather.16.cloned.1.call-done
  122.8 89.7 %all-gather.24.cloned.1.call-done = bf16[1536,3456]{1,0:T(8,128)(2,1)} async-done(((bf16[96,3456]{1,0:T(8,128)(2,1)}), bf16[1536,3456]{1,0:T(8,128)(2,1)}) %all-gather.24.cloned.1.call-update) | async-done | bytes 10616848 | tf_op jit(solution)/shard_map/all_gather | solution.py:73
  212.6 89.0 %all-gather.20.cloned.1.call-done = bf16[1536,3456]{1,0:T(8,128)(2,1)} async-done(((bf16[96,3456]{1,0:T(8,128)(2,1)}), bf16[1536,3456]{1,0:T(8,128)(2,1)}) %all-gather.20.cloned.1.call-update) | async-done | bytes 10616848 | tf_op jit(solution)/shard_map/all_gather | solution.py:72
  301.7 89.0 %all-gather.28.cloned.1.call-done = bf16[1536,3456]{1,0:T(8,128)(2,1)} async-done(((bf16[96,3456]{1,0:T(8,128)(2,1)}), bf16[1536,3456]{1,0:T(8,128)(2,1)}) %all-gather.28.cloned.1.call-update) | async-done | bytes 10616848 | tf_op jit(solution)/shard_map/all_gather | solution.py:74
  391.3 0.6 fusion.36
  393.0 31.4 all-reduce.10
  424.5 17.1 all-gather
  442.6 117.0 %all-gather.14.cloned.1.call-done = bf16[1536,3,1536]{0,2,1:T(8,128)(2,1)} async-done(((bf16[1536,3,768]{0,2,1:T(8,128)(2,1)}), bf16[1536,3,1536]{0,2,1:T(8,128)(2,1)}) %all-gather.14.cloned.1.call-update) | async-done | bytes 14155792 | tf_op jit(solution)/shard_map/all_gather | solution.py:64
  559.6 7.9 convolution_bitcast_fusion
  567.7 2.0 collective-permute-start
  570.4 1.7 fusion.20
  572.1 51.8 %all-gather.18.cloned.1.call-done = bf16[1536,1536]{1,0:T(8,128)(2,1)} async-done(((bf16[1536,768]{1,0:T(8,128)(2,1)}), bf16[1536,1536]{1,0:T(8,128)(2,1)}) %all-gather.18.cloned.1.call-update) | async-done | bytes 4718608 | tf_op jit(solution)/shard_map/all_gather | solution.py:65
  623.9 4.1 multiply_reduce_fusion.5
  628.0 1.0 copy-done.8
  629.2 246.4 %all-gather.26.cloned.1.call-done = bf16[1536,6912]{1,0:T(8,128)(2,1)} async-done(((bf16[1536,3456]{1,0:T(8,128)(2,1)}), bf16[1536,6912]{1,0:T(8,128)(2,1)}) %all-gather.26.cloned.1.call-update) | async-done | bytes 21233680 | tf_op jit(solution)/shard_map/all_gather | solution.py:78
  875.6 15.2 fusion.38
  890.8 236.6 %all-gather.22.cloned.1.call-done = bf16[1536,6912]{1,0:T(8,128)(2,1)} async-done(((bf16[1536,3456]{1,0:T(8,128)(2,1)}), bf16[1536,6912]{1,0:T(8,128)(2,1)}) %all-gather.22.cloned.1.call-update) | async-done | bytes 21233680 | tf_op jit(solution)/shard_map/all_gather | solution.py:77
  1127.4 15.2 fusion.37
  1142.5 236.4 %all-gather.30.cloned.1.call-done = bf16[1536,6912]{1,0:T(8,128)(2,1)} async-done(((bf16[1536,3456]{1,0:T(8,128)(2,1)}), bf16[1536,6912]{1,0:T(8,128)(2,1)}) %all-gather.30.cloned.1.call-update) | async-done | bytes 21233680 | tf_op jit(solution)/shard_map/all_gather | solution.py:79
  1379.0 18.6 multiply_convert_fusion
  1397.5 12.2 fusion.39
  1409.8 13.6 multiply_reduce_fusion
  1423.4 1.8 subtract_add_fusion
  1425.2 3.6 convolution_convert_fusion.4
  1428.9 3.6 convolution_bitcast_fusion.1
  1432.6 0.7 multiply_reduce_fusion.3
  1433.7 1.3 collective-permute-start.1
  1435.3 1.4 collective-permute-done.1
  1437.3 0.7 copy-done.16
  1438.7 7.9 convolution_convert_fusion.3
  1446.6 1.0 copy-done.22
  1447.6 12.4 fusion
  1460.0 12.1 convolution_convert_fusion.1
  1472.1 28.2 copy.38
  1500.4 12.3 convolution_convert_fusion.2
  1512.7 27.0 copy.36
  1539.8 1.2 copy.34
  1541.1 4.1 convert_element_type.161
  1545.3 107.4 %reduce-scatter.20.cloned.1.call-done = bf16[1536,3,768]{2,0,1:T(8,128)(2,1)} async-done(((bf16[1536,3,1536]{2,0,1:T(8,128)(2,1)}), bf16[1536,3,768]{2,0,1:T(8,128)(2,1)}) %reduce-scatter.20.cloned.1.call-update) | async-done | bytes 7077904 | tf_op jit(solution)/shard_map/reduce_scatter | solution.py:184
  1652.7 9.8 convert_element_type.159
  1662.5 229.6 %reduce-scatter.32.cloned.1.call-done = bf16[1536,3456]{0,1:T(8,128)(2,1)} async-done(((bf16[1536,6912]{0,1:T(8,128)(2,1)}), bf16[1536,3456]{0,1:T(8,128)(2,1)}) %reduce-scatter.32.cloned.1.call-update) | async-done | bytes 10616848 | tf_op jit(solution)/shard_map/reduce_scatter | solution.py:143
  1892.1 15.3 copy.40
  1907.5 223.8 %reduce-scatter.38.cloned.1.call-done = bf16[3456,1536]{1,0:T(8,128)(2,1)} async-done(((bf16[6912,1536]{1,0:T(8,128)(2,1)}), bf16[3456,1536]{1,0:T(8,128)(2,1)}) %reduce-scatter.38.cloned.1.call-update) | async-done | bytes 10616848
  2131.4 14.1 copy.39
  2145.4 11.9 convert_element_type.165
  2157.4 213.3 %reduce-scatter.36.cloned.1.call-done = bf16[3456,1536]{1,0:T(8,128)(2,1)} async-done(((bf16[6912,1536]{1,0:T(8,128)(2,1)}), bf16[3456,1536]{1,0:T(8,128)(2,1)}) %reduce-scatter.36.cloned.1.call-update) | async-done | bytes 10616848
  2370.7 13.9 copy.37
  2384.6 11.9 convert_element_type.163
  2397.8 12.9 fusion.2
  2410.8 8.3 fusion.17
  2419.0 61.7 %all-reduce.8 = (f32[1536]{0:T(1024)S(1)}, f32[1536]{0:T(1024)S(1)}) all-reduce(f32[1536]{0:T(1024)S(1)} %get-tuple-element.55, f32[1536]{0:T(1024)S(1)} %copy-done.27), channel_id=2, replica_groups=mesh['seq'=16,'fsdp'=2] {'seq'}, use_global_device_ids=true, to_apply=%region_5.6.clone | all-reduce | flops 3072 | bytes 24576
  2480.9 1.2 fusion.24
  2482.1 0.9 copy.35
  2483.0 5.5 all-reduce.9
  2488.5 21.7 reduce-scatter.26.cloned.1.call-done
  2510.2 149.3 %reduce-scatter.22.cloned.1.call-done = f32[96,3,768]{2,0,1:T(8,128)} async-done(((f32[1536,3,768]{2,0,1:T(8,128)}), f32[96,3,768]{2,0,1:T(8,128)}) %reduce-scatter.22.cloned.1.call-update) | async-done | bytes 884752 | tf_op jit(solution)/shard_map/reduce_scatter | solution.py:193
  2659.5 216.7 %reduce-scatter.40.cloned.1.call-done = f32[96,3456]{1,0:T(8,128)} async-done(((f32[1536,3456]{1,0:T(8,128)}), f32[96,3456]{1,0:T(8,128)}) %reduce-scatter.40.cloned.1.call-update) | async-done | bytes 1327120
  2876.1 217.1 %reduce-scatter.30.cloned.1.call-done = f32[96,3456]{1,0:T(8,128)} async-done(((f32[1536,3456]{1,0:T(8,128)}), f32[96,3456]{1,0:T(8,128)}) %reduce-scatter.30.cloned.1.call-update) | async-done | bytes 1327120 | tf_op jit(solution)/shard_map/reduce_scatter | solution.py:150
  3093.2 216.7 %reduce-scatter.28.cloned.1.call-done = f32[96,3456]{1,0:T(8,128)} async-done(((f32[1536,3456]{1,0:T(8,128)}), f32[96,3456]{1,0:T(8,128)}) %reduce-scatter.28.cloned.1.call-update) | async-done | bytes 1327120 | tf_op jit(solution)/shard_map/reduce_scatter | solution.py:149
  (134 shorter events, 8.1 us)
Async XLA Ops:
  7.2 72.5 %all-gather.12.cloned.1.call-start = ((), (), s32[]{:S(2)}) async-start(), calls=%async_computation.11 | async-start | bytes 7520256 | tf_op jit(solution)/shard_map/all_gather | solution.py:59
  7.9 114.9 %all-gather.16.cloned.1.call-start = ((), (), s32[]{:S(2)}) async-start(), calls=%async_computation.13 | async-start | bytes 2506752 | tf_op jit(solution)/shard_map/all_gather | solution.py:61
  8.7 203.9 %all-gather.24.cloned.1.call-start = ((), (), s32[]{:S(2)}) async-start(), calls=%async_computation.17 | async-start | bytes 11280384 | tf_op jit(solution)/shard_map/all_gather | solution.py:73
  9.4 292.2 %all-gather.20.cloned.1.call-start = ((), (), s32[]{:S(2)}) async-start(), calls=%async_computation.15 | async-start | bytes 11280384 | tf_op jit(solution)/shard_map/all_gather | solution.py:72
  10.0 380.6 %all-gather.28.cloned.1.call-start = ((), (), s32[]{:S(2)}) async-start(), calls=%async_computation.19 | async-start | bytes 11280384 | tf_op jit(solution)/shard_map/all_gather | solution.py:74
  10.6 549.1 %all-gather.14.cloned.1.call-start = ((), (), s32[]{:S(2)}) async-start(), calls=%async_computation.12 | async-start | bytes 21233664 | tf_op jit(solution)/shard_map/all_gather | solution.py:64
  90.0 533.9 %all-gather.18.cloned.1.call-start = ((), (), s32[]{:S(2)}) async-start(), calls=%async_computation.14 | async-start | bytes 7077888 | tf_op jit(solution)/shard_map/all_gather | solution.py:65
  122.8 752.8 %all-gather.26.cloned.1.call-start = ((), (), s32[]{:S(2)}) async-start(), calls=%async_computation.18 | async-start | bytes 31850496 | tf_op jit(solution)/shard_map/all_gather | solution.py:78
  212.6 914.8 %all-gather.22.cloned.1.call-start = ((), (), s32[]{:S(2)}) async-start(), calls=%async_computation.16 | async-start | bytes 31850496 | tf_op jit(solution)/shard_map/all_gather | solution.py:77
  301.6 1077.3 %all-gather.30.cloned.1.call-start = ((), (), s32[]{:S(2)}) async-start(), calls=%async_computation.20 | async-start | bytes 31850496 | tf_op jit(solution)/shard_map/all_gather | solution.py:79
  390.6 0.7 copy-start.29
  390.6 1.9 copy-start.31
  390.6 2.2 copy-start.32
  390.6 33.8 %copy-start.30 = (bf16[96,3]{0,1:T(4,128)(2,1)S(1)}, bf16[96,3]{0,1:T(4,128)(2,1)}, u32[]{:S(2)}) copy-start(bf16[96,3]{0,1:T(4,128)(2,1)} %param.13) | copy-start | bytes 1732
  390.6 51.2 %copy-start.4 = (bf16[1,192,1536]{2,1,0:T(8,128)(2,1)S(1)}, bf16[1,192,1536]{2,1,0:T(8,128)(2,1)}, u32[]{:S(2)}) copy-start(bf16[1,192,1536]{2,1,0:T(8,128)(2,1)} %param.10) | copy-start | bytes 1769476
  390.7 1150.4 %reduce-scatter.24.cloned.1.call-start = ((), (), s32[]{:S(2)}) async-start(), calls=%async_computation.23 | async-start | bytes 7077888 | tf_op jit(solution)/shard_map/reduce_scatter | solution.py:187
  424.4 1013.7 %copy-start.23 = (f32[1536]{0:T(1024)}, f32[1536]{0:T(1024)S(1)}, u32[]{:S(2)}) copy-start(f32[1536]{0:T(1024)S(1)} %convert_element_type.139) | copy-start | bytes 18436
  442.6 995.6 %copy-start.25 = (f32[192]{0:T(256)}, f32[192]{0:T(256)S(1)}, u32[]{:S(2)}) copy-start(f32[192]{0:T(256)S(1)} %get-tuple-element.80) | copy-start | bytes 2308
  567.5 2.9 copy-start.2
  567.7 2.6 collective-permute-start
  572.1 55.9 %copy-start.12 = (bf16[192,1536]{1,0:T(8,128)(2,1)}, bf16[192,1536]{1,0:T(8,128)(2,1)S(1)}, u32[]{:S(2)}) copy-start(bf16[192,1536]{1,0:T(8,128)(2,1)S(1)} %get-tuple-element.68) | copy-start | bytes 1769476
  628.0 1.1 copy-start.8
  890.8 488.2 %copy-start.20 = (bf16[1,192,1536]{2,1,0:T(8,128)(2,1)S(1)}, bf16[1,192,1536]{2,1,0:T(8,128)(2,1)}, u32[]{:S(2)}) copy-start(bf16[1,192,1536]{2,1,0:T(8,128)(2,1)} %param.19) | copy-start | bytes 1769476
  1397.5 12.2 copy-start.11
  1397.5 12.2 copy-start.9
  1409.8 13.6 copy-start.21
  1423.4 1.8 copy-start.13
  1425.2 3.7 copy-start
  1428.8 223.9 %reduce-scatter.20.cloned.1.call-start = ((), (), s32[]{:S(2)}) async-start(), calls=%async_computation.21 | async-start | bytes 21233664 | tf_op jit(solution)/shard_map/reduce_scatter | solution.py:184
  1428.8 3.6 copy-start.3
  1428.8 3.7 copy-start.7
  1433.3 3.9 copy-start.14
  1433.7 3.1 collective-permute-start.1
  1437.1 0.8 copy-start.16
  1437.2 1.0 copy-start.18
  1437.2 1.5 copy-start.5
  1446.5 1.1 copy-start.22
  1446.6 445.6 %reduce-scatter.32.cloned.1.call-start = ((), (), s32[]{:S(2)}) async-start(), calls=%async_computation.27 | async-start | bytes 31850496 | tf_op jit(solution)/shard_map/reduce_scatter | solution.py:143
  1460.0 671.4 %reduce-scatter.38.cloned.1.call-start = ((), (), s32[]{:S(2)}) async-start(), calls=%async_computation.30 | async-start | bytes 31850496
  1500.4 870.3 %reduce-scatter.36.cloned.1.call-start = ((), (), s32[]{:S(2)}) async-start(), calls=%async_computation.29 | async-start | bytes 31850496
  1539.7 942.4 %reduce-scatter.34.cloned.1.call-start = ((), (), s32[]{:S(2)}) async-start(), calls=%async_computation.28 | async-start | bytes 835584
  1541.0 969.2 %reduce-scatter.26.cloned.1.call-start = ((), (), s32[]{:S(2)}) async-start(), calls=%async_computation.24 | async-start | bytes 5013504 | tf_op jit(solution)/shard_map/reduce_scatter | solution.py:195
  1545.3 1114.2 %reduce-scatter.22.cloned.1.call-start = ((), (), s32[]{:S(2)}) async-start(), calls=%async_computation.22 | async-start | bytes 15040512 | tf_op jit(solution)/shard_map/reduce_scatter | solution.py:193
  1662.5 1213.7 %reduce-scatter.40.cloned.1.call-start = ((), (), s32[]{:S(2)}) async-start(), calls=%async_computation.31 | async-start | bytes 22560768
  1907.5 1185.8 %reduce-scatter.30.cloned.1.call-start = ((), (), s32[]{:S(2)}) async-start(), calls=%async_computation.26 | async-start | bytes 22560768 | tf_op jit(solution)/shard_map/reduce_scatter | solution.py:150
  2157.4 1152.5 %reduce-scatter.28.cloned.1.call-start = ((), (), s32[]{:S(2)}) async-start(), calls=%async_computation.25 | async-start | bytes 22560768 | tf_op jit(solution)/shard_map/reduce_scatter | solution.py:149
  2396.4 1.3 copy-start.10
  2397.7 13.0 copy-start.6
  2397.7 13.0 copy-start.15
  2397.7 13.0 copy-start.17
  2397.7 13.0 copy-start.19
  2397.7 13.0 copy-start.24
  2397.7 13.0 copy-start.26
  2410.7 8.3 copy-start.27
  2410.7 70.2 %copy-start.1 = (f32[192,1536]{1,0:T(8,128)S(1)}, f32[192,1536]{1,0:T(8,128)}, u32[]{:S(2)}) copy-start(f32[192,1536]{1,0:T(8,128)} %copy-done) | copy-start | bytes 3538948
  2410.8 70.1 %copy-start.28 = (f32[192]{0:T(256)S(1)}, f32[192]{0:T(256)}, u32[]{:S(2)}) copy-start(f32[192]{0:T(256)} %get-tuple-element.79) | copy-start | bytes 2308
Sparse Core Ops, SparseCore 0:
  10.3 69.3 all-gather.11
  82.0 40.7 all-gather.15
  125.1 87.4 all-gather.23
  214.7 86.8 all-gather.19
  303.7 86.8 all-gather.27
  392.0 167.5 all-gather.13
  561.2 62.6 all-gather.17
  625.4 250.1 all-gather.25
  877.2 250.1 all-gather.21
  1128.8 250.1 all-gather.29
  1428.9 59.9 reduce-scatter.23
  1491.2 161.4 reduce-scatter.19
  1655.1 237.0 reduce-scatter.31
  1894.3 237.0 reduce-scatter.37
  2133.6 237.0 reduce-scatter.35
  2374.1 56.5 reduce-scatter.33
  2435.4 74.7 reduce-scatter.25
  2514.8 144.6 reduce-scatter.21
  2664.2 211.9 reduce-scatter.39
  2881.2 211.9 reduce-scatter.29
  3097.9 211.9 reduce-scatter.27
where the time goes:
time: 3320 us
  waiting for transfers between devices  2860 us (86%)
  matrix products  160 us (5%)
  local copies, waits for them, and re-layouts  117 us (4%)
  blocking collectives  116 us (3%)
  other arithmetic  45.6 us (1%)
    unnamed x25, waiting for transfers between devices  657 us
    all_gather x1, waiting for transfers between devices, fetch_ffn(): lax.all_gather(w_up, 'fsdp', axis=1, tiled=True)  246 us
    all_gather x1, waiting for transfers between devices, fetch_ffn(): lax.all_gather(w_gate, 'fsdp', axis=1, tiled=True)  237 us
    all_gather x1, waiting for transfers between devices, fetch_ffn(): lax.all_gather(w_down, 'fsdp', axis=1, tiled=True)  236 us
    reduce_scatter x1, waiting for transfers between devices, on_device(): lax.psum_scatter(d_down.astype(jnp.bfloat16), 'fsdp', scatter_dimension=1...  230 us
    reduce_scatter x1, waiting for transfers between devices, on_device(): lax.psum_scatter(d_up_w, 'seq', scatter_dimension=0, tiled=True)  217 us
    reduce_scatter x1, waiting for transfers between devices, on_device(): lax.psum_scatter(d_gate_w, 'seq', scatter_dimension=0, tiled=True)  217 us
    reduce_scatter x1, waiting for transfers between devices, on_device(): lax.psum_scatter(d_in_w, 'seq', scatter_dimension=0, tiled=True)  149 us
  transfers between devices with their start and end apart: 23, of which 21 were waited for; matrix products, arithmetic and copies ran while one was open for 8% of the time, Pallas kernels for 0%

commit v1 on v0

v1 whole, which is shorter than its diff:
```python
import jax
import jax.numpy as jnp
from jax import lax
from jax.sharding import PartitionSpec as P

SEQS = 3
EPSILON = 1e-05
BOTH = ("seq", "fsdp")


def times_transposed(left, right):
    return lax.dot_general(
        left, right, (((1,), (1,)), ((), ())), preferred_element_type=jnp.float32
    )


def transposed_times(left, right):
    return lax.dot_general(
        left, right, (((0,), (0,)), ((), ())), preferred_element_type=jnp.float32
    )


def times(left, right):
    return jnp.dot(left, right, preferred_element_type=jnp.float32)


def root_norm(hidden, gain):
    scale = lax.rsqrt(jnp.mean(hidden * hidden, axis=-1, keepdims=True) + EPSILON)
    return (hidden * scale * gain, scale)


def norm_back(grad, hidden, scale, gain):
    weighted = grad * gain
    inner = jnp.sum(weighted * hidden, axis=-1, keepdims=True)
    d_hidden = scale * weighted - hidden * (scale * scale * scale) * inner / hidden.shape[-1]
    d_gain = jnp.sum(grad * hidden * scale, axis=0)
    return (d_hidden, d_gain)


def device(z, y, c, x):
    return (z * 4 + y * 2 + c) * 2 + x


def every(planes):
    return [
        (z, y, c, x) for z in range(planes) for y in range(2) for c in range(2) for x in range(2)
    ]


def on_device(
    tokens,
    norm1_gain,
    in_weight,
    conv_kernel,
    out_weight,
    norm2_gain,
    gate_weight,
    up_weight,
    down_weight,
    d_out,
):
    planes = lax.axis_size("seq") // 4
    here = lax.axis_index("seq")
    y, c, x = (here // 2) % 2, here % 2, lax.axis_index("fsdp")
    z = here // 4
    rows, width = tokens.shape[1:]
    share = gate_weight.shape[0]
    plane_groups = [
        [device(z, y, c, x) for x in range(2) for y in range(2)]
        for z in range(planes)
        for c in range(2)
    ]
    column_groups = [
        [z * 4 + y * 2 + c for z in range(planes) for c in range(2)] for y in range(2)
    ]
    members = 2 * planes

    def moved(value, target):
        pairs = []
        for place in every(planes):
            to = target(*place)
            if to is not None:
                pairs.append((device(*place), device(*to)))
        return lax.ppermute(value, BOTH, pairs)

    def swap_y(value):
        return moved(value, lambda z, y, c, x: (z, 1 - y, c, x))

    def swap_x(value):
        return moved(value, lambda z, y, c, x: (z, y, c, 1 - x))

    def swap_both(value):
        return moved(value, lambda z, y, c, x: (z, 1 - y, c, 1 - x))

    def ordered(first, second, flag):
        return jnp.where(flag == 0, jnp.stack([first, second]), jnp.stack([second, first]))

    def plane_gather(value):
        by_y = ordered(value, swap_y(value), y)
        other = ordered(swap_x(value), swap_both(value), y)
        return ordered(by_y, other, x).reshape((4 * value.shape[0],) + value.shape[1:])

    def plane_sum(partial):
        sent = partial.astype(jnp.bfloat16).reshape(4, rows, width)
        got = lax.all_to_all(sent, BOTH, 0, 0, axis_index_groups=plane_groups, tiled=True)
        return jnp.sum(got.astype(jnp.float32), axis=0)

    def fetch(weight):
        halves = weight.reshape(share, 2, -1)
        mine = jnp.where(y == 0, halves[:, 0], halves[:, 1])
        theirs = jnp.where(y == 0, halves[:, 1], halves[:, 0])
        pair = ordered(mine, swap_y(theirs), y)
        got = lax.all_gather(pair, "seq", axis=0, tiled=False, axis_index_groups=column_groups)
        got = got.reshape(planes, 2, 2, share, -1)
        return jnp.swapaxes(got, 1, 2).reshape(width, -1)

    def give(grad):
        sent = grad.astype(jnp.bfloat16).reshape(planes, 2, 2, share, -1)
        sent = jnp.swapaxes(sent, 1, 2).reshape(members * 2, share, -1)
        got = lax.psum_scatter(
            sent, "seq", scatter_dimension=0, tiled=True, axis_index_groups=column_groups
        )
        mine = jnp.where(y == 0, got[0], got[1])
        theirs = jnp.where(y == 0, got[1], got[0])
        pair = ordered(mine, swap_y(theirs), y).astype(jnp.float32)
        return jnp.concatenate([pair[0], pair[1]], axis=1)

    gains = lax.all_gather(
        jnp.concatenate(
            [norm1_gain[:, None], norm2_gain[:, None], conv_kernel], axis=1
        ),
        "seq",
        axis=0,
        tiled=True,
    ).astype(jnp.float32)
    gain_one, gain_two, kernel = gains[:, 0], gains[:, 1], gains[:, 2:]
    taps = kernel.shape[1]
    margin = taps - 1
    channels = in_weight.shape[2] // 2
    first_channel = x * (2 * channels) + y * channels
    kernel_here = lax.dynamic_slice_in_dim(kernel, first_channel, channels, 0)

    w_in_halves = jnp.swapaxes(in_weight.reshape(share, 3, 2, channels), 1, 2)
    w_mixer = fetch(
        jnp.concatenate(
            [w_in_halves.reshape(share, 2, 3 * channels), out_weight.reshape(share, 2, channels)],
            axis=2,
        ).reshape(share, 8 * channels)
    )
    w_in, w_out = w_mixer[:, : 3 * channels], w_mixer[:, 3 * channels :]

    hidden = tokens[0].astype(jnp.float32)
    normed, scale_one = root_norm(hidden, gain_one)
    normed_low = plane_gather(normed.astype(jnp.bfloat16))
    grad_low = plane_gather(d_out[0])

    w_gate = fetch(gate_weight)
    w_up = fetch(up_weight)
    w_down = fetch(down_weight)

    projected = times(normed_low, w_in).reshape(2, 2, rows, 3 * channels)
    b_part = projected[..., :channels]
    c_part = projected[..., channels : 2 * channels]
    x_part = projected[..., 2 * channels :]
    gated = (b_part * x_part).astype(jnp.bfloat16)

    def swap_core(value):
        return moved(value, lambda z, y, c, x: (z, y, 1 - c, x))

    def to_next(value):
        return moved(
            value, lambda z, y, c, x: (z + 1, y, 0, x) if c == 1 and z + 1 < planes else None
        )

    def to_last(value):
        return moved(value, lambda z, y, c, x: (z - 1, y, 1, x) if c == 0 and z > 0 else None)

    tail = gated[:, :, rows - margin :]
    from_core, from_plane = swap_core(tail), to_next(tail[:, 1])
    before = jnp.where(
        c == 1, from_core, jnp.stack([from_plane, from_core[:, 0]], axis=1)
    )
    padded = jnp.concatenate([before, gated], axis=2).astype(jnp.float32)
    seq_len = lax.axis_size("seq") * rows // SEQS
    block = z * 4 + jnp.arange(2, dtype=jnp.int32) * 2 + c
    position = block[:, None] * rows + jnp.arange(rows, dtype=jnp.int32)
    in_sequence = position % seq_len
    masks = [
        (in_sequence >= margin - offset).astype(jnp.float32)[None, :, :, None]
        for offset in range(taps)
    ]
    conv = jnp.zeros_like(b_part)
    for offset in range(taps):
        conv = conv + masks[offset] * padded[:, :, offset : offset + rows] * kernel_here[:, offset]
    mixed = (c_part * conv).astype(jnp.bfloat16).reshape(4 * rows, channels)
    hidden_one = hidden + plane_sum(times_transposed(mixed, w_out))

    normed_two, scale_two = root_norm(hidden_one, gain_two)
    normed_two_low = plane_gather(normed_two.astype(jnp.bfloat16))
    gate = times(normed_two_low, w_gate)
    upper = times(normed_two_low, w_up)
    sigma = jax.nn.sigmoid(gate)
    active = (gate * sigma * upper).astype(jnp.bfloat16)
    d_active = times(grad_low, w_down)
    d_upper = (d_active * gate * sigma).astype(jnp.bfloat16)
    d_gate = (d_active * upper * sigma * (1.0 + gate * (1.0 - sigma))).astype(jnp.bfloat16)
    d_normed_two = plane_sum(times_transposed(d_gate, w_gate) + times_transposed(d_upper, w_up))
    result = hidden_one + plane_sum(times_transposed(active, w_down))
    d_gate_w = give(transposed_times(normed_two_low, d_gate))
    d_up_w = give(transposed_times(normed_two_low, d_upper))
    d_down_w = give(transposed_times(grad_low, active))

    d_hidden_two, d_gain_two = norm_back(d_normed_two, hidden_one, scale_two, gain_two)
    grad_one = d_out[0].astype(jnp.float32) + d_hidden_two
    grad_one_low = plane_gather(grad_one.astype(jnp.bfloat16))
    d_out_w = transposed_times(grad_one_low, mixed)
    d_mixed = times(grad_one_low, w_out).reshape(2, 2, rows, channels)
    d_c = d_mixed * conv
    d_conv = d_mixed * c_part
    kernel_cols = []
    d_padded = jnp.zeros((2, 2, rows + margin, channels), jnp.float32)
    for offset in range(taps):
        masked = masks[offset] * d_conv
        kernel_cols.append(jnp.sum(masked * padded[:, :, offset : offset + rows], axis=(0, 1, 2)))
        d_padded = d_padded + jnp.pad(
            masked * kernel_here[:, offset],
            ((0, 0), (0, 0), (offset, margin - offset), (0, 0)),
        )
    head = d_padded[:, :, :margin]
    from_core, from_plane = swap_core(head), to_last(head[:, 0])
    after = jnp.where(c == 0, from_core, jnp.stack([from_core[:, 1], from_plane], axis=1))
    d_gated = d_padded[:, :, margin:] + jnp.pad(
        after, ((0, 0), (0, 0), (rows - margin, 0), (0, 0))
    )
    d_projected = (
        jnp.concatenate([d_gated * x_part, d_c, d_gated * b_part], axis=3)
        .astype(jnp.bfloat16)
        .reshape(4 * rows, 3 * channels)
    )
    d_in_w = transposed_times(normed_low, d_projected)
    d_normed = plane_sum(times_transposed(d_projected, w_in))
    d_mixer = give(jnp.concatenate([d_in_w, d_out_w], axis=1)).reshape(share, 2, 4 * channels)
    d_in_w = jnp.swapaxes(d_mixer[:, :, : 3 * channels].reshape(share, 2, 3, channels), 1, 2)
    d_in_w = d_in_w.reshape(share, 3, 2 * channels)
    d_out_w = d_mixer[:, :, 3 * channels :].reshape(share, 2 * channels)
    d_hidden, d_gain_one = norm_back(d_normed, hidden, scale_one, gain_one)
    d_tokens = (grad_one + d_hidden).astype(jnp.bfloat16)

    d_kernel = lax.dynamic_update_slice(
        jnp.zeros((width, taps), jnp.float32), jnp.stack(kernel_cols, axis=1), (first_channel, 0)
    )
    small = jnp.concatenate([d_gain_one[:, None], d_gain_two[:, None], d_kernel], axis=1)
    small = lax.psum(small, BOTH)
    small = lax.dynamic_slice_in_dim(small, here * share, share, 0)
    return (
        result.astype(jnp.bfloat16)[None],
        d_tokens[None],
        small[:, 0],
        d_in_w,
        small[:, 2:],
        d_out_w,
        small[:, 1],
        d_gate_w,
        d_up_w,
        d_down_w,
    )


def solution(mesh):
    return jax.shard_map(
        on_device,
        mesh=mesh,
        in_specs=(
            P("fsdp", "seq", None),
            P("seq"),
            P("seq", None, "fsdp"),
            P("seq", None),
            P("seq", "fsdp"),
            P("seq"),
            P("seq", "fsdp"),
            P("seq", "fsdp"),
            P("seq", "fsdp"),
            P("fsdp", "seq", None),
        ),
        out_specs=(
            P("fsdp", "seq", None),
            P("fsdp", "seq", None),
            P("seq"),
            P("seq", None, "fsdp"),
            P("seq", None),
            P("seq", "fsdp"),
            P("seq"),
            P("seq", "fsdp"),
            P("seq", "fsdp"),
            P("seq", "fsdp"),
        ),
        check_vma=False,
    )
```

time: 3320 us -> 640 us (0.19)
  waiting for transfers between devices: 2860 us -> 282 us
  matrix products: 160 us -> 96.6 us
  blocking collectives: 116 us -> 62.2 us
  starting transfers between devices: 4.08 us -> 48.8 us
  local copies, waits for them, and re-layouts: 117 us -> 74.9 us
    all_gather x10 -> x4, waiting for transfers between devices: 1260 us -> 44.7 us  [fetch(): lax.all_gather(pair, 'seq', axis=0, tiled=False, axis_index_groups=column...]
    reduce_scatter x7 -> x4, waiting for transfers between devices: 942 us -> 0.02 us  [give(): lax.psum_scatter(sent, 'seq', scatter_dimension=0, tiled=True, axis_index...]
    unnamed x25 -> x8, waiting for transfers between devices: 657 us -> 0.13 us
    ppermute x2 -> x24, waiting for transfers between devices: 1.99 us -> 169 us  [moved(): return lax.ppermute(value, BOTH, pairs)]
    unnamed x80 -> x116, local copies, waits for them, and re-layouts: 106 us -> 5.77 us
    unnamed x2 -> x0, blocking collectives: 93.1 us -> none
    all_to_all x0 -> x4, waiting for transfers between devices: none -> 68 us  [plane_sum(): lax.all_to_all(sent, BOTH, 0, 0, axis_index_groups=plane_groups, tiled=True)]
    psum x1, blocking collectives: 5.51 us -> 40.6 us  [on_device(): small = lax.psum(small, BOTH)]
  transfers between devices with their start and end apart: 23 -> 36, of which waited for: 21 -> 22; matrix products, arithmetic and copies ran while one was open for 8% -> 26% of each run, Pallas kernels for 0% -> 0%
where the time goes in v1:
time: 640 us; the launch traced here: 631 us
  waiting for transfers between devices  282 us (44%)
  matrix products  96.6 us (15%)
  local copies, waits for them, and re-layouts  74.9 us (12%)
  blocking collectives  62.2 us (10%)
  other arithmetic  50.8 us (8%)
  starting transfers between devices  48.8 us (8%)
  between operations  15.9 us (2%)
    ppermute x24, waiting for transfers between devices, moved(): return lax.ppermute(value, BOTH, pairs)  169 us
    all_to_all x4, waiting for transfers between devices, plane_sum(): lax.all_to_all(sent, BOTH, 0, 0, axis_index_groups=plane_groups, tiled=True)  68 us
    all_gather x4, waiting for transfers between devices, fetch(): lax.all_gather(pair, 'seq', axis=0, tiled=False, axis_index_groups=column...  44.7 us
    psum x1, blocking collectives, on_device(): small = lax.psum(small, BOTH)  40.6 us
    dot_general x5, matrix products, times_transposed(): lax.dot_general(left, right, (((1,), (1,)), ((), ())), preferred_element_...  36.5 us
    dot_general x5, matrix products, times(): return jnp.dot(left, right, preferred_element_type=jnp.float32)  31.1 us
    ppermute x24, starting transfers between devices, moved(): return lax.ppermute(value, BOTH, pairs)  29.8 us
    dot_general x5, matrix products, transposed_times(): lax.dot_general(left, right, (((0,), (0,)), ((), ())), preferred_element_...  29 us
  transfers between devices with their start and end apart: 36, of which 22 were waited for; matrix products, arithmetic and copies ran while one was open for 26% of the time, Pallas kernels for 0%

profile of v1, /device:TPU:0, one launch (start us, length us, event | category | flops | bytes accessed | tf_op | source)
XLA Modules:
  0.0 630.9 jit_solution(17432788080722247980)
XLA Ops:
  9.8 3.0 collective-permute-start.3
  12.8 7.0 %collective-permute-done.3 = bf16[96,1536]{1,0:T(8,128)(2,1)S(1)} collective-permute-done((bf16[96,1536]{1,0:T(8,128)(2,1)S(1)}, bf16[96,1536]{1,0:T(8,128)(2,1)S(1)}, u32[]{:S(2)}, u32[]{:S(2)}) %collective-permute-start.3) | collective-permute-done | bytes 294944 | tf_op jit(solution)/shard_map/ppermute | solution.py:84
  25.0 7.5 %collective-permute-done.10 = bf16[96,1728]{1,0:T(8,128)(2,1)S(1)} collective-permute-done((bf16[96,1728]{1,0:T(8,128)(2,1)S(1)}, bf16[96,1728]{1,0:T(8,128)(2,1)S(1)}, u32[]{:S(2)}, u32[]{:S(2)}) %collective-permute-start.10) | collective-permute-done | bytes 331808 | tf_op jit(solution)/shard_map/ppermute | solution.py:84
  37.4 6.8 %collective-permute-done.9 = bf16[96,1728]{1,0:T(8,128)(2,1)S(1)} collective-permute-done((bf16[96,1728]{1,0:T(8,128)(2,1)S(1)}, bf16[96,1728]{1,0:T(8,128)(2,1)S(1)}, u32[]{:S(2)}, u32[]{:S(2)}) %collective-permute-start.9) | collective-permute-done | bytes 331808 | tf_op jit(solution)/shard_map/ppermute | solution.py:84
  48.9 6.3 %collective-permute-done.11 = bf16[96,1728]{1,0:T(8,128)(2,1)S(1)} collective-permute-done((bf16[96,1728]{1,0:T(8,128)(2,1)S(1)}, bf16[96,1728]{1,0:T(8,128)(2,1)S(1)}, u32[]{:S(2)}, u32[]{:S(2)}) %collective-permute-start.11) | collective-permute-done | bytes 331808 | tf_op jit(solution)/shard_map/ppermute | solution.py:84
  56.3 21.6 %all-gather = bf16[16,96,5]{1,2,0:T(8,128)(2,1)S(1)} all-gather(bf16[1,96,5]{1,2,0:T(8,128)(2,1)S(1)} %maximum_bitcast_fusion), channel_id=1, replica_groups=mesh['seq'=16,'fsdp'=2] {'seq'}, dimensions={0}, use_global_device_ids=true | all-gather | bytes 16320 | tf_op jit(solution)/shard_map/all_gather | solution.py:128
  81.4 2.0 collective-permute-start
  84.1 12.1 %collective-permute-done.1 = bf16[192,1536]{1,0:T(8,128)(2,1)S(1)} collective-permute-done((bf16[192,1536]{1,0:T(8,128)(2,1)}, bf16[192,1536]{1,0:T(8,128)(2,1)S(1)}, u32[]{:S(2)}, u32[]{:S(2)}) %collective-permute-start.1) | collective-permute-done | bytes 589856 | tf_op jit(solution)/shard_map/ppermute | solution.py:84
  96.2 11.2 %collective-permute-done.2 = bf16[192,1536]{1,0:T(8,128)(2,1)S(1)} collective-permute-done((bf16[192,1536]{1,0:T(8,128)(2,1)}, bf16[192,1536]{1,0:T(8,128)(2,1)S(1)}, u32[]{:S(2)}, u32[]{:S(2)}) %collective-permute-start.2) | collective-permute-done | bytes 589856 | tf_op jit(solution)/shard_map/ppermute | solution.py:84
  109.8 3.1 copy.237
  112.9 3.3 fusion.1
  119.7 3.3 multiply_convert_fusion.8
  123.1 4.3 convolution_convert_fusion.4
  127.4 4.6 all-to-all-start
  132.1 1.9 collective-permute-start.13
  135.6 37.8 %collective-permute-done.13 = bf16[192,1536]{1,0:T(8,128)(2,1)S(1)} collective-permute-done((bf16[192,1536]{1,0:T(8,128)(2,1)S(1)}, bf16[192,1536]{1,0:T(8,128)(2,1)S(1)}, u32[]{:S(2)}, u32[]{:S(2)}) %collective-permute-start.13) | collective-permute-done | bytes 589856 | tf_op jit(solution)/shard_map/ppermute | solution.py:84
  173.4 13.5 %collective-permute-done.14 = bf16[192,1536]{1,0:T(8,128)(2,1)S(1)} collective-permute-done((bf16[192,1536]{1,0:T(8,128)(2,1)S(1)}, bf16[192,1536]{1,0:T(8,128)(2,1)S(1)}, u32[]{:S(2)}, u32[]{:S(2)}) %collective-permute-start.14) | collective-permute-done | bytes 589856 | tf_op jit(solution)/shard_map/ppermute | solution.py:84
  188.4 2.1 convert_reduce_fusion.3
  194.8 5.4 copy.240
  200.1 5.8 copy.239
  205.9 44.7 %all-gather.12.cloned.1.call-done = bf16[8,2,96,1728]{3,2,1,0:T(8,128)(2,1)} async-done(((bf16[1,2,96,1728]{3,2,1,0:T(8,128)(2,1)}), bf16[8,2,96,1728]{3,2,1,0:T(8,128)(2,1)}) %all-gather.12.cloned.1.call-update) | async-done | bytes 5308432 | tf_op jit(solution)/shard_map/all_gather | solution.py:113
  250.6 3.1 copy.241
  258.4 11.8 %collective-permute-done.7 = bf16[192,1536]{1,0:T(8,128)(2,1)S(1)} collective-permute-done((bf16[192,1536]{1,0:T(8,128)(2,1)}, bf16[192,1536]{1,0:T(8,128)(2,1)S(1)}, u32[]{:S(2)}, u32[]{:S(2)}) %collective-permute-start.7) | collective-permute-done | bytes 589856 | tf_op jit(solution)/shard_map/ppermute | solution.py:84
  270.1 12.9 %collective-permute-done.8 = bf16[192,1536]{1,0:T(8,128)(2,1)S(1)} collective-permute-done((bf16[192,1536]{1,0:T(8,128)(2,1)}, bf16[192,1536]{1,0:T(8,128)(2,1)S(1)}, u32[]{:S(2)}, u32[]{:S(2)}) %collective-permute-start.8) | collective-permute-done | bytes 589856 | tf_op jit(solution)/shard_map/ppermute | solution.py:84
  283.6 6.6 %fusion.59 = f32[768,1728]{0,1:T(8,128)} fusion(bf16[768,1536]{1,0:T(8,128)(2,1)S(1)} %bitcast.293, bf16[1536,1728]{1,0:T(8,128)(2,1)S(1)} %bitcast.273), kind=kOutput, calls=%fused_computation.193 | convolution fusion | flops 4076863488 | bytes 12976128 | tf_op jit(solution)/shard_map/dot_general | solution.py:24
  290.3 6.2 fusion.58
  296.5 11.8 %multiply_convert_fusion = (bf16[768,1728]{0,1:T(8,128)(2,1)}, bf16[768,1728]{0,1:T(8,128)(2,1)}, bf16[768,1728]{0,1:T(8,128)(2,1)S(1)}) fusion(f32[768,1728]{0,1:T(8,128)} %fusion.58, f32[768,1728]{0,1:T(8,128)} %fusion.59, bf16[768,1536]{1,0:T(8,128)(2,1)} %bitcast.291, bf16[1536,1728]{1,0:T(8,128)(2,1)S(1)} %bitcast.274), kind=kOutput, calls=%fused_computation.5 | convolution fusion | flops 4098097152 | bytes 26247168 | tf_op jit(solution)/shard_map/dot_general | solution.py:24
  309.8 5.9 convolution_convert_fusion
  315.8 7.8 %copy.254 = bf16[1536,1728]{1,0:T(8,128)(2,1)} copy(bf16[1536,1728]{0,1:T(8,128)(2,1)} %convolution_convert_fusion) | data formatting | bytes 10616832 | tf_op jit(solution)/shard_map/convert_element_type | solution.py:118
  323.6 5.4 copy.255
  329.2 9.1 %convolution_convert_fusion.1 = bf16[1536,1728]{0,1:T(8,128)(2,1)} fusion(bf16[768,1728]{0,1:T(8,128)(2,1)} %get-tuple-element.27, bf16[768,1536]{1,0:T(8,128)(2,1)} %bitcast.295), kind=kOutput, calls=%fused_computation.3 | convolution fusion | flops 4079517696 | bytes 10321920 | tf_op jit(solution)/shard_map/dot_general | solution.py:18
  338.3 8.0 %copy.252 = bf16[1536,1728]{1,0:T(8,128)(2,1)} copy(bf16[1536,1728]{0,1:T(8,128)(2,1)} %convolution_convert_fusion.1) | data formatting | bytes 10616832 | tf_op jit(solution)/shard_map/convert_element_type | solution.py:118
  346.3 5.4 copy.253
  351.8 9.1 %convolution_convert_fusion.2 = bf16[1536,1728]{0,1:T(8,128)(2,1)} fusion(bf16[768,1728]{0,1:T(8,128)(2,1)} %get-tuple-element.28, bf16[768,1536]{1,0:T(8,128)(2,1)} %bitcast.296), kind=kOutput, calls=%fused_computation.4 | convolution fusion | flops 4079517696 | bytes 10321920 | tf_op jit(solution)/shard_map/dot_general | solution.py:18
  360.9 8.0 %copy.250 = bf16[1536,1728]{1,0:T(8,128)(2,1)} copy(bf16[1536,1728]{0,1:T(8,128)(2,1)} %convolution_convert_fusion.2) | data formatting | bytes 10616832 | tf_op jit(solution)/shard_map/convert_element_type | solution.py:118
  368.9 5.3 copy.251
  374.3 7.6 %fusion.60 = f32[768,1536]{1,0:T(8,128)S(1)} fusion(bf16[768,1728]{0,1:T(8,128)(2,1)} %get-tuple-element.28, bf16[1536,1728]{1,0:T(8,128)(2,1)} %bitcast.276), kind=kOutput, calls=%fused_computation.194 | convolution fusion | flops 4076863488 | bytes 12681216 | tf_op jit(solution)/shard_map/dot_general | solution.py:12
  381.9 8.5 %add_convert_fusion = bf16[768,1536]{1,0:T(8,128)(2,1)} fusion(f32[768,1536]{1,0:T(8,128)S(1)} %fusion.60, bf16[768,1728]{0,1:T(8,128)(2,1)S(1)} %copy-done.48, bf16[1536,1728]{1,0:T(8,128)(2,1)} %bitcast.270), kind=kOutput, calls=%fused_computation.12 | convolution fusion | flops 4079222784 | bytes 15040512 | tf_op jit(solution)/shard_map/dot_general | solution.py:12
  390.4 4.7 all-to-all-start.2
  395.1 9.6 %convolution_convert_fusion.5 = bf16[768,1536]{1,0:T(8,128)(2,1)} fusion(bf16[768,1728]{0,1:T(8,128)(2,1)} %copy-done.49, bf16[1536,1728]{1,0:T(8,128)(2,1)} %bitcast.275), kind=kOutput, calls=%fused_computation.19 | convolution fusion | flops 4078043136 | bytes 10321920 | tf_op jit(solution)/shard_map/dot_general | solution.py:12
  404.7 18.0 %all-to-all-done.2 = bf16[4,192,1536]{2,1,0:T(8,128)(2,1)} async-done(((bf16[4,192,1536]{2,1,0:T(8,128)(2,1)}), bf16[4,192,1536]{2,1,0:T(8,128)(2,1)}, u32[]{:S(2)}, u32[]{:S(2)}) %all-to-all-start.2) | async-done | bytes 2359328 | tf_op jit(solution)/shard_map/all_to_all | solution.py:105
  422.7 4.5 all-to-all-start.1
  427.3 2.2 convert_reduce_fusion.1
  431.8 1.9 collective-permute-start.15
  435.3 21.1 %all-to-all-done.1 = bf16[4,192,1536]{2,1,0:T(8,128)(2,1)} async-done(((bf16[4,192,1536]{2,1,0:T(8,128)(2,1)}), bf16[4,192,1536]{2,1,0:T(8,128)(2,1)}, u32[]{:S(2)}, u32[]{:S(2)}) %all-to-all-start.1) | async-done | bytes 2359328 | tf_op jit(solution)/shard_map/all_to_all | solution.py:105
  456.4 2.2 convert_reduce_fusion.2
  458.6 2.4 convert_bitcast_fusion.1
  461.0 7.0 %collective-permute-done.15 = bf16[192,1536]{1,0:T(8,128)(2,1)} collective-permute-done((bf16[192,1536]{1,0:T(8,128)(2,1)}, bf16[192,1536]{1,0:T(8,128)(2,1)}, u32[]{:S(2)}, u32[]{:S(2)}) %collective-permute-start.15) | collective-permute-done | bytes 589856 | tf_op jit(solution)/shard_map/ppermute | solution.py:84
  469.6 11.0 %collective-permute-done.17 = bf16[192,1536]{1,0:T(8,128)(2,1)} collective-permute-done((bf16[192,1536]{1,0:T(8,128)(2,1)}, bf16[192,1536]{1,0:T(8,128)(2,1)}, u32[]{:S(2)}, u32[]{:S(2)}) %collective-permute-start.17) | collective-permute-done | bytes 589856 | tf_op jit(solution)/shard_map/ppermute | solution.py:84
  482.7 3.1 multiply_reduce_fusion.2
  490.8 3.4 fusion
  494.7 2.7 copy.260
  497.4 6.5 %convolution_convert_fusion.3 = bf16[768,1536]{1,0:T(8,128)(2,1)} fusion(bf16[1536,1536]{1,0:T(8,128)(2,1)} %bitcast.287, bf16[768,384]{1,0:T(8,128)(2,1)S(1)} %bitcast.314, bf16[768,384]{1,0:T(8,128)(2,1)S(1)} %bitcast.332, bf16[768,384]{1,0:T(8,128)(2,1)S(1)} %bitcast.313), kind=kOutput, calls=%fused_computation.17 | convolution fusion | flops 2724397056 | bytes 7667712 | tf_op jit(solution)/shard_map/dot_general | solution.py:12
  504.0 4.7 all-to-all-start.3
  508.8 28.9 %all-to-all-done.3 = bf16[4,192,1536]{2,1,0:T(8,128)(2,1)} async-done(((bf16[4,192,1536]{2,1,0:T(8,128)(2,1)}), bf16[4,192,1536]{2,1,0:T(8,128)(2,1)}, u32[]{:S(2)}, u32[]{:S(2)}) %all-to-all-start.3) | async-done | bytes 2359328 | tf_op jit(solution)/shard_map/all_to_all | solution.py:105
  537.7 2.1 convert_reduce_fusion
  540.3 40.6 %psum.7 = f32[1536,5]{0,1:T(8,128)S(1)} all-reduce(f32[1536,5]{0,1:T(8,128)S(1)} %pad_maximum_fusion.5), channel_id=1, replica_groups=mesh['seq'=16,'fsdp'=2] {'seq','fsdp'}, use_global_device_ids=true, to_apply=%region_13.14 | all-reduce | flops 7680 | bytes 61440 | tf_op jit(solution)/shard_map/psum | solution.py:253
  584.5 2.4 collective-permute-start.23
  589.2 2.0 collective-permute-start.21
  591.3 4.5 collective-permute-done.23
  595.9 7.2 %collective-permute-done.22 = bf16[96,1728]{1,0:T(8,128)(2,1)S(1)} collective-permute-done((bf16[96,1728]{1,0:T(8,128)(2,1)S(1)}, bf16[96,1728]{1,0:T(8,128)(2,1)S(1)}, u32[]{:S(2)}, u32[]{:S(2)}) %collective-permute-start.22) | collective-permute-done | bytes 331808 | tf_op jit(solution)/shard_map/ppermute | solution.py:84
  603.3 5.6 collective-permute-done.21
  609.4 1.9 pad_maximum_fusion.1
  615.5 4.4 collective-permute-done.20
  (258 shorter events, 70.1 us)
Async XLA Ops:
  7.2 102.6 %all-gather.6.cloned.1.call-start = ((), (), s32[]{:S(2)}) async-start(), calls=%async_computation.8 | async-start | bytes 5308416 | tf_op jit(solution)/shard_map/all_gather | solution.py:113
  9.8 11.0 %copy-start.17 = (bf16[96,3456]{1,0:T(8,128)(2,1)S(1)}, bf16[96,3456]{1,0:T(8,128)(2,1)}, u32[]{:S(2)}) copy-start(bf16[96,3456]{1,0:T(8,128)(2,1)} %param.17) | copy-start | bytes 1990660
  9.8 10.0 %collective-permute-start.3 = (bf16[96,1536]{1,0:T(8,128)(2,1)S(1)}, bf16[96,1536]{1,0:T(8,128)(2,1)S(1)}, u32[]{:S(2)}, u32[]{:S(2)}) collective-permute-start(bf16[96,1536]{1,0:T(8,128)(2,1)S(1)} %get-tuple-element.60), channel_id=1, source_target_pairs={{0,4},{1,5},{2,6},{3,7},{4,0},{5,1},{6,2},{7,3},{8,12},{9,13},{10,... | collective-permute-start | bytes 884744 | tf_op jit(solution)/shard_map/ppermute | solution.py:84
  20.7 174.0 %all-gather.10.cloned.1.call-start = ((), (), s32[]{:S(2)}) async-start(), calls=%async_computation.10 | async-start | bytes 6193152 | tf_op jit(solution)/shard_map/all_gather | solution.py:113
  23.1 9.3 %collective-permute-start.10 = (bf16[96,1728]{1,0:T(8,128)(2,1)S(1)}, bf16[96,1728]{1,0:T(8,128)(2,1)S(1)}, u32[]{:S(2)}, u32[]{:S(2)}) collective-permute-start(bf16[96,1728]{1,0:T(8,128)(2,1)S(1)} %bitcast.315), channel_id=1, source_target_pairs={{0,4},{1,5},{2,6},{3,7},{4,0},{5,1},{6,2},{7,3},{8,12},{9,13},{10,... | collective-permute-start | bytes 995336 | tf_op jit(solution)/shard_map/ppermute | solution.py:84
  25.0 8.5 %copy-start.18 = (bf16[96,3456]{1,0:T(8,128)(2,1)S(1)}, bf16[96,3456]{1,0:T(8,128)(2,1)}, u32[]{:S(2)}) copy-start(bf16[96,3456]{1,0:T(8,128)(2,1)} %param.16) | copy-start | bytes 1990660
  33.4 166.7 %all-gather.8.cloned.1.call-start = ((), (), s32[]{:S(2)}) async-start(), calls=%async_computation.9 | async-start | bytes 6193152 | tf_op jit(solution)/shard_map/all_gather | solution.py:113
  35.9 8.4 %collective-permute-start.9 = (bf16[96,1728]{1,0:T(8,128)(2,1)S(1)}, bf16[96,1728]{1,0:T(8,128)(2,1)S(1)}, u32[]{:S(2)}, u32[]{:S(2)}) collective-permute-start(bf16[96,1728]{1,0:T(8,128)(2,1)S(1)} %bitcast.317), channel_id=1, source_target_pairs={{0,4},{1,5},{2,6},{3,7},{4,0},{5,1},{6,2},{7,3},{8,12},{9,13},{10,... | collective-permute-start | bytes 995336 | tf_op jit(solution)/shard_map/ppermute | solution.py:84
  37.4 7.9 %copy-start.19 = (bf16[96,3456]{1,0:T(8,128)(2,1)S(1)}, bf16[96,3456]{1,0:T(8,128)(2,1)}, u32[]{:S(2)}) copy-start(bf16[96,3456]{1,0:T(8,128)(2,1)} %param.18) | copy-start | bytes 1990660
  45.2 205.4 %all-gather.12.cloned.1.call-start = ((), (), s32[]{:S(2)}) async-start(), calls=%async_computation.11 | async-start | bytes 6193152 | tf_op jit(solution)/shard_map/all_gather | solution.py:113
  47.6 7.6 %collective-permute-start.11 = (bf16[96,1728]{1,0:T(8,128)(2,1)S(1)}, bf16[96,1728]{1,0:T(8,128)(2,1)S(1)}, u32[]{:S(2)}, u32[]{:S(2)}) collective-permute-start(bf16[96,1728]{1,0:T(8,128)(2,1)S(1)} %bitcast.319), channel_id=1, source_target_pairs={{0,4},{1,5},{2,6},{3,7},{4,0},{5,1},{6,2},{7,3},{8,12},{9,13},{10,... | collective-permute-start | bytes 995336 | tf_op jit(solution)/shard_map/ppermute | solution.py:84
  48.9 7.4 %copy-start.44 = (bf16[96,3]{0,1:T(4,128)(2,1)S(1)}, bf16[96,3]{0,1:T(4,128)(2,1)}, u32[]{:S(2)}) copy-start(bf16[96,3]{0,1:T(4,128)(2,1)} %param.13) | copy-start | bytes 1732
  48.9 7.4 %copy-start.45 = (bf16[96]{0:T(256)(128)(2,1)S(1)}, bf16[96]{0:T(256)(128)(2,1)}, u32[]{:S(2)}) copy-start(bf16[96]{0:T(256)(128)(2,1)} %param.15) | copy-start | bytes 580
  48.9 7.4 %copy-start.46 = (bf16[96]{0:T(256)(128)(2,1)S(1)}, bf16[96]{0:T(256)(128)(2,1)}, u32[]{:S(2)}) copy-start(bf16[96]{0:T(256)(128)(2,1)} %param.11) | copy-start | bytes 580
  48.9 29.2 %copy-start = (bf16[1,192,1536]{2,1,0:T(8,128)(2,1)S(1)}, bf16[1,192,1536]{2,1,0:T(8,128)(2,1)}, u32[]{:S(2)}) copy-start(bf16[1,192,1536]{2,1,0:T(8,128)(2,1)} %param.10) | copy-start | bytes 1769476
  78.0 6.1 copy-start.24
  78.0 6.1 copy-start.22
  78.9 5.3 copy-start.28
  79.9 16.4 %collective-permute-start.1 = (bf16[192,1536]{1,0:T(8,128)(2,1)}, bf16[192,1536]{1,0:T(8,128)(2,1)S(1)}, u32[]{:S(2)}, u32[]{:S(2)}) collective-permute-start(bf16[192,1536]{1,0:T(8,128)(2,1)} %fusion.23), channel_id=1, source_target_pairs={{0,1},{1,0},{2,3},{3,2},{4,5},{5,4},{6,7},{7,6},{8,9},{9,8},{10,11... | collective-permute-start | bytes 1769480 | tf_op jit(solution)/shard_map/ppermute | solution.py:84
  81.4 26.1 %collective-permute-start.2 = (bf16[192,1536]{1,0:T(8,128)(2,1)}, bf16[192,1536]{1,0:T(8,128)(2,1)S(1)}, u32[]{:S(2)}, u32[]{:S(2)}) collective-permute-start(bf16[192,1536]{1,0:T(8,128)(2,1)} %fusion.23), channel_id=1, source_target_pairs={{0,5},{1,4},{2,7},{3,6},{4,1},{5,0},{6,3},{7,2},{8,13},{9,12},{10,... | collective-permute-start | bytes 1769480 | tf_op jit(solution)/shard_map/ppermute | solution.py:84
  81.4 28.1 %collective-permute-start = (bf16[192,1536]{1,0:T(8,128)(2,1)}, bf16[192,1536]{1,0:T(8,128)(2,1)S(1)}, u32[]{:S(2)}, u32[]{:S(2)}) collective-permute-start(bf16[192,1536]{1,0:T(8,128)(2,1)} %fusion.23), channel_id=1, source_target_pairs={{0,4},{1,5},{2,6},{3,7},{4,0},{5,1},{6,2},{7,3},{8,12},{9,13},{10,... | collective-permute-start | bytes 1769480 | tf_op jit(solution)/shard_map/ppermute | solution.py:84
  107.7 5.2 copy-start.12
  118.3 1.2 collective-permute-start.4
  118.4 1.1 collective-permute-start.5
  123.1 4.3 copy-start.20
  127.4 4.7 copy-start.6
  127.4 61.0 %all-to-all-start = ((bf16[4,192,1536]{2,1,0:T(8,128)(2,1)}), bf16[4,192,1536]{2,1,0:T(8,128)(2,1)}, u32[]{:S(2)}, u32[]{:S(2)}) async-start(bf16[4,192,1536]{2,1,0:T(8,128)(2,1)} %bitcast.20), calls=%async_computation | async-start | bytes 4718592 | tf_op jit(solution)/shard_map/all_to_all | solution.py:105
  132.0 451.3 %reduce-scatter.11.cloned.1.call-start = ((), (), s32[]{:S(2)}) async-start(), calls=%async_computation.15 | async-start | bytes 6193152 | tf_op jit(solution)/shard_map/reduce_scatter | solution.py:120
  132.1 41.3 %collective-permute-start.13 = (bf16[192,1536]{1,0:T(8,128)(2,1)S(1)}, bf16[192,1536]{1,0:T(8,128)(2,1)S(1)}, u32[]{:S(2)}, u32[]{:S(2)}) collective-permute-start(bf16[192,1536]{1,0:T(8,128)(2,1)S(1)} %bitcast.280), channel_id=1, source_target_pairs={{0,1},{1,0},{2,3},{3,2},{4,5},{5,4},{6,7},{7,6},{8,9},{9,8},{10,11... | collective-permute-start | bytes 1769480 | tf_op jit(solution)/shard_map/ppermute | solution.py:84
  134.0 53.0 %collective-permute-start.14 = (bf16[192,1536]{1,0:T(8,128)(2,1)S(1)}, bf16[192,1536]{1,0:T(8,128)(2,1)S(1)}, u32[]{:S(2)}, u32[]{:S(2)}) collective-permute-start(bf16[192,1536]{1,0:T(8,128)(2,1)S(1)} %bitcast.281), channel_id=1, source_target_pairs={{0,5},{1,4},{2,7},{3,6},{4,1},{5,0},{6,3},{7,2},{8,13},{9,12},{10,... | collective-permute-start | bytes 1769480 | tf_op jit(solution)/shard_map/ppermute | solution.py:84
  135.5 51.7 %collective-permute-start.12 = (bf16[192,1536]{1,0:T(8,128)(2,1)S(1)}, bf16[192,1536]{1,0:T(8,128)(2,1)S(1)}, u32[]{:S(2)}, u32[]{:S(2)}) collective-permute-start(bf16[192,1536]{1,0:T(8,128)(2,1)S(1)} %bitcast.282), channel_id=1, source_target_pairs={{0,4},{1,5},{2,6},{3,7},{4,0},{5,1},{6,2},{7,3},{8,12},{9,13},{10,... | collective-permute-start | bytes 1769480 | tf_op jit(solution)/shard_map/ppermute | solution.py:84
  192.3 64.5 %collective-permute-start.6 = (bf16[192,1536]{1,0:T(8,128)(2,1)}, bf16[192,1536]{1,0:T(8,128)(2,1)}, u32[]{:S(2)}, u32[]{:S(2)}) collective-permute-start(bf16[192,1536]{1,0:T(8,128)(2,1)} %multiply_convert_fusion.6), channel_id=1, source_target_pairs={{0,4},{1,5},{2,6},{3,7},{4,0},{5,1},{6,2},{7,3},{8,12},{9,13},{10,... | collective-permute-start | bytes 1769480 | tf_op jit(solution)/shard_map/ppermute | solution.py:84
  250.6 33.0 %slice-start = ((s8[5505024]{0:T(1024)(128)(4,1)}), s8[1310720]{0:T(1024)(128)(4,1)S(1)}, s32[]{:S(2)}) async-start(s8[5505024]{0:T(1024)(128)(4,1)} %bitcast.271), calls=%async_computation.16 | async-start | bytes 2621440
  253.7 42.9 %copy-start.5 = (bf16[4,2,2,96,1728]{4,3,1,2,0:T(8,128)(2,1)}, bf16[4,2,2,96,1728]{4,3,1,2,0:T(8,128)(2,1)S(1)}, u32[]{:S(2)}) copy-start(bf16[4,2,2,96,1728]{4,3,1,2,0:T(8,128)(2,1)S(1)} %copy.241) | copy-start | bytes 15925252
  253.7 29.9 %slice-start.1 = ((s8[5505024]{0:T(1024)(128)(4,1)}), s8[4194304]{0:T(1024)(128)(4,1)S(1)}, s32[]{:S(2)}) async-start(s8[5505024]{0:T(1024)(128)(4,1)} %bitcast.271), calls=%async_computation.17 | async-start | bytes 8388608
  253.7 16.4 %collective-permute-start.7 = (bf16[192,1536]{1,0:T(8,128)(2,1)}, bf16[192,1536]{1,0:T(8,128)(2,1)S(1)}, u32[]{:S(2)}, u32[]{:S(2)}) collective-permute-start(bf16[192,1536]{1,0:T(8,128)(2,1)} %multiply_convert_fusion.6), channel_id=1, source_target_pairs={{0,1},{1,0},{2,3},{3,2},{4,5},{5,4},{6,7},{7,6},{8,9},{9,8},{10,11... | collective-permute-start | bytes 1769480 | tf_op jit(solution)/shard_map/ppermute | solution.py:84
  255.2 27.8 %collective-permute-start.8 = (bf16[192,1536]{1,0:T(8,128)(2,1)}, bf16[192,1536]{1,0:T(8,128)(2,1)S(1)}, u32[]{:S(2)}, u32[]{:S(2)}) collective-permute-start(bf16[192,1536]{1,0:T(8,128)(2,1)} %multiply_convert_fusion.6), channel_id=1, source_target_pairs={{0,5},{1,4},{2,7},{3,6},{4,1},{5,0},{6,3},{7,2},{8,13},{9,12},{10,... | collective-permute-start | bytes 1769480 | tf_op jit(solution)/shard_map/ppermute | solution.py:84
  283.2 7.1 %slice-start.2 = ((s8[5505024]{0:T(1024)(128)(4,1)}), s8[4194304]{0:T(1024)(128)(4,1)S(1)}, s32[]{:S(2)}) async-start(s8[5505024]{0:T(1024)(128)(4,1)} %bitcast.277), calls=%async_computation.18 | async-start | bytes 8388608
  283.6 6.7 %copy-start.11 = (bf16[2,2,192,1536]{3,2,1,0:T(8,128)(2,1)}, bf16[2,2,192,1536]{3,2,1,0:T(8,128)(2,1)S(1)}, u32[]{:S(2)}) copy-start(bf16[2,2,192,1536]{3,2,1,0:T(8,128)(2,1)S(1)} %maximum_select_fusion.1) | copy-start | bytes 7077892
  283.6 6.7 %slice-start.3 = ((s8[5505024]{0:T(1024)(128)(4,1)}), s8[1310720]{0:T(1024)(128)(4,1)S(1)}, s32[]{:S(2)}) async-start(s8[5505024]{0:T(1024)(128)(4,1)} %bitcast.277), calls=%async_computation.19 | async-start | bytes 2621440
  296.5 13.3 %copy-start.10 = (bf16[2,2,192,1536]{3,2,1,0:T(8,128)(2,1)S(1)}, bf16[2,2,192,1536]{3,2,1,0:T(8,128)(2,1)}, u32[]{:S(2)}) copy-start(bf16[2,2,192,1536]{3,2,1,0:T(8,128)(2,1)} %maximum_select_fusion.2) | copy-start | bytes 7077892
  329.0 257.9 %reduce-scatter.9.cloned.1.call-start = ((), (), s32[]{:S(2)}) async-start(), calls=%async_computation.14 | async-start | bytes 6193152 | tf_op jit(solution)/shard_map/reduce_scatter | solution.py:120
  351.8 236.3 %reduce-scatter.7.cloned.1.call-start = ((), (), s32[]{:S(2)}) async-start(), calls=%async_computation.13 | async-start | bytes 6193152 | tf_op jit(solution)/shard_map/reduce_scatter | solution.py:120
  374.3 7.6 %copy-start.48 = (bf16[768,1728]{0,1:T(8,128)(2,1)S(1)}, bf16[768,1728]{0,1:T(8,128)(2,1)}, u32[]{:S(2)}) copy-start(bf16[768,1728]{0,1:T(8,128)(2,1)} %get-tuple-element.27) | copy-start | bytes 7962628
  390.4 32.3 %all-to-all-start.2 = ((bf16[4,192,1536]{2,1,0:T(8,128)(2,1)}), bf16[4,192,1536]{2,1,0:T(8,128)(2,1)}, u32[]{:S(2)}, u32[]{:S(2)}) async-start(bf16[4,192,1536]{2,1,0:T(8,128)(2,1)} %bitcast.298), calls=%async_computation.2 | async-start | bytes 4718592 | tf_op jit(solution)/shard_map/all_to_all | solution.py:105
  422.7 33.7 %all-to-all-start.1 = ((bf16[4,192,1536]{2,1,0:T(8,128)(2,1)}), bf16[4,192,1536]{2,1,0:T(8,128)(2,1)}, u32[]{:S(2)}, u32[]{:S(2)}) async-start(bf16[4,192,1536]{2,1,0:T(8,128)(2,1)} %bitcast.297), calls=%async_computation.1 | async-start | bytes 4718592 | tf_op jit(solution)/shard_map/all_to_all | solution.py:105
  427.3 184.0 %reduce-scatter.5.cloned.1.call-start = ((), (), s32[]{:S(2)}) async-start(), calls=%async_computation.12 | async-start | bytes 5308416 | tf_op jit(solution)/shard_map/reduce_scatter | solution.py:120
  431.8 36.3 %collective-permute-start.15 = (bf16[192,1536]{1,0:T(8,128)(2,1)}, bf16[192,1536]{1,0:T(8,128)(2,1)}, u32[]{:S(2)}, u32[]{:S(2)}) collective-permute-start(bf16[192,1536]{1,0:T(8,128)(2,1)} %add_convert_fusion.1), channel_id=1, source_target_pairs={{0,4},{1,5},{2,6},{3,7},{4,0},{5,1},{6,2},{7,3},{8,12},{9,13},{10,... | collective-permute-start | bytes 1769480 | tf_op jit(solution)/shard_map/ppermute | solution.py:84
  433.7 35.9 %collective-permute-start.16 = (bf16[192,1536]{1,0:T(8,128)(2,1)}, bf16[192,1536]{1,0:T(8,128)(2,1)}, u32[]{:S(2)}, u32[]{:S(2)}) collective-permute-start(bf16[192,1536]{1,0:T(8,128)(2,1)} %add_convert_fusion.1), channel_id=1, source_target_pairs={{0,1},{1,0},{2,3},{3,2},{4,5},{5,4},{6,7},{7,6},{8,9},{9,8},{10,11... | collective-permute-start | bytes 1769480 | tf_op jit(solution)/shard_map/ppermute | solution.py:84
  435.2 45.4 %collective-permute-start.17 = (bf16[192,1536]{1,0:T(8,128)(2,1)}, bf16[192,1536]{1,0:T(8,128)(2,1)}, u32[]{:S(2)}, u32[]{:S(2)}) collective-permute-start(bf16[192,1536]{1,0:T(8,128)(2,1)} %add_convert_fusion.1), channel_id=1, source_target_pairs={{0,5},{1,4},{2,7},{3,6},{4,1},{5,0},{6,3},{7,2},{8,13},{9,12},{10,... | collective-permute-start | bytes 1769480 | tf_op jit(solution)/shard_map/ppermute | solution.py:84
  458.6 24.0 %copy-start.4 = (f32[2,2,192,1152]{3,2,1,0:T(8,128)S(1)}, f32[2,2,192,1152]{3,2,1,0:T(8,128)}, u32[]{:S(2)}) copy-start(f32[2,2,192,1152]{3,2,1,0:T(8,128)} %copy-done.3) | copy-start | bytes 10616836
  468.1 14.5 %copy-start.16 = (f32[2,2,192,384]{3,2,1,0:T(8,128)S(1)}, f32[2,2,192,384]{3,2,1,0:T(8,128)}, u32[]{:S(2)}) copy-start(f32[2,2,192,384]{3,2,1,0:T(8,128)} %get-tuple-element.26) | copy-start | bytes 3538948
  486.2 2.9 collective-permute-start.19
  487.3 1.8 collective-permute-start.18
  504.0 4.7 copy-start.27
  504.0 33.7 %all-to-all-start.3 = ((bf16[4,192,1536]{2,1,0:T(8,128)(2,1)}), bf16[4,192,1536]{2,1,0:T(8,128)(2,1)}, u32[]{:S(2)}, u32[]{:S(2)}) async-start(bf16[4,192,1536]{2,1,0:T(8,128)(2,1)} %bitcast.63), calls=%async_computation.3 | async-start | bytes 4718592 | tf_op jit(solution)/shard_map/all_to_all | solution.py:105
  508.8 31.1 %copy-start.23 = (f32[1536]{0:T(1024)S(1)}, f32[1536]{0:T(1024)}, u32[]{:S(2)}) copy-start(f32[1536]{0:T(1024)} %copy-done.22) | copy-start | bytes 18436
  508.8 31.1 %copy-start.29 = (f32[192]{0:T(256)S(1)}, f32[192]{0:T(256)}, u32[]{:S(2)}) copy-start(f32[192]{0:T(256)} %copy-done.28) | copy-start | bytes 2308
  539.8 42.3 %copy-start.7 = (f32[1,192,1536]{2,1,0:T(8,128)S(1)}, f32[1,192,1536]{2,1,0:T(8,128)}, u32[]{:S(2)}) copy-start(f32[1,192,1536]{2,1,0:T(8,128)} %get-tuple-element.24) | copy-start | bytes 3538948
  539.9 42.3 %copy-start.43 = (f32[192]{0:T(256)S(1)}, f32[192]{0:T(256)}, u32[]{:S(2)}) copy-start(f32[192]{0:T(256)} %get-tuple-element.63) | copy-start | bytes 2308
  584.5 11.3 %collective-permute-start.23 = (bf16[96,1728]{1,0:T(8,128)(2,1)S(1)}, bf16[96,1728]{1,0:T(8,128)(2,1)S(1)}, u32[]{:S(2)}, u32[]{:S(2)}) collective-permute-start(bf16[96,1728]{1,0:T(8,128)(2,1)S(1)} %get-tuple-element.46), channel_id=1, source_target_pairs={{0,4},{1,5},{2,6},{3,7},{4,0},{5,1},{6,2},{7,3},{8,12},{9,13},{10,... | collective-permute-start | bytes 995336 | tf_op jit(solution)/shard_map/ppermute | solution.py:84
  588.0 15.2 %collective-permute-start.22 = (bf16[96,1728]{1,0:T(8,128)(2,1)S(1)}, bf16[96,1728]{1,0:T(8,128)(2,1)S(1)}, u32[]{:S(2)}, u32[]{:S(2)}) collective-permute-start(bf16[96,1728]{1,0:T(8,128)(2,1)S(1)} %get-tuple-element.48), channel_id=1, source_target_pairs={{0,4},{1,5},{2,6},{3,7},{4,0},{5,1},{6,2},{7,3},{8,12},{9,13},{10,... | collective-permute-start | bytes 995336 | tf_op jit(solution)/shard_map/ppermute | solution.py:84
  589.2 19.7 %collective-permute-start.21 = (bf16[96,1728]{1,0:T(8,128)(2,1)S(1)}, bf16[96,1728]{1,0:T(8,128)(2,1)S(1)}, u32[]{:S(2)}, u32[]{:S(2)}) collective-permute-start(bf16[96,1728]{1,0:T(8,128)(2,1)S(1)} %get-tuple-element.50), channel_id=1, source_target_pairs={{0,4},{1,5},{2,6},{3,7},{4,0},{5,1},{6,2},{7,3},{8,12},{9,13},{10,... | collective-permute-start | bytes 995336 | tf_op jit(solution)/shard_map/ppermute | solution.py:84
  612.4 7.5 %collective-permute-start.20 = (bf16[96,1536]{1,0:T(8,128)(2,1)S(1)}, bf16[96,1536]{1,0:T(8,128)(2,1)S(1)}, u32[]{:S(2)}, u32[]{:S(2)}) collective-permute-start(bf16[96,1536]{1,0:T(8,128)(2,1)S(1)} %get-tuple-element.58), channel_id=1, source_target_pairs={{0,4},{1,5},{2,6},{3,7},{4,0},{5,1},{6,2},{7,3},{8,12},{9,13},{10,... | collective-permute-start | bytes 884744 | tf_op jit(solution)/shard_map/ppermute | solution.py:84
  (26 other events, 61.0 us)
Sparse Core Ops, SparseCore 0:
  20.9 53.2 all-gather.5
  75.8 57.0 all-gather.9
  135.1 56.9 all-gather.7
  193.6 56.9 all-gather.11
  329.1 60.2 reduce-scatter.10
  391.5 60.7 reduce-scatter.8
  454.6 60.7 reduce-scatter.6
  517.7 54.2 reduce-scatter.4

commit v2 on v1

--- a/solution.py
+++ b/solution.py
@@ -1,11 +1,17 @@
+import functools
+
 import jax
 import jax.numpy as jnp
 from jax import lax
+from jax.experimental import pallas as pl
+from jax.experimental.pallas import tpu as pltpu
 from jax.sharding import PartitionSpec as P
 
 SEQS = 3
 EPSILON = 1e-05
 BOTH = ("seq", "fsdp")
+MESH = pl.DeviceIdType.MESH
+PART = 256
 
 
 def times_transposed(left, right):
@@ -47,7 +53,7 @@
     ]
 
 
-def on_device(
+def plain_on_device(
     tokens,
     norm1_gain,
     in_weight,
@@ -266,9 +272,940 @@
     )
 
 
+class Place:
+    def __init__(self, planes):
+        self.planes = planes
+        self.me, self.x = lax.axis_index("seq"), lax.axis_index("fsdp")
+        self.z = lax.div(self.me, 4)
+        self.y = lax.rem(lax.div(self.me, 2), 2)
+        self.c = lax.rem(self.me, 2)
+        self.core = (self.me + 1 - 2 * self.c, self.x)
+        self.across = (self.me + 2 - 4 * self.y, self.x)
+        self.low, self.high = (self.me - 4, self.x), (self.me + 4, self.x)
+        self.has_low, self.has_high = self.z > 0, self.z < planes - 1
+        self.block = self.x * 2 + self.y
+        self.peers = [
+            (self.me, 1 - self.x),
+            self.across,
+            (self.across[0], 1 - self.x),
+        ]
+        self.peer_blocks = [
+            (1 - self.x) * 2 + self.y,
+            self.x * 2 + 1 - self.y,
+            (1 - self.x) * 2 + 1 - self.y,
+        ]
+        self.is_first, self.is_last = self.c == 0, self.c == 1
+        self.gives_next = jnp.logical_and(self.is_last, self.has_high)
+        self.gives_last = jnp.logical_and(self.is_first, self.has_low)
+        self.next, self.last = (self.me + 3, self.x), (self.me - 3, self.x)
+
+
+def remote(source, target, send, receive, device_id):
+    return pltpu.make_async_remote_copy(
+        src_ref=source,
+        dst_ref=target,
+        send_sem=send,
+        recv_sem=receive,
+        device_id=device_id,
+        device_id_type=MESH,
+    )
+
+
+def signal(semaphore, device_id):
+    pl.semaphore_signal(semaphore, inc=1, device_id=device_id, device_id_type=MESH)
+
+
+def dot(left, right):
+    return jnp.dot(left, right, preferred_element_type=jnp.float32)
+
+
+def kernel(
+    planes,
+    parts,
+    seq_len,
+    weights,
+    tokens,
+    d_out,
+    gains,
+    taps,
+    result,
+    d_tokens,
+    own_grad,
+    other_grad,
+    small,
+    d_taps,
+    kept_weights,
+    kept_mixer,
+    w,
+    core_in,
+    extra,
+    n_one,
+    n_two,
+    e_all,
+    sent_a,
+    sent_b,
+    total_a,
+    total_b,
+    got_a,
+    got_b,
+    gated,
+    d_conv,
+    mixed,
+    active,
+    d_gate_up,
+    hidden_one,
+    d_hidden,
+    halo,
+    local_sem,
+    y_send,
+    y_recv,
+    z_send,
+    z_recv,
+    c_send,
+    c_recv,
+    core_send,
+    core_recv,
+    core_free,
+    sum_send,
+    sum_recv,
+    ready,
+    last_send,
+    last_recv,
+    own_sem,
+    all_send,
+    all_recv,
+    part_send,
+    part_recv,
+    halo_send,
+    halo_recv,
+    keep_sem,
+):
+    at = Place(planes)
+    z, y, c = at.z, at.y, at.c
+    rows, width = tokens.shape
+    channels = taps.shape[1]
+    share = weights.shape[2]
+    wide = 4 * share
+    chunks = parts + 2
+    step_cols = weights.shape[3] // 3
+
+    def y_copies(k):
+        return (
+            pltpu.make_async_copy(weights.at[k, y], w.at[k, z, y, c], local_sem.at[k]),
+            remote(weights.at[k, 1 - y], w.at[k, z, y, c], y_send.at[k], y_recv.at[k], at.across),
+        )
+
+    def piece(k, p):
+        return w.at[k, p, :, c]
+
+    def to_side(k, p, side):
+        return remote(
+            piece(k, p),
+            piece(k, p),
+            z_send.at[k, side, p],
+            z_recv.at[k, p],
+            at.high if side else at.low,
+        )
+
+    def to_core(k, p):
+        return remote(piece(k, p), piece(k, p), c_send.at[k, p], c_recv.at[k, p], at.core)
+
+    def begin(k):
+        for copy in y_copies(k):
+            copy.start()
+
+    def own(k):
+        y_copies(k)[0].wait()
+        remote(
+            weights.at[k, y], w.at[k, z, 1 - y, c], y_send.at[k], y_recv.at[k], at.across
+        ).wait_recv()
+        pl.when(at.has_low)(lambda: to_side(k, z, 0).start())
+        pl.when(at.has_high)(lambda: to_side(k, z, 1).start())
+        to_core(k, z).start()
+
+    def relay(k, t):
+        below, above = z - t, z + t
+
+        @pl.when(below >= 0)
+        def _():
+            to_side(k, below, 1).wait_recv()
+            pl.when(at.has_high)(lambda: to_side(k, below, 1).start())
+            to_core(k, below).start()
+
+        @pl.when(above < planes)
+        def _():
+            to_side(k, above, 0).wait_recv()
+            pl.when(at.has_low)(lambda: to_side(k, above, 0).start())
+            to_core(k, above).start()
+
+    def relays(k):
+        for t in range(1, planes):
+            relay(k, t)
+
+    def core_wait(k):
+        for p in range(planes):
+            remote(
+                w.at[k, p, :, 1 - c], w.at[k, p, :, 1 - c], c_send.at[k, p], c_recv.at[k, p], at.core
+            ).wait_recv()
+
+    def gather_done(k):
+        y_copies(k)[1].wait_send()
+        for p in range(planes):
+            pl.when(jnp.logical_and(at.has_low, p >= z))(lambda: to_side(k, p, 0).wait_send())
+            pl.when(jnp.logical_and(at.has_high, p <= z))(lambda: to_side(k, p, 1).wait_send())
+            to_core(k, p).wait_send()
+
+    def chunk_of(v):
+        return lax.rem(v + 2, chunks)
+
+    def core_copy(v):
+        k = chunk_of(v)
+        return remote(
+            w.at[k, :, :, 1 - c],
+            core_in.at[lax.rem(v, 2)],
+            core_send.at[k],
+            core_recv.at[k],
+            at.core,
+        )
+
+    def core_start(v):
+        pl.when(v >= 2)(lambda: pl.semaphore_wait(core_free, 1))
+        core_copy(v).start()
+
+    def core_add(v):
+        k, slot = chunk_of(v), lax.rem(v, 2)
+        core_copy(v).wait()
+
+        def add(p, carry):
+            total = w[k, p, :, c].astype(jnp.float32) + core_in[slot, p].astype(jnp.float32)
+            w[k, p, :, c] = total.astype(jnp.bfloat16)
+            return carry
+
+        lax.fori_loop(0, planes, add, 0)
+        pl.when(v < chunks - 2)(lambda: signal(core_free, at.core))
+        pl.when(at.has_low)(lambda: signal(ready.at[1], at.low))
+        pl.when(at.has_high)(lambda: signal(ready.at[0], at.high))
+
+    def landing(k, d):
+        return w.at[k, d, :, 1 - c]
+
+    def sum_up(k, d):
+        return remote(
+            landing(k, d), landing(k, d), sum_send.at[k, 1, d], sum_recv.at[k, 1, d], at.high
+        )
+
+    def sum_down(k, d):
+        return remote(
+            landing(k, d), landing(k, d), sum_send.at[k, 0, d], sum_recv.at[k, 0, d], at.low
+        )
+
+    def sum_down_last(k, d):
+        return remote(
+            landing(k, d), extra.at[k], sum_send.at[k, 0, d], sum_recv.at[k, 0, d], at.low
+        )
+
+    def add_here(k, d, arrived):
+        here = w[k, d, :, c].astype(jnp.float32)
+
+        @pl.when(arrived)
+        def _():
+            w[k, d, :, 1 - c] = (w[k, d, :, 1 - c].astype(jnp.float32) + here).astype(jnp.bfloat16)
+
+        @pl.when(jnp.logical_not(arrived))
+        def _():
+            w[k, d, :, 1 - c] = w[k, d, :, c]
+
+    def add_up(v):
+        k = chunk_of(v)
+        pl.when(at.has_high)(lambda: pl.semaphore_wait(ready.at[1], 1))
+        for d in range(planes - 1, -1, -1):
+
+            @pl.when(d > z)
+            def _():
+                pl.when(at.has_low)(lambda: sum_up(k, d).wait_recv())
+                add_here(k, d, at.has_low)
+                sum_up(k, d).start()
+
+            @pl.when(jnp.logical_and(z == d, at.has_low))
+            def _():
+                sum_up(k, d).wait_recv()
+                total = w[k, d, :, c].astype(jnp.float32) + w[k, d, :, 1 - c].astype(jnp.float32)
+                w[k, d, :, c] = total.astype(jnp.bfloat16)
+
+    def add_down(v):
+        k = chunk_of(v)
+        pl.when(at.has_low)(lambda: pl.semaphore_wait(ready.at[0], 1))
+        for d in range(planes):
+
+            @pl.when(d < z)
+            def _():
+                pl.when(at.has_high)(lambda: sum_down(k, d).wait_recv())
+                add_here(k, d, at.has_high)
+                pl.when(z - 1 > d)(lambda: sum_down(k, d).start())
+                pl.when(z - 1 == d)(lambda: sum_down_last(k, d).start())
+
+            @pl.when(jnp.logical_and(z == d, at.has_high))
+            def _():
+                sum_down_last(k, d).wait_recv()
+                total = w[k, d, :, c].astype(jnp.float32) + extra[k].astype(jnp.float32)
+                w[k, d, :, c] = total.astype(jnp.bfloat16)
+
+    def give_copies(k):
+        return (
+            pltpu.make_async_copy(w.at[k, z, y, c], own_grad.at[k], own_sem.at[k]),
+            remote(
+                w.at[k, z, 1 - y, c], other_grad.at[k], last_send.at[k], last_recv.at[k], at.across
+            ),
+        )
+
+    def give(v):
+        for copy in give_copies(chunk_of(v)):
+            copy.start()
+
+    def sum_done(v):
+        k = chunk_of(v)
+        for d in range(planes):
+            pl.when(d > z)(lambda: sum_up(k, d).wait_send())
+            pl.when(d < z)(lambda: sum_down(k, d).wait_send())
+        for copy in give_copies(k):
+            copy.wait()
+
+    pause = planes - 1
+
+    def stage(o, do):
+        early = jnp.logical_and(o >= 0, o < parts)
+        late = jnp.logical_and(o >= parts + pause, o < parts + pause + 2)
+        pl.when(jnp.logical_or(early, late))(lambda: do(jnp.where(late, o - pause, o)))
+
+    def tick(i):
+        far = jnp.maximum(z, planes - 1 - z)
+        stage(i - 1, core_add)
+        stage(i - 1 - z, add_up)
+        stage(i - 1 - (planes - 1 - z), add_down)
+        stage(i - 1 - far, give)
+
+    def all_copies(buffer, which):
+        return [
+            remote(
+                buffer.at[at.block],
+                buffer.at[at.block],
+                all_send.at[which, i],
+                all_recv.at[which, i],
+                peer,
+            )
+            for i, peer in enumerate(at.peers)
+        ]
+
+    def all_start(buffer, which):
+        for copy in all_copies(buffer, which):
+            copy.start()
+
+    def all_wait(buffer, which):
+        for i, peer in enumerate(at.peers):
+            landed = buffer.at[at.peer_blocks[i]]
+            remote(
+                landed, landed, all_send.at[which, i], all_recv.at[which, i], peer
+            ).wait_recv()
+
+    def all_done(buffer, which):
+        for copy in all_copies(buffer, which):
+            copy.wait_send()
+
+    def part_copies(source, target, which):
+        return [
+            remote(
+                source.at[at.peer_blocks[i]],
+                target.at[i],
+                part_send.at[which, i],
+                part_recv.at[which, i],
+                peer,
+            )
+            for i, peer in enumerate(at.peers)
+        ]
+
+    def part_start(source, target, which):
+        for copy in part_copies(source, target, which):
+            copy.start()
+
+    def part_wait(source, target, which):
+        for copy in part_copies(source, target, which):
+            copy.wait_recv()
+
+    def part_done(source, target, which):
+        for copy in part_copies(source, target, which):
+            copy.wait_send()
+
+    tile = 48
+
+    def by_rows(body):
+        def run(i, carry):
+            body(pl.ds(pl.multiple_of(i * tile, tile), tile))
+            return carry
+
+        lax.fori_loop(0, rows // tile, run, 0)
+
+    def scale_of(hidden):
+        return lax.rsqrt(jnp.mean(hidden * hidden, axis=-1, keepdims=True) + EPSILON)
+
+    def summed(source, target, span):
+        total = source[at.block, span, :].astype(jnp.float32)
+        for i in range(3):
+            total = total + target[i, span, :].astype(jnp.float32)
+        return total
+
+    def back_through_norm(grad, hidden, gain, row):
+        scale = scale_of(hidden)
+        weighted = grad * gain
+        inner = jnp.sum(weighted * hidden, axis=-1, keepdims=True)
+        small[row : row + 1, :] += jnp.sum(grad * hidden * scale, axis=0, keepdims=True)
+        return scale * weighted - hidden * (scale * scale * scale) * inner / width
+
+    def transposed(buffer, k):
+        def one(p, carry):
+            cols = pl.ds(pl.multiple_of(p * wide, wide), wide)
+            block = buffer[:, :, cols].reshape(4 * rows, wide).T
+            w[k, p] = block.reshape(2, 2, share, 4 * rows)
+            return carry
+
+        lax.fori_loop(0, planes, one, 0)
+
+    def whole(k, low, high):
+        return w[k, :, :, :, :, low:high].reshape(planes * wide, high - low)
+
+    def plane_rows(k, p, low, high):
+        return w[k, p, :, :, :, low:high].reshape(wide, high - low)
+
+    def pair(t):
+        return pl.ds(2 * t, 2)
+
+    def columns(p):
+        return pl.ds(pl.multiple_of(p * wide, wide), wide)
+
+    halo[...] = jnp.zeros_like(halo)
+    barrier = pltpu.get_barrier_semaphore()
+    for device_id in [at.core] + at.peers:
+        signal(barrier, device_id)
+    pl.when(at.has_low)(lambda: signal(barrier, at.low))
+    pl.when(at.has_high)(lambda: signal(barrier, at.high))
+    pl.when(at.gives_next)(lambda: signal(barrier, at.next))
+    pl.when(at.gives_last)(lambda: signal(barrier, at.last))
+    count = 4
+    for flag in (at.has_low, at.has_high, at.gives_next, at.gives_last):
+        count = count + jnp.where(flag, 1, 0)
+    pl.semaphore_wait(barrier, count)
+
+    begin(0)
+    begin(1)
+    e_copy = pltpu.make_async_copy(d_out, e_all.at[at.block], keep_sem.at[0])
+    e_copy.start()
+    small[...] = jnp.zeros_like(small)
+    d_taps[...] = jnp.zeros_like(d_taps)
+
+    def first_norm(span):
+        hidden = tokens[span, :].astype(jnp.float32)
+        n_one[at.block, span, :] = (hidden * scale_of(hidden) * gains[0:1, :]).astype(jnp.bfloat16)
+
+    by_rows(first_norm)
+    all_start(n_one, 0)
+    own(0)
+    own(1)
+    for k in range(2, chunks):
+        begin(k)
+    relay(0, 1)
+    relay(1, 1)
+    own(2)
+    for t in range(2, planes):
+        relay(0, t)
+        relay(1, t)
+    own(3)
+    own(4)
+    e_copy.wait()
+    all_start(e_all, 1)
+    core_wait(0)
+    core_wait(1)
+    all_wait(n_one, 0)
+
+    def project(t, carry):
+        normed = n_one[pair(t)].reshape(2 * rows, width)
+        b_c = dot(normed, whole(0, 0, 2 * channels))
+        x_part = dot(normed, whole(1, 0, channels))
+        total_a[pair(t), :, 0 : 2 * channels] = b_c.reshape(2, rows, 2 * channels)
+        total_a[pair(t), :, 2 * channels : 3 * channels] = x_part.reshape(2, rows, channels)
+        product = (b_c[:, :channels] * x_part).astype(jnp.bfloat16).astype(jnp.float32)
+        gated[pair(t), 8 : 8 + rows, :] = product.reshape(2, rows, channels)
+        return carry
+
+    lax.fori_loop(0, 2, project, 0)
+
+    def halo_core(which, edge):
+        return remote(
+            edge, halo.at[2 * which], halo_send.at[2 * which], halo_recv.at[2 * which], at.core
+        )
+
+    def halo_plane(which, edge, target):
+        return remote(
+            edge,
+            halo.at[2 * which + 1],
+            halo_send.at[2 * which + 1],
+            halo_recv.at[2 * which + 1],
+            target,
+        )
+
+    tail = gated.at[:, pl.ds(rows, 8), :]
+    halo_core(0, tail).start()
+    pl.when(at.gives_next)(lambda: halo_plane(0, tail, at.next).start())
+    halo_core(0, tail).wait_recv()
+    pl.when(at.gives_last)(lambda: halo_plane(0, tail, at.last).wait_recv())
+    for group in range(2):
+
+        @pl.when(at.is_last)
+        def _():
+            gated[2 * group, 0:8, :] = halo[0, 2 * group]
+            gated[2 * group + 1, 0:8, :] = halo[0, 2 * group + 1]
+
+        @pl.when(at.is_first)
+        def _():
+            gated[2 * group, 0:8, :] = halo[1, 2 * group + 1]
+            gated[2 * group + 1, 0:8, :] = halo[0, 2 * group]
+
+    def start_of(block):
+        return lax.rem((z * 4 + lax.rem(block, 2) * 2 + c) * rows, seq_len)
+
+    def place_in(block, ahead):
+        place = start_of(block) + ahead + lax.broadcasted_iota(jnp.int32, (rows, channels), 0)
+        return jnp.where(place >= seq_len, place - seq_len, place)
+
+    def convolve(b, carry):
+        place = place_in(b, 0)
+        conv = jnp.zeros((rows, channels), jnp.float32)
+        for j in range(3):
+            moved = gated[b, 6 + j : 6 + j + rows, :]
+            conv = conv + jnp.where(place >= 2 - j, moved, 0.0) * taps[j : j + 1, :]
+        total_a[b, :, 3 * channels : 4 * channels] = conv
+        mixed[b] = (total_a[b, :, channels : 2 * channels] * conv).astype(jnp.bfloat16)
+        return carry
+
+    lax.fori_loop(0, 4, convolve, 0)
+
+    def branch(i, carry):
+        t, p = lax.div(i, planes), lax.rem(i, planes)
+        left = mixed[pair(t)].reshape(2 * rows, channels)
+        out = times_transposed(left, plane_rows(1, p, channels, 2 * channels))
+        sent_a[pair(t), :, columns(p)] = out.reshape(2, rows, wide).astype(jnp.bfloat16)
+        return carry
+
+    lax.fori_loop(0, 2 * planes, branch, 0)
+    part_start(sent_a, got_a, 0)
+    gather_done(0)
+    gather_done(1)
+    keep_weights = pltpu.make_async_copy(w.at[pl.ds(0, 2)], kept_weights, keep_sem.at[1])
+    keep_mixer = pltpu.make_async_copy(total_a, kept_mixer, keep_sem.at[2])
+    keep_weights.start()
+    keep_mixer.start()
+    relays(2)
+    keep_weights.wait()
+    keep_mixer.wait()
+    total_a[...] = jnp.zeros_like(total_a)
+    total_b[...] = jnp.zeros_like(total_b)
+    all_wait(e_all, 1)
+    transposed(e_all, 1)
+    part_wait(sent_a, got_a, 0)
+
+    def second_norm(span):
+        hidden = tokens[span, :].astype(jnp.float32) + summed(sent_a, got_a, span)
+        hidden_one[span, :] = hidden
+        n_two[at.block, span, :] = (hidden * scale_of(hidden) * gains[1:2, :]).astype(jnp.bfloat16)
+
+    by_rows(second_norm)
+    all_start(n_two, 2)
+    part_done(sent_a, got_a, 0)
+    own(5)
+    relays(3)
+    own(6)
+    relays(4)
+    all_wait(n_two, 2)
+    transposed(n_two, 0)
+
+    def feed_forward(k):
+        def half(t, carry):
+            normed = n_two[pair(t)].reshape(2 * rows, width)
+            both = dot(normed, whole(k, 0, 2 * step_cols))
+            d_active = dot(
+                e_all[pair(t)].reshape(2 * rows, width), whole(k, 2 * step_cols, 3 * step_cols)
+            )
+            gate, upper = both[:, :step_cols], both[:, step_cols:]
+            sigma = jax.nn.sigmoid(gate)
+            soft = gate * sigma
+            here = pl.ds(pl.multiple_of(t * 2 * rows, 2 * rows), 2 * rows)
+            active[here, :] = (soft * upper).astype(jnp.bfloat16)
+            d_gate_up[here, step_cols:] = (d_active * soft).astype(jnp.bfloat16)
+            d_gate_up[here, :step_cols] = (
+                d_active * upper * sigma * (1.0 + gate * (1.0 - sigma))
+            ).astype(jnp.bfloat16)
+
+            def spread(p, inner):
+                back = times_transposed(d_gate_up[here, :], plane_rows(k, p, 0, 2 * step_cols))
+                total_b[pair(t), :, columns(p)] += back.reshape(2, rows, wide)
+                out = times_transposed(
+                    active[here, :], plane_rows(k, p, 2 * step_cols, 3 * step_cols)
+                )
+                total_a[pair(t), :, columns(p)] += out.reshape(2, rows, wide)
+                return inner
+
+            lax.fori_loop(0, planes, spread, 0)
+            return carry
+
+        lax.fori_loop(0, 2, half, 0)
+        gather_done(k)
+
+        def grads(p, carry):
+            low = dot(w[0, p].reshape(wide, 4 * rows), d_gate_up[...])
+            w[k, p, :, :, :, 0 : 2 * step_cols] = low.astype(jnp.bfloat16).reshape(
+                2, 2, share, 2 * step_cols
+            )
+            high = dot(w[1, p].reshape(wide, 4 * rows), active[...])
+            w[k, p, :, :, :, 2 * step_cols : 3 * step_cols] = high.astype(jnp.bfloat16).reshape(
+                2, 2, share, step_cols
+            )
+            return carry
+
+        lax.fori_loop(0, planes, grads, 0)
+
+    def one_part(i, carry):
+        k = i + 2
+        pl.when(k + 5 < chunks)(lambda: own(k + 5))
+        tick(i)
+        core_wait(k)
+        feed_forward(k)
+        core_start(i)
+        pl.when(k + 3 < chunks)(lambda: relays(k + 3))
+        return carry
+
+    lax.fori_loop(0, parts, one_part, 0)
+
+    restore_weights = pltpu.make_async_copy(kept_weights, w.at[pl.ds(0, 2)], keep_sem.at[1])
+    restore_weights.start()
+    sum_done(0)
+    sum_done(1)
+    transposed(n_one, 2)
+
+    def cast(source, target):
+        def run(b, carry):
+            target[b] = source[b].astype(jnp.bfloat16)
+            return carry
+
+        lax.fori_loop(0, 4, run, 0)
+
+    cast(total_b, sent_a)
+    part_start(sent_a, got_a, 2)
+    cast(total_a, sent_b)
+    part_start(sent_b, got_b, 1)
+    restore_mixer = pltpu.make_async_copy(kept_mixer, total_a, keep_sem.at[2])
+    restore_mixer.start()
+    tick(parts)
+    part_wait(sent_a, got_a, 2)
+    all_done(n_one, 0)
+
+    def through_second(span):
+        grad = back_through_norm(
+            summed(sent_a, got_a, span), hidden_one[span, :], gains[1:2, :], 1
+        )
+        grad = e_all[at.block, span, :].astype(jnp.float32) + grad
+        d_hidden[span, :] = grad
+        n_one[at.block, span, :] = grad.astype(jnp.bfloat16)
+
+    by_rows(through_second)
+    all_start(n_one, 3)
+    part_done(sent_a, got_a, 2)
+    tick(parts + 1)
+    part_wait(sent_b, got_b, 1)
+
+    def last_out(span):
+        result[span, :] = (hidden_one[span, :] + summed(sent_b, got_b, span)).astype(jnp.bfloat16)
+
+    by_rows(last_out)
+    part_done(sent_b, got_b, 1)
+    restore_weights.wait()
+    restore_mixer.wait()
+    all_wait(n_one, 3)
+
+    def into_mixer(t, carry):
+        grad = n_one[pair(t)].reshape(2 * rows, width)
+        d_mixed = dot(grad, whole(1, channels, 2 * channels)).reshape(2, rows, channels)
+        conv = total_a[pair(t), :, 3 * channels : 4 * channels]
+        c_part = total_a[pair(t), :, channels : 2 * channels]
+        sent_b[pair(t), :, channels : 2 * channels] = (d_mixed * conv).astype(jnp.bfloat16)
+        d_conv[pair(t), 0:rows, :] = d_mixed * c_part
+        return carry
+
+    lax.fori_loop(0, 2, into_mixer, 0)
+    head = d_conv.at[:, pl.ds(0, 8), :]
+    halo_core(1, head).start()
+    pl.when(at.gives_last)(lambda: halo_plane(1, head, at.last).start())
+    transposed(n_one, 3)
+
+    def d_out_weight(p, carry):
+        grad = dot(w[3, p].reshape(wide, 4 * rows), mixed[...].reshape(4 * rows, channels))
+        w[1, p, :, :, :, channels : 2 * channels] = grad.astype(jnp.bfloat16).reshape(
+            2, 2, share, channels
+        )
+        return carry
+
+    lax.fori_loop(0, planes, d_out_weight, 0)
+    halo_core(1, head).wait_recv()
+    pl.when(at.gives_next)(lambda: halo_plane(1, head, at.next).wait_recv())
+    for group in range(2):
+
+        @pl.when(at.is_first)
+        def _():
+            d_conv[2 * group, rows : rows + 8, :] = halo[2, 2 * group]
+            d_conv[2 * group + 1, rows : rows + 8, :] = halo[2, 2 * group + 1]
+
+        @pl.when(at.is_last)
+        def _():
+            d_conv[2 * group, rows : rows + 8, :] = halo[2, 2 * group + 1]
+            d_conv[2 * group + 1, rows : rows + 8, :] = halo[3, 2 * group]
+
+    def convolve_back(b, carry):
+        place = place_in(b, 0)
+        d_gated = jnp.zeros((rows, channels), jnp.float32)
+        for j in range(3):
+            ahead = 2 - j
+            moved = jnp.where(
+                place_in(b, ahead) >= ahead, d_conv[b, ahead : ahead + rows, :], 0.0
+            )
+            d_gated = d_gated + moved * taps[j : j + 1, :]
+            product = d_conv[b, 0:rows, :] * gated[b, 6 + j : 6 + j + rows, :]
+            d_taps[j : j + 1, :] += jnp.sum(
+                jnp.where(place >= ahead, product, 0.0), axis=0, keepdims=True
+            )
+        x_part = total_a[b, :, 2 * channels : 3 * channels]
+        sent_b[b, :, 0:channels] = (d_gated * x_part).astype(jnp.bfloat16)
+        b_part = total_a[b, :, 0:channels]
+        sent_b[b, :, 2 * channels : 3 * channels] = (d_gated * b_part).astype(jnp.bfloat16)
+        return carry
+
+    lax.fori_loop(0, 4, convolve_back, 0)
+
+    def d_normed(i, carry):
+        t, p = lax.div(i, planes), lax.rem(i, planes)
+        grad = sent_b[pair(t), :, 0 : 2 * channels].reshape(2 * rows, 2 * channels)
+        out = times_transposed(grad, plane_rows(0, p, 0, 2 * channels))
+        grad = sent_b[pair(t), :, 2 * channels : 3 * channels].reshape(2 * rows, channels)
+        out = out + times_transposed(grad, plane_rows(1, p, 0, channels))
+        sent_a[pair(t), :, columns(p)] = out.reshape(2, rows, wide).astype(jnp.bfloat16)
+        return carry
+
+    lax.fori_loop(0, 2 * planes, d_normed, 0)
+    part_start(sent_a, got_a, 3)
+
+    def d_in_weight(p, carry):
+        normed = w[2, p].reshape(wide, 4 * rows)
+        grad = dot(normed, sent_b[:, :, 0 : 2 * channels].reshape(4 * rows, 2 * channels))
+        w[0, p] = grad.astype(jnp.bfloat16).reshape(2, 2, share, 2 * channels)
+        grad = dot(normed, sent_b[:, :, 2 * channels : 3 * channels].reshape(4 * rows, channels))
+        w[1, p, :, :, :, 0:channels] = grad.astype(jnp.bfloat16).reshape(2, 2, share, channels)
+        return carry
+
+    lax.fori_loop(0, planes, d_in_weight, 0)
+    core_start(jnp.int32(parts))
+    core_start(jnp.int32(parts + 1))
+    for i in range(parts + 2, parts + pause + 2):
+        tick(i)
+    part_wait(sent_a, got_a, 3)
+
+    def through_first(span):
+        hidden = tokens[span, :].astype(jnp.float32)
+        grad = back_through_norm(summed(sent_a, got_a, span), hidden, gains[0:1, :], 0)
+        d_tokens[span, :] = (d_hidden[span, :] + grad).astype(jnp.bfloat16)
+
+    by_rows(through_first)
+    for i in range(parts + pause + 2, parts + pause + planes + 2):
+        tick(i)
+
+    part_done(sent_a, got_a, 3)
+    all_done(e_all, 1)
+    all_done(n_two, 2)
+    all_done(n_one, 3)
+    halo_core(0, tail).wait_send()
+    halo_core(1, head).wait_send()
+    pl.when(at.gives_next)(lambda: halo_plane(0, tail, at.next).wait_send())
+    pl.when(at.gives_last)(lambda: halo_plane(1, head, at.last).wait_send())
+    for v in range(2, chunks):
+        sum_done(v)
+
+
+def one_kernel(planes, seq_len, weights, tokens, d_out, gains, taps):
+    chunks, _, share, cols = weights.shape
+    parts = chunks - 2
+    rows, width = tokens.shape
+    channels = taps.shape[1]
+    low, full = jnp.bfloat16, jnp.float32
+    shape = jax.ShapeDtypeStruct
+    vmem, anywhere = pl.BlockSpec(memory_space=pltpu.VMEM), pl.BlockSpec(memory_space=pl.ANY)
+    dma = pltpu.SemaphoreType.DMA
+    block = (4, rows, width)
+    return pl.pallas_call(
+        functools.partial(kernel, planes, parts, seq_len),
+        out_shape=(
+            shape((rows, width), low),
+            shape((rows, width), low),
+            shape((chunks, share, cols), low),
+            shape((chunks, share, cols), low),
+            shape((8, width), full),
+            shape((8, channels), full),
+            shape((2, planes, 2, 2, share, cols), low),
+            shape(block, full),
+        ),
+        in_specs=[anywhere, vmem, anywhere, vmem, vmem],
+        out_specs=[vmem, vmem, anywhere, anywhere, vmem, vmem, anywhere, anywhere],
+        scratch_shapes=[
+            pltpu.VMEM((chunks, planes, 2, 2, share, cols), low),
+            pltpu.VMEM((2, planes, 2, share, cols), low),
+            pltpu.VMEM((chunks, 2, share, cols), low),
+            pltpu.VMEM(block, low),
+            pltpu.VMEM(block, low),
+            pltpu.VMEM(block, low),
+            pltpu.VMEM(block, low),
+            pltpu.VMEM(block, low),
+            pltpu.VMEM(block, full),
+            pltpu.VMEM(block, full),
+            pltpu.VMEM((3, rows, width), low),
+            pltpu.VMEM((3, rows, width), low),
+            pltpu.VMEM((4, rows + 8, channels), full),
+            pltpu.VMEM((4, rows + 8, channels), full),
+            pltpu.VMEM((4, rows, channels), low),
+            pltpu.VMEM((4 * rows, PART), low),
+            pltpu.VMEM((4 * rows, 2 * PART), low),
+            pltpu.VMEM((rows, width), full),
+            pltpu.VMEM((rows, width), full),
+            pltpu.VMEM((4, 4, 8, channels), full),
+            dma((chunks,)),
+            dma((chunks,)),
+            dma((chunks,)),
+            dma((chunks, 2, planes)),
+            dma((chunks, planes)),
+            dma((chunks, planes)),
+            dma((chunks, planes)),
+            dma((chunks,)),
+            dma((chunks,)),
+            pltpu.SemaphoreType.REGULAR,
+            dma((chunks, 2, planes)),
+            dma((chunks, 2, planes)),
+            pltpu.SemaphoreType.REGULAR((2,)),
+            dma((chunks,)),
+            dma((chunks,)),
+            dma((chunks,)),
+            dma((4, 3)),
+            dma((4, 3)),
+            dma((4, 3)),
+            dma((4, 3)),
+            dma((4,)),
+            dma((4,)),
+            dma((3,)),
+        ],
+        compiler_params=pltpu.CompilerParams(
+            collective_id=0, has_side_effects=True, vmem_limit_bytes=64 * 1024 * 1024
+        ),
+    )(weights, tokens, d_out, gains, taps)
+
+
+def on_device(
+    tokens,
+    norm1_gain,
+    in_weight,
+    conv_kernel,
+    out_weight,
+    norm2_gain,
+    gate_weight,
+    up_weight,
+    down_weight,
+    d_out,
+):
+    planes = lax.axis_size("seq") // 4
+    here = lax.axis_index("seq")
+    y, x = (here // 2) % 2, lax.axis_index("fsdp")
+    rows, width = tokens.shape[1:]
+    share = gate_weight.shape[0]
+    channels = in_weight.shape[2] // 2
+    hidden = gate_weight.shape[1] // 2
+    parts = -(-hidden // PART)
+
+    gains = lax.all_gather(
+        jnp.concatenate([norm1_gain[:, None], norm2_gain[:, None], conv_kernel], axis=1),
+        "seq",
+        axis=0,
+        tiled=True,
+    ).astype(jnp.float32)
+    gains = jnp.pad(gains.T, ((0, 3), (0, 0)))
+    first_channel = x * (2 * channels) + y * channels
+    taps = lax.dynamic_slice_in_dim(gains, first_channel, channels, 1)[2:]
+    taps = jnp.pad(taps, ((0, 2), (0, 0)))
+
+    mixer = jnp.concatenate(
+        [in_weight.reshape(share, 3, 2, channels), out_weight.reshape(share, 1, 2, channels)],
+        axis=1,
+    )
+    mixer = mixer.reshape(share, 2, 2, 2, channels).transpose(1, 3, 0, 2, 4)
+    mixer = mixer.reshape(2, 2, share, 2 * channels)
+
+    def in_parts(weight):
+        halves = jnp.pad(
+            weight.reshape(share, 2, hidden), ((0, 0), (0, 0), (0, parts * PART - hidden))
+        )
+        return halves.reshape(share, 2, parts, PART).transpose(2, 1, 0, 3)
+
+    ffn = jnp.concatenate(
+        [in_parts(gate_weight), in_parts(up_weight), in_parts(down_weight)], axis=3
+    )
+    weights = jnp.concatenate([mixer, ffn], axis=0)
+    result, d_tokens, own_grad, other_grad, small, d_taps, _, _ = one_kernel(
+        planes,
+        lax.axis_size("seq") * rows // SEQS,
+        weights,
+        tokens[0],
+        d_out[0],
+        gains,
+        taps,
+    )
+    both = jnp.where(
+        y == 0, jnp.stack([own_grad, other_grad]), jnp.stack([other_grad, own_grad])
+    )
+    d_mixer = both[:, :2].reshape(2, 2, share, 2, channels).transpose(2, 1, 3, 0, 4)
+    d_mixer = d_mixer.reshape(share, 4, 2 * channels).astype(jnp.float32)
+
+    def whole_grad(which):
+        grad = both[:, 2:, :, which * PART : (which + 1) * PART].transpose(2, 0, 1, 3)
+        grad = grad.reshape(share, 2, parts * PART)[:, :, :hidden]
+        return grad.reshape(share, 2 * hidden).astype(jnp.float32)
+
+    taps_count = conv_kernel.shape[1]
+    d_kernel = lax.dynamic_update_slice(
+        jnp.zeros((taps_count, width), jnp.float32), d_taps[:taps_count], (0, first_channel)
+    )
+    sums = lax.psum(jnp.concatenate([small[:2], d_kernel], axis=0), BOTH)
+    sums = lax.dynamic_slice_in_dim(sums, here * share, share, 1)
+    return (
+        result[None],
+        d_tokens[None],
+        sums[0],
+        d_mixer[:, :3],
+        sums[2:].T,
+        d_mixer[:, 3],
+        sums[1],
+        whole_grad(0),
+        whole_grad(1),
+        whole_grad(2),
+    )
+
+
+def fits(mesh):
+    return mesh.shape["seq"] <= 16
+
+
 def solution(mesh):
     return jax.shard_map(
-        on_device,
+        on_device if fits(mesh) else plain_on_device,
         mesh=mesh,
         in_specs=(
             P("fsdp", "seq", None),

time: 640 us -> 566 us (0.88)
  Pallas kernels: 0 us -> 453 us
  waiting for transfers between devices: 282 us -> 0 us
  matrix products: 96.6 us -> 0 us
  starting transfers between devices: 48.8 us -> 0 us
  other arithmetic: 50.8 us -> 7.62 us
  local copies, waits for them, and re-layouts: 74.9 us -> 35 us
  between operations: 15.9 us -> 1.15 us
    pallas_call x0 -> x1, Pallas kernels: none -> 453 us  [one_kernel(): pl.pallas_call(functools.partial(kernel, planes, parts, seq_len), out_sha...]
    ppermute x24 -> x0, waiting for transfers between devices: 169 us -> none  [moved(): return lax.ppermute(value, BOTH, pairs)]
    dot_general x15 -> x0, matrix products: 96.6 us -> none  [the longest x5 36.5 us: times_transposed(): lax.dot_general(left, right, (((1,), (1,)), ((), ())), preferred_element_...]
    all_to_all x4 -> x0, waiting for transfers between devices: 68 us -> none  [plane_sum(): lax.all_to_all(sent, BOTH, 0, 0, axis_index_groups=plane_groups, tiled=True)]
    all_gather x4 -> x0, waiting for transfers between devices: 44.7 us -> none  [fetch(): lax.all_gather(pair, 'seq', axis=0, tiled=False, axis_index_groups=column...]
    ppermute x24 -> x0, starting transfers between devices: 29.8 us -> none  [moved(): return lax.ppermute(value, BOTH, pairs)]
    select_n x23 -> x1, other arithmetic: 22.2 us -> 3 us  [on_device(): jnp.where(y == 0, jnp.stack([own_grad, other_grad]), jnp.stack([other_gra...]
    transpose x5 -> x2, local copies, waits for them, and re-layouts: 19.9 us -> 0.76 us  [the longest x1 0.58 us: on_device(): sums[2:]]
  transfers between devices with their start and end apart: 36 -> 0, of which waited for: 22 -> 0; matrix products, arithmetic and copies ran while one was open for 26% -> 0% of each run, Pallas kernels for 0% -> 0%
where the time goes in v2:
time: 566 us; the launch traced here: 559 us
  Pallas kernels  453 us (80%)
  blocking collectives  61.6 us (11%)
  local copies, waits for them, and re-layouts  35 us (6%)
  other arithmetic  7.62 us (1%)
    pallas_call x1, Pallas kernels, one_kernel(): pl.pallas_call(functools.partial(kernel, planes, parts, seq_len), out_sha...  453 us
    psum x1, blocking collectives, on_device(): sums = lax.psum(jnp.concatenate([small[:2], d_kernel], axis=0), BOTH)  38.4 us
    all_gather x1, blocking collectives, on_device(): lax.all_gather(jnp.concatenate([norm1_gain[:, None], norm2_gain[:, None],...  23.2 us
    convert_element_type x6, local copies, waits for them, and re-layouts, whole_grad(): return grad.reshape(share, 2 * hidden).astype(jnp.float32)  16.1 us

profile of v2, /device:TPU:0, one launch (start us, length us, event | category | flops | bytes accessed | tf_op | source)
XLA Modules:
  0.0 558.7 jit_solution(26435892612192130)
XLA Ops:
  0.6 0.0 copy-start
  0.7 0.8 maximum_bitcast_fusion
  1.5 23.2 %all-gather = bf16[16,96,5]{1,2,0:T(8,128)(2,1)S(1)} all-gather(bf16[1,96,5]{1,2,0:T(8,128)(2,1)S(1)} %maximum_bitcast_fusion), channel_id=1, replica_groups=mesh['seq'=16,'fsdp'=2] {'seq'}, dimensions={0}, use_global_device_ids=true | all-gather | bytes 16320 | tf_op jit(solution)/shard_map/all_gather | solution.py:1134
  24.6 0.1 reshape.93
  24.8 0.0 copy-start.5
  24.8 0.1 dynamic-slice
  24.9 0.5 copy-done.5
  25.4 0.6 pad.25.taps
  26.0 2.4 reshape.80
  28.4 0.1 copy.54
  28.5 0.1 pad.21
  28.6 0.0 copy-done
  28.6 0.7 reshape.82
  29.3 0.0 copy-start.1
  29.3 0.1 copy.56
  29.4 0.1 pad.22
  29.4 0.2 bitcast_bitcast_fusion
  29.6 0.8 copy-done.1
  30.4 0.0 copy-start.4
  30.4 0.7 reshape.78
  31.1 0.0 copy-start.6
  31.1 0.1 copy.52
  31.2 0.1 pad.20
  31.2 0.1 copy.76
  31.3 0.1 copy-done.4
  31.4 0.1 reshape.74
  31.5 0.5 copy-done.6
  32.1 0.8 pad_maximum_fusion
  32.9 0.1 copy.50
  33.0 0.1 copy.69
  33.0 1.6 maximum_maximum_fusion.weights
  34.7 453.4 %shard_map.177 = (bf16[192,1536]{1,0:T(8,128)(2,1)}, bf16[192,1536]{1,0:T(8,128)(2,1)}, bf16[9,96,768]{2,1,0:T(8,128)(2,1)}, bf16[9,96,768]{2,1,0:T(8,128)(2,1)}...) custom-call(bf16[9,2,96,768]{3,2,1,0:T(8,128)(2,1)} %maximum_maximum_, ...), custom_call_target="tpu_custom_call" | custom-call | tf_op jit(solution)/shard_map/pallas_call | solution.py:1048
  488.0 3.0 maximum_select_fusion
  491.1 1.0 slice_bitcast_fusion
  492.2 0.1 slice_convert_fusion.2
  492.3 2.2 copy.61
  494.4 3.2 reshape.88
  497.6 1.1 copy.71
  498.8 0.1 slice_convert_fusion.1
  498.9 2.2 copy.63
  501.0 3.2 reshape.89
  504.3 0.1 slice_convert_fusion
  504.4 2.2 copy.65
  506.6 3.2 reshape.90
  509.8 1.1 slice_convert_fusion.3
  510.9 1.9 reshape.91
  512.8 0.9 copy.59
  513.7 0.0 copy-start.7
  513.7 0.0 copy-start.3
  513.7 0.0 copy-start.2
  513.8 0.9 reshape.87
  514.7 1.0 slice.61
  515.7 0.7 slice_bitcast_fusion.3
  516.4 0.0 copy-done.7
  516.4 0.8 slice.46
  517.3 38.4 %psum.7 = f32[5,1536]{1,0:T(8,128)S(1)} all-reduce(f32[5,1536]{1,0:T(8,128)S(1)} %pad_maximum_fusion.1), channel_id=1, replica_groups=mesh['seq'=16,'fsdp'=2] {'seq','fsdp'}, use_global_device_ids=true, to_apply=%region_0.1 | all-reduce | flops 7680 | bytes 61440 | tf_op jit(solution)/shard_map/psum | solution.py:1186
  555.7 0.1 constant_dynamic-slice_fusion
  555.7 0.6 slice_bitcast_fusion.4
  556.3 0.5 slice_bitcast_fusion.5
  556.9 0.0 copy-done.3
  556.9 0.8 copy.80
  557.7 0.0 copy-done.2
  557.7 0.8 copy.81
  (8 shorter events, 0.2 us)
Async XLA Ops:
  0.6 27.9 %copy-start = (bf16[96,3456]{1,0:T(8,128)(2,1)S(1)}, bf16[96,3456]{1,0:T(8,128)(2,1)}, u32[]{:S(2)}) copy-start(bf16[96,3456]{1,0:T(8,128)(2,1)} %param.18) | copy-start | bytes 1990660
  24.8 0.6 copy-start.5
  29.3 1.1 copy-start.1
  30.4 1.0 copy-start.4
  31.1 0.9 copy-start.6
  513.7 2.7 copy-start.7
  513.7 43.1 %copy-start.3 = (bf16[192,1536]{1,0:T(8,128)(2,1)S(1)}, bf16[192,1536]{1,0:T(8,128)(2,1)}, u32[]{:S(2)}) copy-start(bf16[192,1536]{1,0:T(8,128)(2,1)} %get-tuple-element.16) | copy-start | bytes 1769476
  513.7 43.9 %copy-start.2 = (bf16[192,1536]{1,0:T(8,128)(2,1)S(1)}, bf16[192,1536]{1,0:T(8,128)(2,1)}, u32[]{:S(2)}) copy-start(bf16[192,1536]{1,0:T(8,128)(2,1)} %get-tuple-element.17) | copy-start | bytes 1769476

commit v3 on v2

--- a/solution.py
+++ b/solution.py
@@ -284,16 +284,10 @@
         self.low, self.high = (self.me - 4, self.x), (self.me + 4, self.x)
         self.has_low, self.has_high = self.z > 0, self.z < planes - 1
         self.block = self.x * 2 + self.y
-        self.peers = [
-            (self.me, 1 - self.x),
-            self.across,
-            (self.across[0], 1 - self.x),
-        ]
-        self.peer_blocks = [
-            (1 - self.x) * 2 + self.y,
-            self.x * 2 + 1 - self.y,
-            (1 - self.x) * 2 + 1 - self.y,
-        ]
+        self.beside = (self.me, 1 - self.x)
+        self.beside_block = (1 - self.x) * 2 + self.y
+        self.across_block = self.x * 2 + 1 - self.y
+        self.far_block = (1 - self.x) * 2 + 1 - self.y
         self.is_first, self.is_last = self.c == 0, self.c == 1
         self.gives_next = jnp.logical_and(self.is_last, self.has_high)
         self.gives_last = jnp.logical_and(self.is_first, self.has_low)
@@ -326,20 +320,19 @@
     weights,
     tokens,
     d_out,
-    gains,
-    taps,
+    gains_here,
     result,
     d_tokens,
     own_grad,
     other_grad,
     small,
-    d_taps,
     kept_weights,
     kept_mixer,
     w,
     core_in,
     extra,
     n_one,
+    f_all,
     n_two,
     e_all,
     sent_a,
@@ -356,6 +349,14 @@
     hidden_one,
     d_hidden,
     halo,
+    gains_in,
+    gains,
+    taps,
+    small_in,
+    gain_send,
+    gain_recv,
+    small_send,
+    small_recv,
     local_sem,
     y_send,
     y_recv,
@@ -384,6 +385,7 @@
     z, y, c = at.z, at.y, at.c
     rows, width = tokens.shape
     channels = taps.shape[1]
+    count = 4 * planes
     share = weights.shape[2]
     wide = 4 * share
     chunks = parts + 2
@@ -570,70 +572,106 @@
         for copy in give_copies(k):
             copy.wait()
 
-    pause = planes - 1
-
-    def stage(o, do):
-        early = jnp.logical_and(o >= 0, o < parts)
-        late = jnp.logical_and(o >= parts + pause, o < parts + pause + 2)
-        pl.when(jnp.logical_or(early, late))(lambda: do(jnp.where(late, o - pause, o)))
-
-    def tick(i):
+    def first_hop(v):
+        core_add(v)
+        pl.when(jnp.logical_not(at.has_low))(lambda: add_up(v))
+        pl.when(jnp.logical_not(at.has_high))(lambda: add_down(v))
+
+    def tick(j):
+        def stage(o, extra_flag, do):
+            there = jnp.logical_and(o >= 0, o < chunks)
+            pl.when(jnp.logical_and(there, extra_flag))(lambda: do(o))
+
         far = jnp.maximum(z, planes - 1 - z)
-        stage(i - 1, core_add)
-        stage(i - 1 - z, add_up)
-        stage(i - 1 - (planes - 1 - z), add_down)
-        stage(i - 1 - far, give)
-
-    def all_copies(buffer, which):
-        return [
-            remote(
-                buffer.at[at.block],
-                buffer.at[at.block],
-                all_send.at[which, i],
-                all_recv.at[which, i],
-                peer,
-            )
-            for i, peer in enumerate(at.peers)
-        ]
+        stage(j - z, at.has_low, add_up)
+        stage(j - (planes - 1 - z), at.has_high, add_down)
+        stage(j - far, far >= 0, give)
+
+    part_rows = rows // 2
+
+    def half_of(buffer, block, which_half):
+        return buffer.at[block, pl.ds(which_half * part_rows, part_rows), :]
+
+    def all_copy(buffer, which, i):
+        block, which_half, to = (
+            (at.block, 0, at.beside),
+            (at.block, 1, at.across),
+            (at.block, 1, at.beside),
+            (at.block, 0, at.across),
+            (at.beside_block, 0, at.across),
+            (at.across_block, 1, at.beside),
+        )[i]
+        ref = half_of(buffer, block, which_half)
+        return remote(ref, ref, all_send.at[which, i], all_recv.at[which, i], to)
+
+    def all_landed(buffer, which, i):
+        block, which_half = (
+            (at.beside_block, 0),
+            (at.across_block, 1),
+            (at.beside_block, 1),
+            (at.across_block, 0),
+            (at.far_block, 0),
+            (at.far_block, 1),
+        )[i]
+        ref = half_of(buffer, block, which_half)
+        remote(
+            ref, ref, all_send.at[which, i], all_recv.at[which, i], at.across
+        ).wait_recv()
 
     def all_start(buffer, which):
-        for copy in all_copies(buffer, which):
-            copy.start()
+        for i in range(4):
+            all_copy(buffer, which, i).start()
+
+    def all_pass(buffer, which):
+        for i in range(2):
+            all_landed(buffer, which, i)
+            all_copy(buffer, which, 4 + i).start()
 
     def all_wait(buffer, which):
-        for i, peer in enumerate(at.peers):
-            landed = buffer.at[at.peer_blocks[i]]
-            remote(
-                landed, landed, all_send.at[which, i], all_recv.at[which, i], peer
-            ).wait_recv()
+        for i in range(2, 6):
+            all_landed(buffer, which, i)
 
     def all_done(buffer, which):
-        for copy in all_copies(buffer, which):
-            copy.wait_send()
-
-    def part_copies(source, target, which):
-        return [
-            remote(
-                source.at[at.peer_blocks[i]],
-                target.at[i],
-                part_send.at[which, i],
-                part_recv.at[which, i],
-                peer,
-            )
-            for i, peer in enumerate(at.peers)
-        ]
+        for i in range(6):
+            all_copy(buffer, which, i).wait_send()
+
+    def part_copy(source, target, which, i):
+        block, which_half, slot, to = (
+            (at.far_block, 0, 2, at.beside),
+            (at.far_block, 1, 2, at.across),
+            (at.beside_block, 0, 0, at.beside),
+            (at.across_block, 1, 1, at.across),
+            (at.across_block, 0, 1, at.across),
+            (at.beside_block, 1, 0, at.beside),
+        )[i]
+        return remote(
+            half_of(source, block, which_half),
+            half_of(target, slot, which_half),
+            part_send.at[which, i],
+            part_recv.at[which, i],
+            to,
+        )
 
     def part_start(source, target, which):
-        for copy in part_copies(source, target, which):
-            copy.start()
+        for i in range(4):
+            part_copy(source, target, which, i).start()
+
+    def part_pass(source, target, which):
+        for i, block in enumerate((at.across_block, at.beside_block)):
+            part_copy(source, target, which, i).wait_recv()
+            here = pl.ds(i * part_rows, part_rows)
+            total = source[block, here, :].astype(jnp.float32)
+            total = total + target[2, here, :].astype(jnp.float32)
+            source[block, here, :] = total.astype(jnp.bfloat16)
+            part_copy(source, target, which, 4 + i).start()
 
     def part_wait(source, target, which):
-        for copy in part_copies(source, target, which):
-            copy.wait_recv()
+        for i in range(2, 6):
+            part_copy(source, target, which, i).wait_recv()
 
     def part_done(source, target, which):
-        for copy in part_copies(source, target, which):
-            copy.wait_send()
+        for i in range(6):
+            part_copy(source, target, which, i).wait_send()
 
     tile = 48
 
@@ -649,7 +687,7 @@
 
     def summed(source, target, span):
         total = source[at.block, span, :].astype(jnp.float32)
-        for i in range(3):
+        for i in range(2):
             total = total + target[i, span, :].astype(jnp.float32)
         return total
 
@@ -683,23 +721,46 @@
 
     halo[...] = jnp.zeros_like(halo)
     barrier = pltpu.get_barrier_semaphore()
-    for device_id in [at.core] + at.peers:
-        signal(barrier, device_id)
-    pl.when(at.has_low)(lambda: signal(barrier, at.low))
-    pl.when(at.has_high)(lambda: signal(barrier, at.high))
-    pl.when(at.gives_next)(lambda: signal(barrier, at.next))
-    pl.when(at.gives_last)(lambda: signal(barrier, at.last))
-    count = 4
-    for flag in (at.has_low, at.has_high, at.gives_next, at.gives_last):
-        count = count + jnp.where(flag, 1, 0)
+    signal(barrier, at.beside)
+
+    def greet(t, carry):
+        signal(barrier, (lax.rem(at.me + t, count), at.x))
+        return carry
+
+    lax.fori_loop(1, count, greet, 0)
     pl.semaphore_wait(barrier, count)
 
+    def gain_copy(t):
+        other = lax.rem(at.me + t, count)
+        return remote(
+            gains_here,
+            gains_in.at[at.me],
+            gain_send.at[t],
+            gain_recv.at[t],
+            (other, at.x),
+        )
+
+    def gain_start(t, carry):
+        gain_copy(t).start()
+        return carry
+
+    def gain_wait(t, carry):
+        gain_copy(t).wait()
+        return carry
+
+    lax.fori_loop(1, count, gain_start, 0)
     begin(0)
     begin(1)
     e_copy = pltpu.make_async_copy(d_out, e_all.at[at.block], keep_sem.at[0])
     e_copy.start()
     small[...] = jnp.zeros_like(small)
-    d_taps[...] = jnp.zeros_like(d_taps)
+    gains_in[at.me] = gains_here[...]
+    lax.fori_loop(1, count, gain_wait, 0)
+    for d in range(count):
+        found = gains_in[d].astype(jnp.float32)[0:8, :share]
+        gains[:, d * share : (d + 1) * share] = found
+    channel_columns = pl.ds(pl.multiple_of(at.block * channels, channels), channels)
+    taps[...] = gains[:, channel_columns]
 
     def first_norm(span):
         hidden = tokens[span, :].astype(jnp.float32)
@@ -707,35 +768,45 @@
 
     by_rows(first_norm)
     all_start(n_one, 0)
+    for k in range(2, 5):
+        begin(k)
     own(0)
     own(1)
-    for k in range(2, chunks):
-        begin(k)
     relay(0, 1)
+    all_pass(n_one, 0)
     relay(1, 1)
     own(2)
     for t in range(2, planes):
         relay(0, t)
+    e_copy.wait()
+    all_start(e_all, 1)
+    begin(5)
+    relay(1, 2)
+    core_wait(0)
+    all_wait(n_one, 0)
+
+    def project_c(t, carry):
+        normed = n_one[pair(t)].reshape(2 * rows, width)
+        c_part = dot(normed, whole(0, 0, channels))
+        total_a[pair(t), :, channels : 2 * channels] = c_part.reshape(2, rows, channels)
+        return carry
+
+    def project_b_x(t, carry):
+        normed = n_one[pair(t)].reshape(2 * rows, width)
+        b_x = dot(normed, whole(1, 0, 2 * channels)).reshape(2, rows, 2 * channels)
+        total_a[pair(t), :, 0:channels] = b_x[:, :, :channels]
+        total_a[pair(t), :, 2 * channels : 3 * channels] = b_x[:, :, channels:]
+        product = (b_x[:, :, :channels] * b_x[:, :, channels:]).astype(jnp.bfloat16)
+        gated[pair(t), 8 : 8 + rows, :] = product.astype(jnp.float32)
+        return carry
+
+    lax.fori_loop(0, 2, project_c, 0)
+    for t in range(3, planes):
         relay(1, t)
     own(3)
-    own(4)
-    e_copy.wait()
-    all_start(e_all, 1)
-    core_wait(0)
+    all_pass(e_all, 1)
     core_wait(1)
-    all_wait(n_one, 0)
-
-    def project(t, carry):
-        normed = n_one[pair(t)].reshape(2 * rows, width)
-        b_c = dot(normed, whole(0, 0, 2 * channels))
-        x_part = dot(normed, whole(1, 0, channels))
-        total_a[pair(t), :, 0 : 2 * channels] = b_c.reshape(2, rows, 2 * channels)
-        total_a[pair(t), :, 2 * channels : 3 * channels] = x_part.reshape(2, rows, channels)
-        product = (b_c[:, :channels] * x_part).astype(jnp.bfloat16).astype(jnp.float32)
-        gated[pair(t), 8 : 8 + rows, :] = product.reshape(2, rows, channels)
-        return carry
-
-    lax.fori_loop(0, 2, project, 0)
+    lax.fori_loop(0, 2, project_b_x, 0)
 
     def halo_core(which, edge):
         return remote(
@@ -780,7 +851,7 @@
         conv = jnp.zeros((rows, channels), jnp.float32)
         for j in range(3):
             moved = gated[b, 6 + j : 6 + j + rows, :]
-            conv = conv + jnp.where(place >= 2 - j, moved, 0.0) * taps[j : j + 1, :]
+            conv = conv + jnp.where(place >= 2 - j, moved, 0.0) * taps[2 + j : 3 + j, :]
         total_a[b, :, 3 * channels : 4 * channels] = conv
         mixed[b] = (total_a[b, :, channels : 2 * channels] * conv).astype(jnp.bfloat16)
         return carry
@@ -790,7 +861,7 @@
     def branch(i, carry):
         t, p = lax.div(i, planes), lax.rem(i, planes)
         left = mixed[pair(t)].reshape(2 * rows, channels)
-        out = times_transposed(left, plane_rows(1, p, channels, 2 * channels))
+        out = times_transposed(left, plane_rows(0, p, channels, 2 * channels))
         sent_a[pair(t), :, columns(p)] = out.reshape(2, rows, wide).astype(jnp.bfloat16)
         return carry
 
@@ -802,13 +873,19 @@
     keep_mixer = pltpu.make_async_copy(total_a, kept_mixer, keep_sem.at[2])
     keep_weights.start()
     keep_mixer.start()
-    relays(2)
+    own(4)
+    begin(6)
+    relay(2, 1)
+    part_pass(sent_a, got_a, 0)
+    for t in range(2, planes):
+        relay(2, t)
     keep_weights.wait()
     keep_mixer.wait()
     total_a[...] = jnp.zeros_like(total_a)
     total_b[...] = jnp.zeros_like(total_b)
     all_wait(e_all, 1)
     transposed(e_all, 1)
+    relay(3, 1)
     part_wait(sent_a, got_a, 0)
 
     def second_norm(span):
@@ -818,13 +895,26 @@
 
     by_rows(second_norm)
     all_start(n_two, 2)
+    begin(7)
     part_done(sent_a, got_a, 0)
     own(5)
-    relays(3)
+    relay(3, 2)
+    all_pass(n_two, 2)
+    begin(8)
+    for t in range(3, planes):
+        relay(3, t)
     own(6)
-    relays(4)
+    relay(4, 1)
     all_wait(n_two, 2)
     transposed(n_two, 0)
+    own(7)
+    relay(4, 2)
+
+    steps = planes - 1
+
+    def relay_step(r):
+        k = 4 + lax.div(r + 2, steps)
+        pl.when(k < chunks)(lambda: relay(k, 1 + lax.rem(r + 2, steps)))
 
     def feed_forward(k):
         def half(t, carry):
@@ -853,6 +943,7 @@
                 return inner
 
             lax.fori_loop(0, planes, spread, 0)
+            pl.when(k < chunks - 1)(lambda: relay_step(2 * (k - 2) + t))
             return carry
 
         lax.fori_loop(0, 2, half, 0)
@@ -873,21 +964,24 @@
 
     def one_part(i, carry):
         k = i + 2
-        pl.when(k + 5 < chunks)(lambda: own(k + 5))
-        tick(i)
+        pl.when(i > 0)(lambda: first_hop(i - 1))
+        pl.when(i == 1)(lambda: own(8))
         core_wait(k)
         feed_forward(k)
         core_start(i)
-        pl.when(k + 3 < chunks)(lambda: relays(k + 3))
+        pl.when(jnp.logical_and(i >= 3, i <= 4))(lambda: tick(i - 2))
+
+        @pl.when(i == parts - 2)
+        def _():
+            for r in range(2 * (parts - 1), 5 * steps - 2):
+                relay_step(jnp.int32(r))
+
         return carry
 
     lax.fori_loop(0, parts, one_part, 0)
 
     restore_weights = pltpu.make_async_copy(kept_weights, w.at[pl.ds(0, 2)], keep_sem.at[1])
     restore_weights.start()
-    sum_done(0)
-    sum_done(1)
-    transposed(n_one, 2)
 
     def cast(source, target):
         def run(b, carry):
@@ -899,12 +993,12 @@
     cast(total_b, sent_a)
     part_start(sent_a, got_a, 2)
     cast(total_a, sent_b)
-    part_start(sent_b, got_b, 1)
     restore_mixer = pltpu.make_async_copy(kept_mixer, total_a, keep_sem.at[2])
     restore_mixer.start()
-    tick(parts)
+    first_hop(jnp.int32(parts - 1))
+    part_pass(sent_a, got_a, 2)
+    tick(3)
     part_wait(sent_a, got_a, 2)
-    all_done(n_one, 0)
 
     def through_second(span):
         grad = back_through_norm(
@@ -912,29 +1006,28 @@
         )
         grad = e_all[at.block, span, :].astype(jnp.float32) + grad
         d_hidden[span, :] = grad
-        n_one[at.block, span, :] = grad.astype(jnp.bfloat16)
+        f_all[at.block, span, :] = grad.astype(jnp.bfloat16)
 
     by_rows(through_second)
-    all_start(n_one, 3)
+    all_start(f_all, 3)
     part_done(sent_a, got_a, 2)
-    tick(parts + 1)
-    part_wait(sent_b, got_b, 1)
-
-    def last_out(span):
-        result[span, :] = (hidden_one[span, :] + summed(sent_b, got_b, span)).astype(jnp.bfloat16)
-
-    by_rows(last_out)
-    part_done(sent_b, got_b, 1)
+    tick(4)
+    all_pass(f_all, 3)
+    part_start(sent_b, got_b, 1)
+    sum_done(0)
+    transposed(n_one, 2)
+    all_done(n_two, 2)
     restore_weights.wait()
     restore_mixer.wait()
-    all_wait(n_one, 3)
+    tick(5)
+    all_wait(f_all, 3)
 
     def into_mixer(t, carry):
-        grad = n_one[pair(t)].reshape(2 * rows, width)
-        d_mixed = dot(grad, whole(1, channels, 2 * channels)).reshape(2, rows, channels)
+        grad = f_all[pair(t)].reshape(2 * rows, width)
+        d_mixed = dot(grad, whole(0, channels, 2 * channels)).reshape(2, rows, channels)
         conv = total_a[pair(t), :, 3 * channels : 4 * channels]
         c_part = total_a[pair(t), :, channels : 2 * channels]
-        sent_b[pair(t), :, channels : 2 * channels] = (d_mixed * conv).astype(jnp.bfloat16)
+        n_two[pair(t), :, channels : 2 * channels] = (d_mixed * conv).astype(jnp.bfloat16)
         d_conv[pair(t), 0:rows, :] = d_mixed * c_part
         return carry
 
@@ -942,16 +1035,30 @@
     head = d_conv.at[:, pl.ds(0, 8), :]
     halo_core(1, head).start()
     pl.when(at.gives_last)(lambda: halo_plane(1, head, at.last).start())
-    transposed(n_one, 3)
-
-    def d_out_weight(p, carry):
+
+    def from_c(i, carry):
+        t, p = lax.div(i, planes), lax.rem(i, planes)
+        grad = n_two[pair(t), :, channels : 2 * channels].reshape(2 * rows, channels)
+        out = times_transposed(grad, plane_rows(0, p, 0, channels))
+        total_b[pair(t), :, columns(p)] = out.reshape(2, rows, wide)
+        return carry
+
+    lax.fori_loop(0, 2 * planes, from_c, 0)
+    sum_done(1)
+    transposed(f_all, 3)
+
+    def c_and_out_weight(p, carry):
+        d_c = n_two[:, :, channels : 2 * channels].reshape(4 * rows, channels)
+        grad = dot(w[2, p].reshape(wide, 4 * rows), d_c).astype(jnp.bfloat16)
+        w[0, p, :, :, :, 0:channels] = grad.reshape(2, 2, share, channels)
         grad = dot(w[3, p].reshape(wide, 4 * rows), mixed[...].reshape(4 * rows, channels))
-        w[1, p, :, :, :, channels : 2 * channels] = grad.astype(jnp.bfloat16).reshape(
+        w[0, p, :, :, :, channels : 2 * channels] = grad.astype(jnp.bfloat16).reshape(
             2, 2, share, channels
         )
         return carry
 
-    lax.fori_loop(0, planes, d_out_weight, 0)
+    lax.fori_loop(0, planes, c_and_out_weight, 0)
+    core_start(jnp.int32(parts))
     halo_core(1, head).wait_recv()
     pl.when(at.gives_next)(lambda: halo_plane(1, head, at.next).wait_recv())
     for group in range(2):
@@ -974,44 +1081,49 @@
             moved = jnp.where(
                 place_in(b, ahead) >= ahead, d_conv[b, ahead : ahead + rows, :], 0.0
             )
-            d_gated = d_gated + moved * taps[j : j + 1, :]
+            d_gated = d_gated + moved * taps[2 + j : 3 + j, :]
             product = d_conv[b, 0:rows, :] * gated[b, 6 + j : 6 + j + rows, :]
-            d_taps[j : j + 1, :] += jnp.sum(
+            small[2 + j : 3 + j, channel_columns] += jnp.sum(
                 jnp.where(place >= ahead, product, 0.0), axis=0, keepdims=True
             )
         x_part = total_a[b, :, 2 * channels : 3 * channels]
-        sent_b[b, :, 0:channels] = (d_gated * x_part).astype(jnp.bfloat16)
+        n_two[b, :, 0:channels] = (d_gated * x_part).astype(jnp.bfloat16)
         b_part = total_a[b, :, 0:channels]
-        sent_b[b, :, 2 * channels : 3 * channels] = (d_gated * b_part).astype(jnp.bfloat16)
+        n_two[b, :, 2 * channels : 3 * channels] = (d_gated * b_part).astype(jnp.bfloat16)
         return carry
 
     lax.fori_loop(0, 4, convolve_back, 0)
+    first_hop(jnp.int32(parts))
 
     def d_normed(i, carry):
         t, p = lax.div(i, planes), lax.rem(i, planes)
-        grad = sent_b[pair(t), :, 0 : 2 * channels].reshape(2 * rows, 2 * channels)
-        out = times_transposed(grad, plane_rows(0, p, 0, 2 * channels))
-        grad = sent_b[pair(t), :, 2 * channels : 3 * channels].reshape(2 * rows, channels)
-        out = out + times_transposed(grad, plane_rows(1, p, 0, channels))
-        sent_a[pair(t), :, columns(p)] = out.reshape(2, rows, wide).astype(jnp.bfloat16)
+        grad = n_two[pair(t), :, 0:channels].reshape(2 * rows, channels)
+        out = times_transposed(grad, plane_rows(1, p, 0, channels))
+        grad = n_two[pair(t), :, 2 * channels : 3 * channels].reshape(2 * rows, channels)
+        out = out + times_transposed(grad, plane_rows(1, p, channels, 2 * channels))
+        out = total_b[pair(t), :, columns(p)] + out.reshape(2, rows, wide)
+        sent_a[pair(t), :, columns(p)] = out.astype(jnp.bfloat16)
         return carry
 
     lax.fori_loop(0, 2 * planes, d_normed, 0)
     part_start(sent_a, got_a, 3)
 
-    def d_in_weight(p, carry):
+    def b_and_x_weight(p, carry):
         normed = w[2, p].reshape(wide, 4 * rows)
-        grad = dot(normed, sent_b[:, :, 0 : 2 * channels].reshape(4 * rows, 2 * channels))
-        w[0, p] = grad.astype(jnp.bfloat16).reshape(2, 2, share, 2 * channels)
-        grad = dot(normed, sent_b[:, :, 2 * channels : 3 * channels].reshape(4 * rows, channels))
-        w[1, p, :, :, :, 0:channels] = grad.astype(jnp.bfloat16).reshape(2, 2, share, channels)
+        for low, here in ((0, 0), (channels, 2 * channels)):
+            grad = n_two[:, :, here : here + channels].reshape(4 * rows, channels)
+            grad = dot(normed, grad).astype(jnp.bfloat16)
+            w[1, p, :, :, :, low : low + channels] = grad.reshape(2, 2, share, channels)
         return carry
 
-    lax.fori_loop(0, planes, d_in_weight, 0)
-    core_start(jnp.int32(parts))
+    lax.fori_loop(0, planes, b_and_x_weight, 0)
     core_start(jnp.int32(parts + 1))
-    for i in range(parts + 2, parts + pause + 2):
-        tick(i)
+    tick(6)
+    part_pass(sent_a, got_a, 3)
+    first_hop(jnp.int32(parts + 1))
+    tick(7)
+    part_pass(sent_b, got_b, 1)
+    tick(8)
     part_wait(sent_a, got_a, 3)
 
     def through_first(span):
@@ -1020,13 +1132,46 @@
         d_tokens[span, :] = (d_hidden[span, :] + grad).astype(jnp.bfloat16)
 
     by_rows(through_first)
-    for i in range(parts + pause + 2, parts + pause + planes + 2):
-        tick(i)
+
+    def small_copy(i, to):
+        return remote(small, small_in.at[i], small_send.at[i], small_recv.at[i], to)
+
+    def small_plane(t):
+        to = lax.rem(at.me + 4 * t, count)
+        return remote(
+            small, small_in.at[2 + t], small_send.at[2 + t], small_recv.at[2 + t], (to, at.x)
+        )
+
+    small_copy(0, at.core).start()
+    tick(9)
+    for i, (here, following) in enumerate(
+        ((at.core, at.beside), (at.beside, at.across), (at.across, None))
+    ):
+        small_copy(i, here).wait()
+        small[...] += small_in[i]
+        if following is not None:
+            small_copy(i + 1, following).start()
+    for t in range(1, planes):
+        small_plane(t).start()
+    tick(10)
+    for t in range(1, planes):
+        small_plane(t).wait()
+    for t in range(1, planes):
+        small[...] += small_in[2 + t]
+    part_wait(sent_b, got_b, 1)
+
+    def last_out(span):
+        result[span, :] = (hidden_one[span, :] + summed(sent_b, got_b, span)).astype(jnp.bfloat16)
+
+    by_rows(last_out)
+    for j in range(11, chunks + planes - 1):
+        tick(j)
 
     part_done(sent_a, got_a, 3)
     all_done(e_all, 1)
-    all_done(n_two, 2)
-    all_done(n_one, 3)
+    part_done(sent_b, got_b, 1)
+    all_done(n_one, 0)
+    all_done(f_all, 3)
     halo_core(0, tail).wait_send()
     halo_core(1, head).wait_send()
     pl.when(at.gives_next)(lambda: halo_plane(0, tail, at.next).wait_send())
@@ -1035,11 +1180,11 @@
         sum_done(v)
 
 
-def one_kernel(planes, seq_len, weights, tokens, d_out, gains, taps):
+def one_kernel(planes, seq_len, weights, tokens, d_out, gains):
     chunks, _, share, cols = weights.shape
     parts = chunks - 2
     rows, width = tokens.shape
-    channels = taps.shape[1]
+    channels = width // 4
     low, full = jnp.bfloat16, jnp.float32
     shape = jax.ShapeDtypeStruct
     vmem, anywhere = pl.BlockSpec(memory_space=pltpu.VMEM), pl.BlockSpec(memory_space=pl.ANY)
@@ -1053,16 +1198,16 @@
             shape((chunks, share, cols), low),
             shape((chunks, share, cols), low),
             shape((8, width), full),
-            shape((8, channels), full),
             shape((2, planes, 2, 2, share, cols), low),
             shape(block, full),
         ),
-        in_specs=[anywhere, vmem, anywhere, vmem, vmem],
-        out_specs=[vmem, vmem, anywhere, anywhere, vmem, vmem, anywhere, anywhere],
+        in_specs=[anywhere, vmem, anywhere, vmem],
+        out_specs=[vmem, vmem, anywhere, anywhere, vmem, anywhere, anywhere],
         scratch_shapes=[
             pltpu.VMEM((chunks, planes, 2, 2, share, cols), low),
             pltpu.VMEM((2, planes, 2, share, cols), low),
             pltpu.VMEM((chunks, 2, share, cols), low),
+            pltpu.VMEM(block, low),
             pltpu.VMEM(block, low),
             pltpu.VMEM(block, low),
             pltpu.VMEM(block, low),
@@ -1080,6 +1225,14 @@
             pltpu.VMEM((rows, width), full),
             pltpu.VMEM((rows, width), full),
             pltpu.VMEM((4, 4, 8, channels), full),
+            pltpu.VMEM((4 * planes,) + gains.shape, low),
+            pltpu.VMEM((8, width), full),
+            pltpu.VMEM((8, channels), full),
+            pltpu.VMEM((2 + planes, 8, width), full),
+            dma((4 * planes,)),
+            dma((4 * planes,)),
+            dma((2 + planes,)),
+            dma((2 + planes,)),
             dma((chunks,)),
             dma((chunks,)),
             dma((chunks,)),
@@ -1096,10 +1249,10 @@
             dma((chunks,)),
             dma((chunks,)),
             dma((chunks,)),
-            dma((4, 3)),
-            dma((4, 3)),
-            dma((4, 3)),
-            dma((4, 3)),
+            dma((4, 6)),
+            dma((4, 6)),
+            dma((4, 6)),
+            dma((4, 6)),
             dma((4,)),
             dma((4,)),
             dma((3,)),
@@ -1107,7 +1260,7 @@
         compiler_params=pltpu.CompilerParams(
             collective_id=0, has_side_effects=True, vmem_limit_bytes=64 * 1024 * 1024
         ),
-    )(weights, tokens, d_out, gains, taps)
+    )(weights, tokens, d_out, gains)
 
 
 def on_device(
@@ -1131,22 +1284,14 @@
     hidden = gate_weight.shape[1] // 2
     parts = -(-hidden // PART)
 
-    gains = lax.all_gather(
-        jnp.concatenate([norm1_gain[:, None], norm2_gain[:, None], conv_kernel], axis=1),
-        "seq",
-        axis=0,
-        tiled=True,
-    ).astype(jnp.float32)
-    gains = jnp.pad(gains.T, ((0, 3), (0, 0)))
-    first_channel = x * (2 * channels) + y * channels
-    taps = lax.dynamic_slice_in_dim(gains, first_channel, channels, 1)[2:]
-    taps = jnp.pad(taps, ((0, 2), (0, 0)))
+    gains = jnp.concatenate([norm1_gain[None], norm2_gain[None], conv_kernel.T], axis=0)
+    gains = jnp.pad(gains, ((0, 16 - gains.shape[0]), (0, 128 - share)))
 
     mixer = jnp.concatenate(
         [in_weight.reshape(share, 3, 2, channels), out_weight.reshape(share, 1, 2, channels)],
         axis=1,
     )
-    mixer = mixer.reshape(share, 2, 2, 2, channels).transpose(1, 3, 0, 2, 4)
+    mixer = mixer[:, (1, 3, 0, 2)].reshape(share, 2, 2, 2, channels).transpose(1, 3, 0, 2, 4)
     mixer = mixer.reshape(2, 2, share, 2 * channels)
 
     def in_parts(weight):
@@ -1159,38 +1304,32 @@
         [in_parts(gate_weight), in_parts(up_weight), in_parts(down_weight)], axis=3
     )
     weights = jnp.concatenate([mixer, ffn], axis=0)
-    result, d_tokens, own_grad, other_grad, small, d_taps, _, _ = one_kernel(
+    result, d_tokens, own_grad, other_grad, small, _, _ = one_kernel(
         planes,
         lax.axis_size("seq") * rows // SEQS,
         weights,
         tokens[0],
         d_out[0],
         gains,
-        taps,
     )
     both = jnp.where(
         y == 0, jnp.stack([own_grad, other_grad]), jnp.stack([other_grad, own_grad])
     )
     d_mixer = both[:, :2].reshape(2, 2, share, 2, channels).transpose(2, 1, 3, 0, 4)
-    d_mixer = d_mixer.reshape(share, 4, 2 * channels).astype(jnp.float32)
+    d_mixer = d_mixer.reshape(share, 4, 2 * channels)[:, (2, 0, 3, 1)].astype(jnp.float32)
 
     def whole_grad(which):
         grad = both[:, 2:, :, which * PART : (which + 1) * PART].transpose(2, 0, 1, 3)
         grad = grad.reshape(share, 2, parts * PART)[:, :, :hidden]
         return grad.reshape(share, 2 * hidden).astype(jnp.float32)
 
-    taps_count = conv_kernel.shape[1]
-    d_kernel = lax.dynamic_update_slice(
-        jnp.zeros((taps_count, width), jnp.float32), d_taps[:taps_count], (0, first_channel)
-    )
-    sums = lax.psum(jnp.concatenate([small[:2], d_kernel], axis=0), BOTH)
-    sums = lax.dynamic_slice_in_dim(sums, here * share, share, 1)
+    sums = lax.dynamic_slice_in_dim(small, here * share, share, 1)
     return (
         result[None],
         d_tokens[None],
         sums[0],
         d_mixer[:, :3],
-        sums[2:].T,
+        sums[2:5].T,
         d_mixer[:, 3],
         sums[1],
         whole_grad(0),

time: 566 us -> 406 us (0.72)
  Pallas kernels: 453 us -> 362 us
  blocking collectives: 61.6 us -> 0 us
    pallas_call x1, Pallas kernels: 453 us -> 362 us  [one_kernel(): pl.pallas_call(functools.partial(kernel, planes, parts, seq_len), out_sha...]
    psum x1 -> x0, blocking collectives: 38.4 us -> none  [on_device(): sums = lax.psum(jnp.concatenate([small[:2], d_kernel], axis=0), BOTH)]
    all_gather x1 -> x0, blocking collectives: 23.2 us -> none  [on_device(): lax.all_gather(jnp.concatenate([norm1_gain[:, None], norm2_gain[:, None],...]
    convert_element_type x6, local copies, waits for them, and re-layouts: 16.1 us -> 9.71 us  [whole_grad(): return grad.reshape(share, 2 * hidden).astype(jnp.float32)]
    reshape x0 -> x3, local copies, waits for them, and re-layouts: none -> 5.99 us  [the longest x2 3.24 us: on_device(): both[:, :2].reshape(2, 2, share, 2, channels).transpose(2, 1, 3, 0, 4)]
where the time goes in v3:
time: 406 us; the launch traced here: 400 us
  Pallas kernels  362 us (89%)
  local copies, waits for them, and re-layouts  31.5 us (8%)
  other arithmetic  5.6 us (1%)
    pallas_call x1, Pallas kernels, one_kernel(): pl.pallas_call(functools.partial(kernel, planes, parts, seq_len), out_sha...  362 us
    convert_element_type x6, local copies, waits for them, and re-layouts, whole_grad(): return grad.reshape(share, 2 * hidden).astype(jnp.float32)  9.71 us

profile of v3, /device:TPU:0, one launch (start us, length us, event | category | flops | bytes accessed | tf_op | source)
XLA Modules:
  0.0 400.0 jit_solution(8673775507669735049)
XLA Ops:
  0.6 0.0 copy-start.1
  0.7 2.5 reshape.82
  3.2 0.1 copy.54
  3.3 0.1 pad.16
  3.3 0.0 copy-done.1
  3.3 0.7 reshape.80
  4.0 0.0 copy-start.2
  4.0 0.1 copy.52
  4.1 0.1 pad.15
  4.2 0.2 bitcast_bitcast_fusion
  4.3 0.8 copy-done.2
  5.1 0.7 reshape.78
  5.8 0.0 copy-start.5
  5.8 0.1 copy.50
  5.9 0.0 copy-start.11
  5.9 0.1 pad.14
  6.0 0.1 copy.76
  6.0 0.0 copy-done.6
  6.1 0.7 copy-done.5
  6.9 0.1 pad_maximum_fusion
  7.0 0.0 copy-done.11
  7.0 0.7 gather_fusion
  7.7 0.1 copy.67
  7.8 0.0 copy-start.7
  7.8 0.0 copy-start.8
  7.8 0.0 copy-start.9
  7.8 1.6 maximum_maximum_fusion.weights
  9.4 0.0 copy-done.7
  9.4 0.0 copy-done.8
  9.4 0.0 copy-done.9
  9.4 0.6 fusion.8.gains_here
  10.0 361.7 %shard_map.195 = (bf16[192,1536]{1,0:T(8,128)(2,1)}, bf16[192,1536]{1,0:T(8,128)(2,1)}, bf16[9,96,768]{2,1,0:T(8,128)(2,1)}, bf16[9,96,768]{2,1,0:T(8,128)(2,1)}...) custom-call(bf16[9,2,96,768]{3,2,1,0:T(8,128)(2,1)} %maximum_maximum_fusion.weights, ...), custom_call_target="tpu_custom_call" | custom-call | tf_op jit(solution)/shard_map/pallas_call | solution.py:1193
  371.7 0.8 constant_dynamic-slice_fusion
  372.5 0.5 slice_bitcast_fusion.5
  373.0 3.0 maximum_select_fusion
  376.0 0.0 copy-start.10
  376.0 0.9 slice.52
  376.8 1.8 reshape.84
  378.7 1.4 copy.77
  380.1 2.8 reshape.85
  382.8 0.0 copy-done.10
  382.9 1.7 gather_fusion.1
  384.5 0.1 convert_bitcast_fusion
  384.6 1.0 slice.53
  385.6 0.6 slice_bitcast_fusion.4
  386.2 0.7 slice_bitcast_fusion.3
  386.9 1.0 slice_bitcast_fusion
  388.0 0.1 slice_convert_fusion.2
  388.1 0.0 copy-start
  388.1 1.1 copy.58
  389.2 2.2 reshape.89
  391.4 0.0 copy-done
  391.4 0.1 slice_convert_fusion.1
  391.5 1.1 copy.60
  392.6 2.2 reshape.90
  394.8 0.1 slice_convert_fusion
  394.9 0.0 copy-start.4
  394.9 0.0 copy-start.3
  394.9 1.1 copy.62
  396.0 2.2 reshape.91
  398.2 0.0 copy-done.4
  398.2 0.8 copy.81
  399.0 0.0 copy-done.3
  399.0 0.8 copy.82
  (9 shorter events, 0.3 us)
Async XLA Ops:
  0.6 2.7 copy-start.1
  4.0 1.1 copy-start.2
  5.1 0.9 copy-start.6
  5.8 1.0 copy-start.5
  5.9 1.1 copy-start.11
  7.8 1.6 copy-start.7
  7.8 1.6 copy-start.8
  7.8 1.6 copy-start.9
  376.0 6.9 %copy-start.10 = (s32[4]{0:T(128)S(1)}, s32[4]{0:T(128)}, u32[]{:S(2)}) copy-start(s32[4]{0:T(128)} %constant.65) | copy-start | bytes 52
  388.1 3.3 copy-start
  394.9 3.3 copy-start.4
  394.9 4.1 %copy-start.3 = (bf16[192,1536]{1,0:T(8,128)(2,1)S(1)}, bf16[192,1536]{1,0:T(8,128)(2,1)}, u32[]{:S(2)}) copy-start(bf16[192,1536]{1,0:T(8,128)(2,1)} %get-tuple-element.16) | copy-start | bytes 1769476

commit v4 on v3

--- a/solution.py
+++ b/solution.py
@@ -340,7 +340,6 @@
     total_a,
     total_b,
     got_a,
-    got_b,
     gated,
     d_conv,
     mixed,
@@ -440,9 +439,16 @@
             pl.when(at.has_low)(lambda: to_side(k, above, 0).start())
             to_core(k, above).start()
 
-    def relays(k):
-        for t in range(1, planes):
-            relay(k, t)
+    between = jnp.logical_and(at.has_low, at.has_high)
+
+    def pass_on(k, t):
+        pl.when(between)(lambda: relay(k, t))
+
+    def take_last(k):
+        @pl.when(jnp.logical_not(between))
+        def _():
+            for t in range(1, planes):
+                relay(k, t)
 
     def core_wait(k):
         for p in range(planes):
@@ -710,14 +716,18 @@
     def whole(k, low, high):
         return w[k, :, :, :, :, low:high].reshape(planes * wide, high - low)
 
-    def plane_rows(k, p, low, high):
-        return w[k, p, :, :, :, low:high].reshape(wide, high - low)
+    def two_planes(k, q, low, high):
+        return w[k, pair(q), :, :, :, low:high].reshape(2 * wide, high - low)
 
     def pair(t):
         return pl.ds(2 * t, 2)
 
-    def columns(p):
-        return pl.ds(pl.multiple_of(p * wide, wide), wide)
+    def two_columns(q):
+        return pl.ds(pl.multiple_of(q * 2 * wide, 2 * wide), 2 * wide)
+
+    def weight_grad(turned, grads, k, span):
+        out = dot(w[turned].reshape(planes * wide, 4 * rows), grads).astype(jnp.bfloat16)
+        w[k, :, :, :, :, span] = out.reshape(planes, 2, 2, share, grads.shape[1])
 
     halo[...] = jnp.zeros_like(halo)
     barrier = pltpu.get_barrier_semaphore()
@@ -768,20 +778,22 @@
 
     by_rows(first_norm)
     all_start(n_one, 0)
-    for k in range(2, 5):
-        begin(k)
+    begin(2)
     own(0)
     own(1)
     relay(0, 1)
     all_pass(n_one, 0)
-    relay(1, 1)
-    own(2)
-    for t in range(2, planes):
-        relay(0, t)
     e_copy.wait()
     all_start(e_all, 1)
-    begin(5)
+    begin(3)
+    relay(1, 1)
+    relay(0, 2)
     relay(1, 2)
+    own(2)
+    all_pass(e_all, 1)
+    begin(4)
+    for t in range(3, planes):
+        relay(0, t)
     core_wait(0)
     all_wait(n_one, 0)
 
@@ -804,7 +816,6 @@
     for t in range(3, planes):
         relay(1, t)
     own(3)
-    all_pass(e_all, 1)
     core_wait(1)
     lax.fori_loop(0, 2, project_b_x, 0)
 
@@ -859,13 +870,14 @@
     lax.fori_loop(0, 4, convolve, 0)
 
     def branch(i, carry):
-        t, p = lax.div(i, planes), lax.rem(i, planes)
+        t, q = lax.div(i, planes // 2), lax.rem(i, planes // 2)
         left = mixed[pair(t)].reshape(2 * rows, channels)
-        out = times_transposed(left, plane_rows(0, p, channels, 2 * channels))
-        sent_a[pair(t), :, columns(p)] = out.reshape(2, rows, wide).astype(jnp.bfloat16)
+        out = times_transposed(left, two_planes(0, q, channels, 2 * channels))
+        out = out.reshape(2, rows, 2 * wide).astype(jnp.bfloat16)
+        sent_a[pair(t), :, two_columns(q)] = out
         return carry
 
-    lax.fori_loop(0, 2 * planes, branch, 0)
+    lax.fori_loop(0, planes, branch, 0)
     part_start(sent_a, got_a, 0)
     gather_done(0)
     gather_done(1)
@@ -873,19 +885,18 @@
     keep_mixer = pltpu.make_async_copy(total_a, kept_mixer, keep_sem.at[2])
     keep_weights.start()
     keep_mixer.start()
+    pass_on(2, 1)
+    part_pass(sent_a, got_a, 0)
     own(4)
-    begin(6)
-    relay(2, 1)
-    part_pass(sent_a, got_a, 0)
+    begin(5)
     for t in range(2, planes):
-        relay(2, t)
+        pass_on(2, t)
     keep_weights.wait()
     keep_mixer.wait()
     total_a[...] = jnp.zeros_like(total_a)
     total_b[...] = jnp.zeros_like(total_b)
     all_wait(e_all, 1)
     transposed(e_all, 1)
-    relay(3, 1)
     part_wait(sent_a, got_a, 0)
 
     def second_norm(span):
@@ -895,26 +906,28 @@
 
     by_rows(second_norm)
     all_start(n_two, 2)
+    part_done(sent_a, got_a, 0)
+    pass_on(3, 1)
+    own(5)
+    all_pass(n_two, 2)
+    begin(6)
     begin(7)
-    part_done(sent_a, got_a, 0)
-    own(5)
-    relay(3, 2)
-    all_pass(n_two, 2)
     begin(8)
-    for t in range(3, planes):
-        relay(3, t)
+    for t in range(2, planes):
+        pass_on(3, t)
     own(6)
-    relay(4, 1)
+    pass_on(4, 1)
     all_wait(n_two, 2)
     transposed(n_two, 0)
     own(7)
-    relay(4, 2)
-
-    steps = planes - 1
-
-    def relay_step(r):
-        k = 4 + lax.div(r + 2, steps)
-        pl.when(k < chunks)(lambda: relay(k, 1 + lax.rem(r + 2, steps)))
+    take_last(2)
+
+    def cast(source, target):
+        def run(b, carry):
+            target[b] = source[b].astype(jnp.bfloat16)
+            return carry
+
+        lax.fori_loop(0, 4, run, 0)
 
     def feed_forward(k):
         def half(t, carry):
@@ -933,48 +946,53 @@
                 d_active * upper * sigma * (1.0 + gate * (1.0 - sigma))
             ).astype(jnp.bfloat16)
 
-            def spread(p, inner):
-                back = times_transposed(d_gate_up[here, :], plane_rows(k, p, 0, 2 * step_cols))
-                total_b[pair(t), :, columns(p)] += back.reshape(2, rows, wide)
+            def spread(q, inner):
+                back = times_transposed(d_gate_up[here, :], two_planes(k, q, 0, 2 * step_cols))
+                total_b[pair(t), :, two_columns(q)] += back.reshape(2, rows, 2 * wide)
                 out = times_transposed(
-                    active[here, :], plane_rows(k, p, 2 * step_cols, 3 * step_cols)
+                    active[here, :], two_planes(k, q, 2 * step_cols, 3 * step_cols)
                 )
-                total_a[pair(t), :, columns(p)] += out.reshape(2, rows, wide)
+                total_a[pair(t), :, two_columns(q)] += out.reshape(2, rows, 2 * wide)
                 return inner
 
-            lax.fori_loop(0, planes, spread, 0)
-            pl.when(k < chunks - 1)(lambda: relay_step(2 * (k - 2) + t))
+            lax.fori_loop(0, planes // 2, spread, 0)
+            early = jnp.logical_and(between, jnp.logical_and(t == 0, k > 2))
+            pl.when(early)(lambda: first_hop(k - 3))
+            pl.when(jnp.logical_and(t == 0, k + 3 < chunks))(lambda: pass_on(k + 3, 1))
+            pl.when(jnp.logical_and(t == 1, k + 2 < chunks))(lambda: pass_on(k + 2, 2))
             return carry
 
         lax.fori_loop(0, 2, half, 0)
+
+        @pl.when(k == chunks - 1)
+        def _():
+            cast(total_b, sent_a)
+            part_start(sent_a, got_a, 2)
+
         gather_done(k)
 
-        def grads(p, carry):
-            low = dot(w[0, p].reshape(wide, 4 * rows), d_gate_up[...])
-            w[k, p, :, :, :, 0 : 2 * step_cols] = low.astype(jnp.bfloat16).reshape(
-                2, 2, share, 2 * step_cols
-            )
-            high = dot(w[1, p].reshape(wide, 4 * rows), active[...])
-            w[k, p, :, :, :, 2 * step_cols : 3 * step_cols] = high.astype(jnp.bfloat16).reshape(
-                2, 2, share, step_cols
-            )
+        def grads(n, carry):
+            span = pl.ds(pl.multiple_of(n * step_cols, step_cols), step_cols)
+            weight_grad(0, d_gate_up[:, span], k, span)
             return carry
 
-        lax.fori_loop(0, planes, grads, 0)
+        lax.fori_loop(0, 2, grads, 0)
+        weight_grad(1, active[...], k, pl.ds(2 * step_cols, step_cols))
 
     def one_part(i, carry):
         k = i + 2
-        pl.when(i > 0)(lambda: first_hop(i - 1))
         pl.when(i == 1)(lambda: own(8))
         core_wait(k)
         feed_forward(k)
         core_start(i)
-        pl.when(jnp.logical_and(i >= 3, i <= 4))(lambda: tick(i - 2))
-
-        @pl.when(i == parts - 2)
+        pl.when(jnp.logical_not(between))(lambda: first_hop(i))
+        pl.when(jnp.logical_and(i >= 3, i < parts - 1))(lambda: tick(i - 2))
+
+        @pl.when(k + 1 < chunks)
         def _():
-            for r in range(2 * (parts - 1), 5 * steps - 2):
-                relay_step(jnp.int32(r))
+            take_last(k + 1)
+            for t in range(3, planes):
+                pass_on(k + 1, t)
 
         return carry
 
@@ -983,21 +1001,12 @@
     restore_weights = pltpu.make_async_copy(kept_weights, w.at[pl.ds(0, 2)], keep_sem.at[1])
     restore_weights.start()
 
-    def cast(source, target):
-        def run(b, carry):
-            target[b] = source[b].astype(jnp.bfloat16)
-            return carry
-
-        lax.fori_loop(0, 4, run, 0)
-
-    cast(total_b, sent_a)
-    part_start(sent_a, got_a, 2)
     cast(total_a, sent_b)
     restore_mixer = pltpu.make_async_copy(kept_mixer, total_a, keep_sem.at[2])
     restore_mixer.start()
-    first_hop(jnp.int32(parts - 1))
+    pl.when(between)(lambda: first_hop(jnp.int32(parts - 1)))
     part_pass(sent_a, got_a, 2)
-    tick(3)
+    tick(4)
     part_wait(sent_a, got_a, 2)
 
     def through_second(span):
@@ -1009,17 +1018,18 @@
         f_all[at.block, span, :] = grad.astype(jnp.bfloat16)
 
     by_rows(through_second)
+    all_done(n_two, 2)
     all_start(f_all, 3)
     part_done(sent_a, got_a, 2)
-    tick(4)
     all_pass(f_all, 3)
-    part_start(sent_b, got_b, 1)
+    part_start(sent_b, n_two, 1)
     sum_done(0)
     transposed(n_one, 2)
-    all_done(n_two, 2)
+    all_done(n_one, 0)
     restore_weights.wait()
     restore_mixer.wait()
     tick(5)
+    tick(6)
     all_wait(f_all, 3)
 
     def into_mixer(t, carry):
@@ -1027,7 +1037,7 @@
         d_mixed = dot(grad, whole(0, channels, 2 * channels)).reshape(2, rows, channels)
         conv = total_a[pair(t), :, 3 * channels : 4 * channels]
         c_part = total_a[pair(t), :, channels : 2 * channels]
-        n_two[pair(t), :, channels : 2 * channels] = (d_mixed * conv).astype(jnp.bfloat16)
+        n_one[pair(t), :, 2 * channels : 3 * channels] = (d_mixed * conv).astype(jnp.bfloat16)
         d_conv[pair(t), 0:rows, :] = d_mixed * c_part
         return carry
 
@@ -1037,27 +1047,19 @@
     pl.when(at.gives_last)(lambda: halo_plane(1, head, at.last).start())
 
     def from_c(i, carry):
-        t, p = lax.div(i, planes), lax.rem(i, planes)
-        grad = n_two[pair(t), :, channels : 2 * channels].reshape(2 * rows, channels)
-        out = times_transposed(grad, plane_rows(0, p, 0, channels))
-        total_b[pair(t), :, columns(p)] = out.reshape(2, rows, wide)
+        t, q = lax.div(i, planes // 2), lax.rem(i, planes // 2)
+        grad = n_one[pair(t), :, 2 * channels : 3 * channels].reshape(2 * rows, channels)
+        out = times_transposed(grad, two_planes(0, q, 0, channels))
+        total_b[pair(t), :, two_columns(q)] = out.reshape(2, rows, 2 * wide)
         return carry
 
-    lax.fori_loop(0, 2 * planes, from_c, 0)
+    lax.fori_loop(0, planes, from_c, 0)
     sum_done(1)
     transposed(f_all, 3)
 
-    def c_and_out_weight(p, carry):
-        d_c = n_two[:, :, channels : 2 * channels].reshape(4 * rows, channels)
-        grad = dot(w[2, p].reshape(wide, 4 * rows), d_c).astype(jnp.bfloat16)
-        w[0, p, :, :, :, 0:channels] = grad.reshape(2, 2, share, channels)
-        grad = dot(w[3, p].reshape(wide, 4 * rows), mixed[...].reshape(4 * rows, channels))
-        w[0, p, :, :, :, channels : 2 * channels] = grad.astype(jnp.bfloat16).reshape(
-            2, 2, share, channels
-        )
-        return carry
-
-    lax.fori_loop(0, planes, c_and_out_weight, 0)
+    d_c = n_one[:, :, 2 * channels : 3 * channels].reshape(4 * rows, channels)
+    weight_grad(2, d_c, 0, pl.ds(0, channels))
+    weight_grad(3, mixed[...].reshape(4 * rows, channels), 0, pl.ds(channels, channels))
     core_start(jnp.int32(parts))
     halo_core(1, head).wait_recv()
     pl.when(at.gives_next)(lambda: halo_plane(1, head, at.next).wait_recv())
@@ -1087,42 +1089,37 @@
                 jnp.where(place >= ahead, product, 0.0), axis=0, keepdims=True
             )
         x_part = total_a[b, :, 2 * channels : 3 * channels]
-        n_two[b, :, 0:channels] = (d_gated * x_part).astype(jnp.bfloat16)
+        n_one[b, :, 0:channels] = (d_gated * x_part).astype(jnp.bfloat16)
         b_part = total_a[b, :, 0:channels]
-        n_two[b, :, 2 * channels : 3 * channels] = (d_gated * b_part).astype(jnp.bfloat16)
+        n_one[b, :, channels : 2 * channels] = (d_gated * b_part).astype(jnp.bfloat16)
         return carry
 
     lax.fori_loop(0, 4, convolve_back, 0)
     first_hop(jnp.int32(parts))
 
     def d_normed(i, carry):
-        t, p = lax.div(i, planes), lax.rem(i, planes)
-        grad = n_two[pair(t), :, 0:channels].reshape(2 * rows, channels)
-        out = times_transposed(grad, plane_rows(1, p, 0, channels))
-        grad = n_two[pair(t), :, 2 * channels : 3 * channels].reshape(2 * rows, channels)
-        out = out + times_transposed(grad, plane_rows(1, p, channels, 2 * channels))
-        out = total_b[pair(t), :, columns(p)] + out.reshape(2, rows, wide)
-        sent_a[pair(t), :, columns(p)] = out.astype(jnp.bfloat16)
+        t, q = lax.div(i, planes // 2), lax.rem(i, planes // 2)
+        grad = n_one[pair(t), :, 0 : 2 * channels].reshape(2 * rows, 2 * channels)
+        out = times_transposed(grad, two_planes(1, q, 0, 2 * channels))
+        out = total_b[pair(t), :, two_columns(q)] + out.reshape(2, rows, 2 * wide)
+        sent_a[pair(t), :, two_columns(q)] = out.astype(jnp.bfloat16)
         return carry
 
-    lax.fori_loop(0, 2 * planes, d_normed, 0)
+    lax.fori_loop(0, planes, d_normed, 0)
     part_start(sent_a, got_a, 3)
 
-    def b_and_x_weight(p, carry):
-        normed = w[2, p].reshape(wide, 4 * rows)
-        for low, here in ((0, 0), (channels, 2 * channels)):
-            grad = n_two[:, :, here : here + channels].reshape(4 * rows, channels)
-            grad = dot(normed, grad).astype(jnp.bfloat16)
-            w[1, p, :, :, :, low : low + channels] = grad.reshape(2, 2, share, channels)
+    def b_and_x_weight(n, carry):
+        span = pl.ds(pl.multiple_of(n * channels, channels), channels)
+        grad = n_one[:, :, span].reshape(4 * rows, channels)
+        weight_grad(2, grad, 1, span)
         return carry
 
-    lax.fori_loop(0, planes, b_and_x_weight, 0)
+    lax.fori_loop(0, 2, b_and_x_weight, 0)
     core_start(jnp.int32(parts + 1))
-    tick(6)
+    tick(7)
     part_pass(sent_a, got_a, 3)
     first_hop(jnp.int32(parts + 1))
-    tick(7)
-    part_pass(sent_b, got_b, 1)
+    part_pass(sent_b, n_two, 1)
     tick(8)
     part_wait(sent_a, got_a, 3)
 
@@ -1158,10 +1155,10 @@
         small_plane(t).wait()
     for t in range(1, planes):
         small[...] += small_in[2 + t]
-    part_wait(sent_b, got_b, 1)
+    part_wait(sent_b, n_two, 1)
 
     def last_out(span):
-        result[span, :] = (hidden_one[span, :] + summed(sent_b, got_b, span)).astype(jnp.bfloat16)
+        result[span, :] = (hidden_one[span, :] + summed(sent_b, n_two, span)).astype(jnp.bfloat16)
 
     by_rows(last_out)
     for j in range(11, chunks + planes - 1):
@@ -1169,8 +1166,7 @@
 
     part_done(sent_a, got_a, 3)
     all_done(e_all, 1)
-    part_done(sent_b, got_b, 1)
-    all_done(n_one, 0)
+    part_done(sent_b, n_two, 1)
     all_done(f_all, 3)
     halo_core(0, tail).wait_send()
     halo_core(1, head).wait_send()
@@ -1215,7 +1211,6 @@
             pltpu.VMEM(block, low),
             pltpu.VMEM(block, full),
             pltpu.VMEM(block, full),
-            pltpu.VMEM((3, rows, width), low),
             pltpu.VMEM((3, rows, width), low),
             pltpu.VMEM((4, rows + 8, channels), full),
             pltpu.VMEM((4, rows + 8, channels), full),
@@ -1263,6 +1258,106 @@
     )(weights, tokens, d_out, gains)
 
 
+def split_kernel(hidden, parts, gate, up, down, in_weight, out_weight, weights):
+    channels = out_weight.shape[1] // 2
+    left = parts * PART - hidden
+    blank = jnp.zeros((gate.shape[0], left), jnp.bfloat16)
+    for which, source in enumerate((gate, up, down)):
+        here = pl.ds(which * PART, PART)
+        for half in range(2):
+            for part in range(parts):
+                low = half * hidden + part * PART
+                if part < parts - 1 or left == 0:
+                    weights[2 + part, half, :, here] = source[:, low : low + PART]
+                else:
+                    last = source[:, low : low + PART - left]
+                    weights[2 + part, half, :, here] = jnp.concatenate([last, blank], axis=1)
+    for half in range(2):
+        span = slice(half * channels, (half + 1) * channels)
+        weights[0, half, :, 0:channels] = in_weight[1, :, span]
+        weights[0, half, :, channels:] = out_weight[:, span]
+        weights[1, half, :, 0:channels] = in_weight[0, :, span]
+        weights[1, half, :, channels:] = in_weight[2, :, span]
+
+
+def split(gate, up, down, in_weight, out_weight, step=32):
+    share, columns = gate.shape
+    hidden = columns // 2
+    parts = -(-hidden // PART)
+    by_rows = pl.BlockSpec((step, columns), lambda i: (i, 0))
+    cols = 3 * PART
+    return pl.pallas_call(
+        functools.partial(split_kernel, hidden, parts),
+        grid=(share // step,),
+        out_shape=jax.ShapeDtypeStruct((parts + 2, 2, share, cols), jnp.bfloat16),
+        in_specs=[
+            by_rows,
+            by_rows,
+            by_rows,
+            pl.BlockSpec((3, step, in_weight.shape[2]), lambda i: (0, i, 0)),
+            pl.BlockSpec((step, out_weight.shape[1]), lambda i: (i, 0)),
+        ],
+        out_specs=pl.BlockSpec((parts + 2, 2, step, cols), lambda i: (0, 0, i, 0)),
+    )(gate, up, down, in_weight, out_weight)
+
+
+def join_kernel(hidden, parts, own, other, gate, up, down, in_weight, out_weight):
+    channels = out_weight.shape[1] // 2
+    side = lax.rem(lax.div(lax.axis_index("seq"), 2), 2)
+
+    def put(half, source):
+        for which, target in enumerate((gate, up, down)):
+            pieces = [
+                source[2 + part, :, which * PART : (which + 1) * PART].astype(jnp.float32)
+                for part in range(parts)
+            ]
+            whole = jnp.concatenate(pieces, axis=1)[:, :hidden]
+            target[:, half * hidden : (half + 1) * hidden] = whole
+        span = slice(half * channels, (half + 1) * channels)
+        in_weight[1, :, span] = source[0, :, 0:channels].astype(jnp.float32)
+        out_weight[:, span] = source[0, :, channels:].astype(jnp.float32)
+        in_weight[0, :, span] = source[1, :, 0:channels].astype(jnp.float32)
+        in_weight[2, :, span] = source[1, :, channels:].astype(jnp.float32)
+
+    @pl.when(side == 0)
+    def _():
+        put(0, own)
+        put(1, other)
+
+    @pl.when(side == 1)
+    def _():
+        put(0, other)
+        put(1, own)
+
+
+def join(own, other, hidden, channels, step=32):
+    chunks, share, cols = own.shape
+    parts = chunks - 2
+    full = jnp.float32
+    part = pl.BlockSpec((chunks, step, cols), lambda i: (0, i, 0))
+    by_rows = pl.BlockSpec((step, 2 * hidden), lambda i: (i, 0))
+    shape = jax.ShapeDtypeStruct
+    return pl.pallas_call(
+        functools.partial(join_kernel, hidden, parts),
+        grid=(share // step,),
+        out_shape=(
+            shape((share, 2 * hidden), full),
+            shape((share, 2 * hidden), full),
+            shape((share, 2 * hidden), full),
+            shape((3, share, 2 * channels), full),
+            shape((share, 2 * channels), full),
+        ),
+        in_specs=[part, part],
+        out_specs=(
+            by_rows,
+            by_rows,
+            by_rows,
+            pl.BlockSpec((3, step, 2 * channels), lambda i: (0, i, 0)),
+            pl.BlockSpec((step, 2 * channels), lambda i: (i, 0)),
+        ),
+    )(own, other)
+
+
 def on_device(
     tokens,
     norm1_gain,
@@ -1277,33 +1372,17 @@
 ):
     planes = lax.axis_size("seq") // 4
     here = lax.axis_index("seq")
-    y, x = (here // 2) % 2, lax.axis_index("fsdp")
     rows, width = tokens.shape[1:]
     share = gate_weight.shape[0]
     channels = in_weight.shape[2] // 2
     hidden = gate_weight.shape[1] // 2
-    parts = -(-hidden // PART)
 
     gains = jnp.concatenate([norm1_gain[None], norm2_gain[None], conv_kernel.T], axis=0)
     gains = jnp.pad(gains, ((0, 16 - gains.shape[0]), (0, 128 - share)))
 
-    mixer = jnp.concatenate(
-        [in_weight.reshape(share, 3, 2, channels), out_weight.reshape(share, 1, 2, channels)],
-        axis=1,
+    weights = split(
+        gate_weight, up_weight, down_weight, jnp.swapaxes(in_weight, 0, 1), out_weight
     )
-    mixer = mixer[:, (1, 3, 0, 2)].reshape(share, 2, 2, 2, channels).transpose(1, 3, 0, 2, 4)
-    mixer = mixer.reshape(2, 2, share, 2 * channels)
-
-    def in_parts(weight):
-        halves = jnp.pad(
-            weight.reshape(share, 2, hidden), ((0, 0), (0, 0), (0, parts * PART - hidden))
-        )
-        return halves.reshape(share, 2, parts, PART).transpose(2, 1, 0, 3)
-
-    ffn = jnp.concatenate(
-        [in_parts(gate_weight), in_parts(up_weight), in_parts(down_weight)], axis=3
-    )
-    weights = jnp.concatenate([mixer, ffn], axis=0)
     result, d_tokens, own_grad, other_grad, small, _, _ = one_kernel(
         planes,
         lax.axis_size("seq") * rows // SEQS,
@@ -1312,29 +1391,19 @@
         d_out[0],
         gains,
     )
-    both = jnp.where(
-        y == 0, jnp.stack([own_grad, other_grad]), jnp.stack([other_grad, own_grad])
-    )
-    d_mixer = both[:, :2].reshape(2, 2, share, 2, channels).transpose(2, 1, 3, 0, 4)
-    d_mixer = d_mixer.reshape(share, 4, 2 * channels)[:, (2, 0, 3, 1)].astype(jnp.float32)
-
-    def whole_grad(which):
-        grad = both[:, 2:, :, which * PART : (which + 1) * PART].transpose(2, 0, 1, 3)
-        grad = grad.reshape(share, 2, parts * PART)[:, :, :hidden]
-        return grad.reshape(share, 2 * hidden).astype(jnp.float32)
-
+    d_gate, d_up, d_down, d_in, d_branch = join(own_grad, other_grad, hidden, channels)
     sums = lax.dynamic_slice_in_dim(small, here * share, share, 1)
     return (
         result[None],
         d_tokens[None],
         sums[0],
-        d_mixer[:, :3],
+        jnp.swapaxes(d_in, 0, 1),
         sums[2:5].T,
-        d_mixer[:, 3],
+        d_branch,
         sums[1],
-        whole_grad(0),
-        whole_grad(1),
-        whole_grad(2),
+        d_gate,
+        d_up,
+        d_down,
     )
 
 

time: 406 us -> 356 us (0.88)
  local copies, waits for them, and re-layouts: 31.5 us -> 3.52 us
  Pallas kernels: 362 us -> 347 us
  other arithmetic: 5.6 us -> 0.6 us
    pallas_call x1, Pallas kernels: 362 us -> 338 us  [one_kernel(): pl.pallas_call(functools.partial(kernel, planes, parts, seq_len), out_sha...]
    reshape x17 -> x0, local copies, waits for them, and re-layouts: 10.5 us -> none  [the longest x6 4.11 us: in_parts(): weight.reshape(share, 2, hidden)]
    convert_element_type x6 -> x0, local copies, waits for them, and re-layouts: 9.71 us -> none  [whole_grad(): return grad.reshape(share, 2 * hidden).astype(jnp.float32)]
    pallas_call x0 -> x2, Pallas kernels: none -> 9.31 us  [the longest x1 4.67 us: join(): pl.pallas_call(functools.partial(join_kernel, hidden, parts), grid=(share...]
where the time goes in v4:
time: 356 us; the launch traced here: 352 us
  Pallas kernels  347 us (97%)
    pallas_call x1, Pallas kernels, one_kernel(): pl.pallas_call(functools.partial(kernel, planes, parts, seq_len), out_sha...  338 us

profile of v4, /device:TPU:0, one launch (start us, length us, event | category | flops | bytes accessed | tf_op | source)
XLA Modules:
  0.0 352.5 jit_solution(17788582082268380033)
XLA Ops:
  0.6 0.0 copy-start.2
  0.7 0.0 copy-start.3
  0.7 0.0 copy-start.4
  0.7 4.6 %shard_map.177.weights = bf16[9,2,96,768]{3,2,1,0:T(8,128)(2,1)} custom-call(bf16[96,3456]{1,0:T(8,128)(2,1)} %gate.1, bf16[96,3456]{1,0:T(8,128)(2,1)} %up.1, bf16[96,3456]{1,0:T(8,128)(2,1)} %down.1, bf16[3,96,768]{2,1,0:T(8,128)(2,1)} %bitcast.19, bf16[96,768]{1,0:T(8,128)(2,1)} %out_weight.1), custom_call_target="tpu_custom_call" | custom-call | tf_op jit(solution)/shard_map/pallas_call | solution.py:1289
  5.3 0.0 copy-done.2
  5.3 0.0 copy-done.3
  5.3 0.0 copy-done.4
  5.3 0.6 fusion.8.gains_here
  5.9 337.9 %shard_map.178 = (bf16[192,1536]{1,0:T(8,128)(2,1)}, bf16[192,1536]{1,0:T(8,128)(2,1)}, bf16[9,96,768]{2,1,0:T(8,128)(2,1)}, bf16[9,96,768]{2,1,0:T(8,128)(2,1)}...) custom-call(bf16[9,2,96,768]{3,2,1,0:T(8,128)(2,1)} %shard_map.177.weights, ...), custom_call_target="tpu_custom_call" | custom-call | tf_op jit(solution)/shard_map/pallas_call | solution.py:1189
  343.8 0.0 copy-start.1
  343.8 0.0 copy-start
  343.8 4.7 %shard_map.179 = (f32[96,3456]{1,0:T(8,128)}, f32[96,3456]{1,0:T(8,128)}, f32[96,3456]{1,0:T(8,128)}, f32[3,96,768]{2,1,0:T(8,128)}, f32[96,768]{1,0:T(8,128)}) custom-call(bf16[9,96,768]{2,1,0:T(8,128)(2,1)} %get-tuple-element.23.own, bf16[9,96,768]{2,1,0:T(8,128)(2,1)} %get-tuple-element.24.other), custom_call_target="tpu_custom_call" | custom-call | tf_op jit(solution)/shard_map/pallas_call | solution.py:1340
  348.5 0.8 constant_dynamic-slice_fusion
  349.3 0.5 slice_bitcast_fusion.1
  349.8 0.6 slice_bitcast_fusion
  350.4 0.0 copy-done.1
  350.4 0.8 copy.22
  351.2 0.0 copy-done
  351.2 0.8 copy.23
Async XLA Ops:
  0.6 4.7 %copy-start.2 = (bf16[96,3]{0,1:T(4,128)(2,1)S(1)}, bf16[96,3]{0,1:T(4,128)(2,1)}, u32[]{:S(2)}) copy-start(bf16[96,3]{0,1:T(4,128)(2,1)} %param.13) | copy-start | bytes 1732
  0.7 4.7 %copy-start.3 = (bf16[96]{0:T(256)(128)(2,1)S(1)}, bf16[96]{0:T(256)(128)(2,1)}, u32[]{:S(2)}) copy-start(bf16[96]{0:T(256)(128)(2,1)} %param.15) | copy-start | bytes 580
  0.7 4.7 %copy-start.4 = (bf16[96]{0:T(256)(128)(2,1)S(1)}, bf16[96]{0:T(256)(128)(2,1)}, u32[]{:S(2)}) copy-start(bf16[96]{0:T(256)(128)(2,1)} %param.11) | copy-start | bytes 580
  343.8 6.6 %copy-start.1 = (bf16[192,1536]{1,0:T(8,128)(2,1)S(1)}, bf16[192,1536]{1,0:T(8,128)(2,1)}, u32[]{:S(2)}) copy-start(bf16[192,1536]{1,0:T(8,128)(2,1)} %get-tuple-element.20) | copy-start | bytes 1769476
  343.8 7.4 %copy-start = (bf16[192,1536]{1,0:T(8,128)(2,1)S(1)}, bf16[192,1536]{1,0:T(8,128)(2,1)}, u32[]{:S(2)}) copy-start(bf16[192,1536]{1,0:T(8,128)(2,1)} %get-tuple-element.21) | copy-start | bytes 1769476

commit v5 on v4

--- a/solution.py
+++ b/solution.py
@@ -444,6 +444,12 @@
     def pass_on(k, t):
         pl.when(between)(lambda: relay(k, t))
 
+    def own_between(k):
+        pl.when(between)(lambda: own(k))
+
+    def own_at_end(k):
+        pl.when(jnp.logical_not(between))(lambda: own(k))
+
     def take_last(k):
         @pl.when(jnp.logical_not(between))
         def _():
@@ -600,11 +606,13 @@
 
     def all_copy(buffer, which, i):
         block, which_half, to = (
-            (at.block, 0, at.beside),
+            (at.block, 0, at.across if which < 2 else at.beside),
             (at.block, 1, at.across),
             (at.block, 1, at.beside),
-            (at.block, 0, at.across),
-            (at.beside_block, 0, at.across),
+            (at.block, 0, at.beside if which < 2 else at.across),
+            (at.across_block, 0, at.beside)
+            if which < 2
+            else (at.beside_block, 0, at.across),
             (at.across_block, 1, at.beside),
         )[i]
         ref = half_of(buffer, block, which_half)
@@ -612,10 +620,10 @@
 
     def all_landed(buffer, which, i):
         block, which_half = (
-            (at.beside_block, 0),
+            (at.across_block if which < 2 else at.beside_block, 0),
             (at.across_block, 1),
             (at.beside_block, 1),
-            (at.across_block, 0),
+            (at.beside_block if which < 2 else at.across_block, 0),
             (at.far_block, 0),
             (at.far_block, 1),
         )[i]
@@ -635,6 +643,13 @@
 
     def all_wait(buffer, which):
         for i in range(2, 6):
+            all_landed(buffer, which, i)
+
+    def near_wait(buffer, which):
+        all_landed(buffer, which, 3)
+
+    def far_wait(buffer, which):
+        for i in (2, 4, 5):
             all_landed(buffer, which, i)
 
     def all_done(buffer, which):
@@ -726,8 +741,17 @@
         return pl.ds(pl.multiple_of(q * 2 * wide, 2 * wide), 2 * wide)
 
     def weight_grad(turned, grads, k, span):
-        out = dot(w[turned].reshape(planes * wide, 4 * rows), grads).astype(jnp.bfloat16)
-        w[k, :, :, :, :, span] = out.reshape(planes, 2, 2, share, grads.shape[1])
+        def some(q, carry):
+            here = pair(q)
+            out = dot(w[turned, here].reshape(2 * wide, 4 * rows), grads).astype(jnp.bfloat16)
+            w[k, here, :, :, :, span] = out.reshape(2, 2, 2, share, grads.shape[1])
+            return carry
+
+        if grads.shape[1] <= PART:
+            out = dot(w[turned].reshape(planes * wide, 4 * rows), grads).astype(jnp.bfloat16)
+            w[k, :, :, :, :, span] = out.reshape(planes, 2, 2, share, grads.shape[1])
+        else:
+            lax.fori_loop(0, planes // 2, some, 0)
 
     halo[...] = jnp.zeros_like(halo)
     barrier = pltpu.get_barrier_semaphore()
@@ -778,9 +802,9 @@
 
     by_rows(first_norm)
     all_start(n_one, 0)
-    begin(2)
     own(0)
     own(1)
+    begin(2)
     relay(0, 1)
     all_pass(n_one, 0)
     e_copy.wait()
@@ -791,7 +815,8 @@
     relay(1, 2)
     own(2)
     all_pass(e_all, 1)
-    begin(4)
+    for k in range(4, chunks - 2):
+        begin(k)
     for t in range(3, planes):
         relay(0, t)
     core_wait(0)
@@ -887,10 +912,12 @@
     keep_mixer.start()
     pass_on(2, 1)
     part_pass(sent_a, got_a, 0)
-    own(4)
-    begin(5)
+    for k in range(4, chunks - 2):
+        own_at_end(k)
+    own_between(4)
     for t in range(2, planes):
         pass_on(2, t)
+    own_between(5)
     keep_weights.wait()
     keep_mixer.wait()
     total_a[...] = jnp.zeros_like(total_a)
@@ -908,19 +935,14 @@
     all_start(n_two, 2)
     part_done(sent_a, got_a, 0)
     pass_on(3, 1)
-    own(5)
     all_pass(n_two, 2)
-    begin(6)
     begin(7)
     begin(8)
     for t in range(2, planes):
         pass_on(3, t)
-    own(6)
     pass_on(4, 1)
-    all_wait(n_two, 2)
-    transposed(n_two, 0)
-    own(7)
     take_last(2)
+    near_wait(n_two, 2)
 
     def cast(source, target):
         def run(b, carry):
@@ -930,7 +952,15 @@
         lax.fori_loop(0, 4, run, 0)
 
     def feed_forward(k):
-        def half(t, carry):
+        def half(j, carry):
+            t = lax.rem(at.x + j, 2)
+
+            @pl.when(jnp.logical_and(k == 2, j == 1))
+            def _():
+                own_at_end(7)
+                own_at_end(8)
+                far_wait(n_two, 2)
+
             normed = n_two[pair(t)].reshape(2 * rows, width)
             both = dot(normed, whole(k, 0, 2 * step_cols))
             d_active = dot(
@@ -956,10 +986,6 @@
                 return inner
 
             lax.fori_loop(0, planes // 2, spread, 0)
-            early = jnp.logical_and(between, jnp.logical_and(t == 0, k > 2))
-            pl.when(early)(lambda: first_hop(k - 3))
-            pl.when(jnp.logical_and(t == 0, k + 3 < chunks))(lambda: pass_on(k + 3, 1))
-            pl.when(jnp.logical_and(t == 1, k + 2 < chunks))(lambda: pass_on(k + 2, 2))
             return carry
 
         lax.fori_loop(0, 2, half, 0)
@@ -970,6 +996,7 @@
             part_start(sent_a, got_a, 2)
 
         gather_done(k)
+        pl.when(k == 2)(lambda: transposed(n_two, 0))
 
         def grads(n, carry):
             span = pl.ds(pl.multiple_of(n * step_cols, step_cols), step_cols)
@@ -981,16 +1008,20 @@
 
     def one_part(i, carry):
         k = i + 2
-        pl.when(i == 1)(lambda: own(8))
         core_wait(k)
         feed_forward(k)
         core_start(i)
-        pl.when(jnp.logical_not(between))(lambda: first_hop(i))
+        pl.when(k + 2 < chunks)(lambda: pass_on(k + 2, 2))
+        pl.when(k + 3 < chunks)(lambda: pass_on(k + 3, 1))
+        pl.when(i == 0)(lambda: own_between(6))
+        pl.when(i == 0)(lambda: own_between(7))
+        pl.when(i == 1)(lambda: own_between(8))
+        pl.when(k + 1 < chunks)(lambda: take_last(k + 1))
+        first_hop(i)
         pl.when(jnp.logical_and(i >= 3, i < parts - 1))(lambda: tick(i - 2))
 
         @pl.when(k + 1 < chunks)
         def _():
-            take_last(k + 1)
             for t in range(3, planes):
                 pass_on(k + 1, t)
 
@@ -1004,7 +1035,6 @@
     cast(total_a, sent_b)
     restore_mixer = pltpu.make_async_copy(kept_mixer, total_a, keep_sem.at[2])
     restore_mixer.start()
-    pl.when(between)(lambda: first_hop(jnp.int32(parts - 1)))
     part_pass(sent_a, got_a, 2)
     tick(4)
     part_wait(sent_a, got_a, 2)
@@ -1029,7 +1059,6 @@
     restore_weights.wait()
     restore_mixer.wait()
     tick(5)
-    tick(6)
     all_wait(f_all, 3)
 
     def into_mixer(t, carry):
@@ -1061,6 +1090,7 @@
     weight_grad(2, d_c, 0, pl.ds(0, channels))
     weight_grad(3, mixed[...].reshape(4 * rows, channels), 0, pl.ds(channels, channels))
     core_start(jnp.int32(parts))
+    tick(6)
     halo_core(1, head).wait_recv()
     pl.when(at.gives_next)(lambda: halo_plane(1, head, at.next).wait_recv())
     for group in range(2):
@@ -1126,9 +1156,11 @@
     def through_first(span):
         hidden = tokens[span, :].astype(jnp.float32)
         grad = back_through_norm(summed(sent_a, got_a, span), hidden, gains[0:1, :], 0)
-        d_tokens[span, :] = (d_hidden[span, :] + grad).astype(jnp.bfloat16)
+        sent_a[at.block, span, :] = (d_hidden[span, :] + grad).astype(jnp.bfloat16)
 
     by_rows(through_first)
+    d_tokens_copy = pltpu.make_async_copy(sent_a.at[at.block], d_tokens, keep_sem.at[3])
+    d_tokens_copy.start()
 
     def small_copy(i, to):
         return remote(small, small_in.at[i], small_send.at[i], small_recv.at[i], to)
@@ -1158,12 +1190,17 @@
     part_wait(sent_b, n_two, 1)
 
     def last_out(span):
-        result[span, :] = (hidden_one[span, :] + summed(sent_b, n_two, span)).astype(jnp.bfloat16)
+        total = hidden_one[span, :] + summed(sent_b, n_two, span)
+        sent_b[at.block, span, :] = total.astype(jnp.bfloat16)
 
     by_rows(last_out)
+    result_copy = pltpu.make_async_copy(sent_b.at[at.block], result, keep_sem.at[4])
+    result_copy.start()
     for j in range(11, chunks + planes - 1):
         tick(j)
 
+    d_tokens_copy.wait()
+    result_copy.wait()
     part_done(sent_a, got_a, 3)
     all_done(e_all, 1)
     part_done(sent_b, n_two, 1)
@@ -1198,7 +1235,7 @@
             shape(block, full),
         ),
         in_specs=[anywhere, vmem, anywhere, vmem],
-        out_specs=[vmem, vmem, anywhere, anywhere, vmem, anywhere, anywhere],
+        out_specs=[anywhere, anywhere, anywhere, anywhere, vmem, anywhere, anywhere],
         scratch_shapes=[
             pltpu.VMEM((chunks, planes, 2, 2, share, cols), low),
             pltpu.VMEM((2, planes, 2, share, cols), low),
@@ -1250,7 +1287,7 @@
             dma((4, 6)),
             dma((4,)),
             dma((4,)),
-            dma((3,)),
+            dma((5,)),
         ],
         compiler_params=pltpu.CompilerParams(
             collective_id=0, has_side_effects=True, vmem_limit_bytes=64 * 1024 * 1024

time: 356 us -> 336 us (0.944)
  Pallas kernels: 347 us -> 331 us
    pallas_call x1, Pallas kernels: 338 us -> 322 us  [one_kernel(): pl.pallas_call(functools.partial(kernel, planes, parts, seq_len), out_sha...]
where the time goes in v5:
time: 336 us
  Pallas kernels  331 us (99%)
  local copies, waits for them, and re-layouts  3.52 us (1%)
    pallas_call x1, Pallas kernels, one_kernel(): pl.pallas_call(functools.partial(kernel, planes, parts, seq_len), out_sha...  322 us

profile of v5, /device:TPU:0, one launch (start us, length us, event | category | flops | bytes accessed | tf_op | source)
XLA Modules:
  0.0 335.7 jit_solution(12143698144073391691)
XLA Ops:
  0.6 0.0 copy-start.2
  0.7 0.0 copy-start.3
  0.7 0.0 copy-start.4
  0.7 4.6 %shard_map.177.weights = bf16[9,2,96,768]{3,2,1,0:T(8,128)(2,1)} custom-call(bf16[96,3456]{1,0:T(8,128)(2,1)} %gate.1, bf16[96,3456]{1,0:T(8,128)(2,1)} %up.1, bf16[96,3456]{1,0:T(8,128)(2,1)} %down.1, bf16[3,96,768]{2,1,0:T(8,128)(2,1)} %bitcast.19, bf16[96,768]{1,0:T(8,128)(2,1)} %out_weight.1), custom_call_target="tpu_custom_call" | custom-call | tf_op jit(solution)/shard_map/pallas_call | solution.py:1326
  5.3 0.0 copy-done.2
  5.3 0.0 copy-done.3
  5.3 0.0 copy-done.4
  5.3 0.6 fusion.8.gains_here
  5.9 321.5 %shard_map.178 = (bf16[192,1536]{1,0:T(8,128)(2,1)}, bf16[192,1536]{1,0:T(8,128)(2,1)}, bf16[9,96,768]{2,1,0:T(8,128)(2,1)}, bf16[9,96,768]{2,1,0:T(8,128)(2,1)}...) custom-call(bf16[9,2,96,768]{3,2,1,0:T(8,128)(2,1)} %shard_map.177.weights, ...), custom_call_target="tpu_custom_call" | custom-call | tf_op jit(solution)/shard_map/pallas_call | solution.py:1226
  327.5 0.0 copy-start.1
  327.5 0.0 copy-start
  327.5 4.7 %shard_map.179 = (f32[96,3456]{1,0:T(8,128)}, f32[96,3456]{1,0:T(8,128)}, f32[96,3456]{1,0:T(8,128)}, f32[3,96,768]{2,1,0:T(8,128)}, f32[96,768]{1,0:T(8,128)}) custom-call(bf16[9,96,768]{2,1,0:T(8,128)(2,1)} %get-tuple-element.23.own, bf16[9,96,768]{2,1,0:T(8,128)(2,1)} %get-tuple-element.24.other), custom_call_target="tpu_custom_call" | custom-call | tf_op jit(solution)/shard_map/pallas_call | solution.py:1377
  332.2 0.8 constant_dynamic-slice_fusion
  332.9 0.5 slice_bitcast_fusion.1
  333.5 0.6 slice_bitcast_fusion
  334.1 0.0 copy-done.1
  334.1 0.8 copy.22
  334.9 0.0 copy-done
  334.9 0.8 copy.23
Async XLA Ops:
  0.6 4.7 %copy-start.2 = (bf16[96,3]{0,1:T(4,128)(2,1)S(1)}, bf16[96,3]{0,1:T(4,128)(2,1)}, u32[]{:S(2)}) copy-start(bf16[96,3]{0,1:T(4,128)(2,1)} %param.13) | copy-start | bytes 1732
  0.7 4.7 %copy-start.3 = (bf16[96]{0:T(256)(128)(2,1)S(1)}, bf16[96]{0:T(256)(128)(2,1)}, u32[]{:S(2)}) copy-start(bf16[96]{0:T(256)(128)(2,1)} %param.15) | copy-start | bytes 580
  0.7 4.7 %copy-start.4 = (bf16[96]{0:T(256)(128)(2,1)S(1)}, bf16[96]{0:T(256)(128)(2,1)}, u32[]{:S(2)}) copy-start(bf16[96]{0:T(256)(128)(2,1)} %param.11) | copy-start | bytes 580
  327.5 6.6 %copy-start.1 = (bf16[192,1536]{1,0:T(8,128)(2,1)S(1)}, bf16[192,1536]{1,0:T(8,128)(2,1)}, u32[]{:S(2)}) copy-start(bf16[192,1536]{1,0:T(8,128)(2,1)} %get-tuple-element.20) | copy-start | bytes 1769476
  327.5 7.4 %copy-start = (bf16[192,1536]{1,0:T(8,128)(2,1)S(1)}, bf16[192,1536]{1,0:T(8,128)(2,1)}, u32[]{:S(2)}) copy-start(bf16[192,1536]{1,0:T(8,128)(2,1)} %get-tuple-element.21) | copy-start | bytes 1769476

commit v6 on v5

--- a/solution.py
+++ b/solution.py
@@ -529,10 +529,19 @@
         def _():
             w[k, d, :, 1 - c] = w[k, d, :, c]
 
-    def add_up(v):
+    def each_plane(body):
+        def run(i, carry):
+            body(i)
+            return carry
+
+        lax.fori_loop(0, planes, run, 0)
+
+    def up_pass(v):
         k = chunk_of(v)
         pl.when(at.has_high)(lambda: pl.semaphore_wait(ready.at[1], 1))
-        for d in range(planes - 1, -1, -1):
+
+        def one(i):
+            d = planes - 1 - i
 
             @pl.when(d > z)
             def _():
@@ -540,17 +549,26 @@
                 add_here(k, d, at.has_low)
                 sum_up(k, d).start()
 
-            @pl.when(jnp.logical_and(z == d, at.has_low))
-            def _():
-                sum_up(k, d).wait_recv()
-                total = w[k, d, :, c].astype(jnp.float32) + w[k, d, :, 1 - c].astype(jnp.float32)
-                w[k, d, :, c] = total.astype(jnp.bfloat16)
-
-    def add_down(v):
+        each_plane(one)
+
+    def up_last(v):
+        k = chunk_of(v)
+
+        @pl.when(at.has_low)
+        def _():
+            sum_up(k, z).wait_recv()
+            total = w[k, z, :, c].astype(jnp.float32) + w[k, z, :, 1 - c].astype(jnp.float32)
+            w[k, z, :, c] = total.astype(jnp.bfloat16)
+
+    def add_up(v):
+        up_pass(v)
+        up_last(v)
+
+    def down_pass(v):
         k = chunk_of(v)
         pl.when(at.has_low)(lambda: pl.semaphore_wait(ready.at[0], 1))
-        for d in range(planes):
-
+
+        def one(d):
             @pl.when(d < z)
             def _():
                 pl.when(at.has_high)(lambda: sum_down(k, d).wait_recv())
@@ -558,11 +576,20 @@
                 pl.when(z - 1 > d)(lambda: sum_down(k, d).start())
                 pl.when(z - 1 == d)(lambda: sum_down_last(k, d).start())
 
-            @pl.when(jnp.logical_and(z == d, at.has_high))
-            def _():
-                sum_down_last(k, d).wait_recv()
-                total = w[k, d, :, c].astype(jnp.float32) + extra[k].astype(jnp.float32)
-                w[k, d, :, c] = total.astype(jnp.bfloat16)
+        each_plane(one)
+
+    def down_last(v):
+        k = chunk_of(v)
+
+        @pl.when(at.has_high)
+        def _():
+            sum_down_last(k, z).wait_recv()
+            total = w[k, z, :, c].astype(jnp.float32) + extra[k].astype(jnp.float32)
+            w[k, z, :, c] = total.astype(jnp.bfloat16)
+
+    def add_down(v):
+        down_pass(v)
+        down_last(v)
 
     def give_copies(k):
         return (
@@ -589,15 +616,48 @@
         pl.when(jnp.logical_not(at.has_low))(lambda: add_up(v))
         pl.when(jnp.logical_not(at.has_high))(lambda: add_down(v))
 
+    near_low = z < planes - 1 - z
+
+    def stage(o, flag, do):
+        there = jnp.logical_and(o >= 0, o < chunks)
+        pl.when(jnp.logical_and(there, flag))(lambda: do(o))
+
+    far = jnp.maximum(z, planes - 1 - z)
+
+    def older(j):
+        stage(j - far, jnp.logical_and(near_low, at.has_high), add_down)
+        stage(j - far, jnp.logical_and(jnp.logical_not(near_low), at.has_low), add_up)
+
     def tick(j):
-        def stage(o, extra_flag, do):
-            there = jnp.logical_and(o >= 0, o < chunks)
-            pl.when(jnp.logical_and(there, extra_flag))(lambda: do(o))
-
-        far = jnp.maximum(z, planes - 1 - z)
-        stage(j - z, at.has_low, add_up)
-        stage(j - (planes - 1 - z), at.has_high, add_down)
+        older(j)
+        near = planes - 1 - far
+        stage(j - near, jnp.logical_and(near_low, at.has_low), add_up)
+        stage(j - near, jnp.logical_and(jnp.logical_not(near_low), at.has_high), add_down)
         stage(j - far, far >= 0, give)
+
+    last = jnp.int32(chunks - 1)
+
+    def last_passes(first):
+        @pl.when(between)
+        def _():
+            older(first)
+            pl.when(near_low)(lambda: up_pass(last))
+            down_pass(last)
+            pl.when(jnp.logical_not(near_low))(lambda: up_pass(last))
+            stage(first - far, far >= 0, give)
+
+    def last_ticks(first):
+        @pl.when(between)
+        def _():
+            up_last(last)
+            down_last(last)
+            give(last)
+
+        @pl.when(jnp.logical_not(between))
+        def _():
+            for j in range(first, chunks + planes - 1):
+                older(j)
+                stage(j - far, far >= 0, give)
 
     part_rows = rows // 2
 
@@ -806,16 +866,16 @@
     own(1)
     begin(2)
     relay(0, 1)
+    relay(1, 1)
     all_pass(n_one, 0)
     e_copy.wait()
     all_start(e_all, 1)
     begin(3)
-    relay(1, 1)
     relay(0, 2)
     relay(1, 2)
     own(2)
     all_pass(e_all, 1)
-    for k in range(4, chunks - 2):
+    for k in range(4, chunks):
         begin(k)
     for t in range(3, planes):
         relay(0, t)
@@ -912,7 +972,7 @@
     keep_mixer.start()
     pass_on(2, 1)
     part_pass(sent_a, got_a, 0)
-    for k in range(4, chunks - 2):
+    for k in range(4, chunks):
         own_at_end(k)
     own_between(4)
     for t in range(2, planes):
@@ -936,8 +996,6 @@
     part_done(sent_a, got_a, 0)
     pass_on(3, 1)
     all_pass(n_two, 2)
-    begin(7)
-    begin(8)
     for t in range(2, planes):
         pass_on(3, t)
     pass_on(4, 1)
@@ -957,8 +1015,6 @@
 
             @pl.when(jnp.logical_and(k == 2, j == 1))
             def _():
-                own_at_end(7)
-                own_at_end(8)
                 far_wait(n_two, 2)
 
             normed = n_two[pair(t)].reshape(2 * rows, width)
@@ -1018,7 +1074,8 @@
         pl.when(i == 1)(lambda: own_between(8))
         pl.when(k + 1 < chunks)(lambda: take_last(k + 1))
         first_hop(i)
-        pl.when(jnp.logical_and(i >= 3, i < parts - 1))(lambda: tick(i - 2))
+        now = jnp.logical_and(i >= 3, i < parts - 1)
+        pl.when(jnp.logical_and(between, now))(lambda: tick(i - 2))
 
         @pl.when(k + 1 < chunks)
         def _():
@@ -1036,6 +1093,7 @@
     restore_mixer = pltpu.make_async_copy(kept_mixer, total_a, keep_sem.at[2])
     restore_mixer.start()
     part_pass(sent_a, got_a, 2)
+    pl.when(jnp.logical_not(between))(lambda: tick(3))
     tick(4)
     part_wait(sent_a, got_a, 2)
 
@@ -1151,6 +1209,7 @@
     first_hop(jnp.int32(parts + 1))
     part_pass(sent_b, n_two, 1)
     tick(8)
+    last_passes(9)
     part_wait(sent_a, got_a, 3)
 
     def through_first(span):
@@ -1172,7 +1231,6 @@
         )
 
     small_copy(0, at.core).start()
-    tick(9)
     for i, (here, following) in enumerate(
         ((at.core, at.beside), (at.beside, at.across), (at.across, None))
     ):
@@ -1182,22 +1240,20 @@
             small_copy(i + 1, following).start()
     for t in range(1, planes):
         small_plane(t).start()
-    tick(10)
+    last_ticks(9)
+    part_wait(sent_b, n_two, 1)
+
+    def last_out(span):
+        total = hidden_one[span, :] + summed(sent_b, n_two, span)
+        sent_b[at.block, span, :] = total.astype(jnp.bfloat16)
+
+    by_rows(last_out)
+    result_copy = pltpu.make_async_copy(sent_b.at[at.block], result, keep_sem.at[4])
+    result_copy.start()
     for t in range(1, planes):
         small_plane(t).wait()
     for t in range(1, planes):
         small[...] += small_in[2 + t]
-    part_wait(sent_b, n_two, 1)
-
-    def last_out(span):
-        total = hidden_one[span, :] + summed(sent_b, n_two, span)
-        sent_b[at.block, span, :] = total.astype(jnp.bfloat16)
-
-    by_rows(last_out)
-    result_copy = pltpu.make_async_copy(sent_b.at[at.block], result, keep_sem.at[4])
-    result_copy.start()
-    for j in range(11, chunks + planes - 1):
-        tick(j)
 
     d_tokens_copy.wait()
     result_copy.wait()

time: 336 us -> 325 us (0.967)
  Pallas kernels: 331 us -> 320 us
    pallas_call x1, Pallas kernels: 322 us -> 311 us  [one_kernel(): pl.pallas_call(functools.partial(kernel, planes, parts, seq_len), out_sha...]
where the time goes in v6:
time: 325 us
  Pallas kernels  320 us (98%)
  local copies, waits for them, and re-layouts  3.52 us (1%)
    pallas_call x1, Pallas kernels, one_kernel(): pl.pallas_call(functools.partial(kernel, planes, parts, seq_len), out_sha...  311 us

profile of v6, /device:TPU:0, one launch (start us, length us, event | category | flops | bytes accessed | tf_op | source)
XLA Modules:
  0.0 324.8 jit_solution(15468383551857008510)
XLA Ops:
  0.6 0.0 copy-start.2
  0.7 0.0 copy-start.3
  0.7 0.0 copy-start.4
  0.7 4.6 %shard_map.177.weights = bf16[9,2,96,768]{3,2,1,0:T(8,128)(2,1)} custom-call(bf16[96,3456]{1,0:T(8,128)(2,1)} %gate.1, bf16[96,3456]{1,0:T(8,128)(2,1)} %up.1, bf16[96,3456]{1,0:T(8,128)(2,1)} %down.1, bf16[3,96,768]{2,1,0:T(8,128)(2,1)} %bitcast.19, bf16[96,768]{1,0:T(8,128)(2,1)} %out_weight.1), custom_call_target="tpu_custom_call" | custom-call | tf_op jit(solution)/shard_map/pallas_call | solution.py:1382
  5.3 0.0 copy-done.2
  5.3 0.0 copy-done.3
  5.3 0.0 copy-done.4
  5.3 0.6 fusion.8.gains_here
  5.9 310.6 %shard_map.178 = (bf16[192,1536]{1,0:T(8,128)(2,1)}, bf16[192,1536]{1,0:T(8,128)(2,1)}, bf16[9,96,768]{2,1,0:T(8,128)(2,1)}, bf16[9,96,768]{2,1,0:T(8,128)(2,1)}...) custom-call(bf16[9,2,96,768]{3,2,1,0:T(8,128)(2,1)} %shard_map.177.weights, ...), custom_call_target="tpu_custom_call" | custom-call | tf_op jit(solution)/shard_map/pallas_call | solution.py:1282
  316.6 0.0 copy-start.1
  316.6 0.0 copy-start
  316.6 4.7 %shard_map.179 = (f32[96,3456]{1,0:T(8,128)}, f32[96,3456]{1,0:T(8,128)}, f32[96,3456]{1,0:T(8,128)}, f32[3,96,768]{2,1,0:T(8,128)}, f32[96,768]{1,0:T(8,128)}) custom-call(bf16[9,96,768]{2,1,0:T(8,128)(2,1)} %get-tuple-element.23.own, bf16[9,96,768]{2,1,0:T(8,128)(2,1)} %get-tuple-element.24.other), custom_call_target="tpu_custom_call" | custom-call | tf_op jit(solution)/shard_map/pallas_call | solution.py:1433
  321.3 0.8 constant_dynamic-slice_fusion
  322.0 0.5 slice_bitcast_fusion.1
  322.5 0.6 slice_bitcast_fusion
  323.1 0.0 copy-done.1
  323.1 0.8 copy.22
  323.9 0.0 copy-done
  323.9 0.8 copy.23
Async XLA Ops:
  0.6 4.7 %copy-start.2 = (bf16[96,3]{0,1:T(4,128)(2,1)S(1)}, bf16[96,3]{0,1:T(4,128)(2,1)}, u32[]{:S(2)}) copy-start(bf16[96,3]{0,1:T(4,128)(2,1)} %param.13) | copy-start | bytes 1732
  0.7 4.7 %copy-start.3 = (bf16[96]{0:T(256)(128)(2,1)S(1)}, bf16[96]{0:T(256)(128)(2,1)}, u32[]{:S(2)}) copy-start(bf16[96]{0:T(256)(128)(2,1)} %param.15) | copy-start | bytes 580
  0.7 4.7 %copy-start.4 = (bf16[96]{0:T(256)(128)(2,1)S(1)}, bf16[96]{0:T(256)(128)(2,1)}, u32[]{:S(2)}) copy-start(bf16[96]{0:T(256)(128)(2,1)} %param.11) | copy-start | bytes 580
  316.6 6.6 %copy-start.1 = (bf16[192,1536]{1,0:T(8,128)(2,1)S(1)}, bf16[192,1536]{1,0:T(8,128)(2,1)}, u32[]{:S(2)}) copy-start(bf16[192,1536]{1,0:T(8,128)(2,1)} %get-tuple-element.20) | copy-start | bytes 1769476
  316.6 7.4 %copy-start = (bf16[192,1536]{1,0:T(8,128)(2,1)S(1)}, bf16[192,1536]{1,0:T(8,128)(2,1)}, u32[]{:S(2)}) copy-start(bf16[192,1536]{1,0:T(8,128)(2,1)} %get-tuple-element.21) | copy-start | bytes 1769476

commit v7 on v6

--- a/solution.py
+++ b/solution.py
@@ -1373,7 +1373,7 @@
         weights[1, half, :, channels:] = in_weight[2, :, span]
 
 
-def split(gate, up, down, in_weight, out_weight, step=32):
+def split(gate, up, down, in_weight, out_weight, step=48):
     share, columns = gate.shape
     hidden = columns // 2
     parts = -(-hidden // PART)
@@ -1423,7 +1423,7 @@
         put(1, own)
 
 
-def join(own, other, hidden, channels, step=32):
+def join(own, other, hidden, channels, step=48):
     chunks, share, cols = own.shape
     parts = chunks - 2
     full = jnp.float32

time: 325 us -> 323 us (level)
  no operation moved by 1% of the time
where the time goes in v7:
time: 323 us
  Pallas kernels  318 us (98%)
  local copies, waits for them, and re-layouts  3.52 us (1%)
    pallas_call x1, Pallas kernels, one_kernel(): pl.pallas_call(functools.partial(kernel, planes, parts, seq_len), out_sha...  311 us

profile of v7, /device:TPU:0, one launch (start us, length us, event | category | flops | bytes accessed | tf_op | source)
XLA Modules:
  0.0 322.6 jit_solution(2607510222530350710)
XLA Ops:
  0.6 0.0 copy-start.2
  0.7 0.0 copy-start.3
  0.7 0.0 copy-start.4
  0.7 3.1 shard_map.177.weights
  3.8 0.0 copy-done.2
  3.8 0.0 copy-done.3
  3.8 0.0 copy-done.4
  3.8 0.6 fusion.8.gains_here
  4.4 310.6 %shard_map.178 = (bf16[192,1536]{1,0:T(8,128)(2,1)}, bf16[192,1536]{1,0:T(8,128)(2,1)}, bf16[9,96,768]{2,1,0:T(8,128)(2,1)}, bf16[9,96,768]{2,1,0:T(8,128)(2,1)}...) custom-call(bf16[9,2,96,768]{3,2,1,0:T(8,128)(2,1)} %shard_map.177.weights, ...), custom_call_target="tpu_custom_call" | custom-call | tf_op jit(solution)/shard_map/pallas_call | solution.py:1282
  315.1 0.0 copy-start.1
  315.1 0.0 copy-start
  315.1 4.0 %shard_map.179 = (f32[96,3456]{1,0:T(8,128)}, f32[96,3456]{1,0:T(8,128)}, f32[96,3456]{1,0:T(8,128)}, f32[3,96,768]{2,1,0:T(8,128)}, f32[96,768]{1,0:T(8,128)}) custom-call(bf16[9,96,768]{2,1,0:T(8,128)(2,1)} %get-tuple-element.23.own, bf16[9,96,768]{2,1,0:T(8,128)(2,1)} %get-tuple-element.24.other), custom_call_target="tpu_custom_call" | custom-call | tf_op jit(solution)/shard_map/pallas_call | solution.py:1433
  319.0 0.8 constant_dynamic-slice_fusion
  319.8 0.5 slice_bitcast_fusion.1
  320.3 0.6 slice_bitcast_fusion
  320.9 0.0 copy-done.1
  320.9 0.8 copy.22
  321.7 0.0 copy-done
  321.7 0.8 copy.23
Async XLA Ops:
  0.6 3.2 copy-start.2
  0.7 3.2 copy-start.3
  0.7 3.2 copy-start.4
  315.1 5.9 %copy-start.1 = (bf16[192,1536]{1,0:T(8,128)(2,1)S(1)}, bf16[192,1536]{1,0:T(8,128)(2,1)}, u32[]{:S(2)}) copy-start(bf16[192,1536]{1,0:T(8,128)(2,1)} %get-tuple-element.20) | copy-start | bytes 1769476
  315.1 6.7 %copy-start = (bf16[192,1536]{1,0:T(8,128)(2,1)S(1)}, bf16[192,1536]{1,0:T(8,128)(2,1)}, u32[]{:S(2)}) copy-start(bf16[192,1536]{1,0:T(8,128)(2,1)} %get-tuple-element.21) | copy-start | bytes 1769476
